TPU v7x, 128 devices: a whole 4x4x4 slice. The times are simulated.
128 devices in a mesh: section: 4 (over x_hi, core), vocab: 32 (over y, x_lo, z).
Axes of the slice: x: 4 (x_hi: 2, x_lo: 2; x = x_hi * 2 + x_lo), y: 4, z: 4, core: 2. Of those that a mesh axis runs over, the one named last changes fastest.
Arguments:
- token_grad: bfloat16 [32768, 4608], P('vocab', 'section'), may hold values from -6 to 6
- token_ids: int32 [32768], P('vocab'), may hold values from -1 to 519, as said below
- block_counts: int32 [32, 32], P('vocab'), may hold values from 0 to 1, as said below
- hidden: bfloat16 [2048, 4608], P('section'), may hold values from -6 to 6
- dlogits: bfloat16 [2048, 16640], P('section', 'vocab'), may hold values from -0.125 to 0.125
- master: float32 [16640, 4608], P('vocab', 'section'), may hold values from -0.046875 to 0.046875
- moment1: float32 [16640, 4608], P('vocab', 'section'), may hold values from -4 to 4
- moment2: float32 [16640, 4608], P('vocab', 'section'), may hold values from 0.01 to 1
Outputs:
- new_master: float32 [16640, 4608], P('vocab', 'section')
- new_moment1: float32 [16640, 4608], P('vocab', 'section')
- new_moment2: float32 [16640, 4608], P('vocab', 'section')
- refreshed: bfloat16 [16640, 4608], P('vocab')
Inputs may be any that keep to these rules, and one draw needn't show every extreme that they name: `block_counts`: row j gives, for each owner in order, how many of sender j's 8 blocks belong to it; each row sums to 8 and sender j's blocks come in owner order; one owner gets 1 block from every sender. `token_ids`: an id is a row among its block's owner's 520 rows, or -1 for a padding row.
All inputs are finite; a program needn't handle non-finite values.
Results may differ from a plain program's by a relative error of at most 0.005.
Values may be sent and summed in bfloat16 or wider, within the bound.
No kernel may reach another device: no remote copies, remote signals or barrier semaphores. Data moves between devices by JAX's collectives and lax.ppermute only.
A program may use at most 128 MiB of HBM per device.

v0:
```python
import jax
import jax.numpy as jnp
from jax import lax
from jax.sharding import PartitionSpec as P

BLOCK = 128


beta_first = 0.9
beta_second = 0.999
learn_rate = 0.01
adam_epsilon = 1e-08
first_fix = 1.0 - 0.9**10
second_fix = 1.0 - 0.999**10


def shards(token_grad, token_ids, block_counts, hidden, dlogits, master, moment1, moment2):
    owners = lax.axis_size("vocab")
    row_total, quarter = token_grad.shape
    block_total = row_total // BLOCK
    capacity = max(1, 2 * block_total // owners)
    slab_rows = master.shape[0]
    counts = block_counts[0]
    starts = jnp.cumsum(counts) - counts
    slot_index = jnp.arange(capacity, dtype=jnp.int32)
    live_slot = slot_index[None, :] < counts[:, None]
    pick_index = jnp.where(live_slot, starts[:, None] + slot_index[None, :], 0)
    grad_blocks = token_grad.reshape(block_total, BLOCK, quarter)
    id_blocks = token_ids.reshape(block_total, BLOCK)
    send_rows = grad_blocks[pick_index.reshape(-1)]
    send_ids = jnp.where(live_slot[:, :, None], id_blocks[pick_index], -1).reshape(
        owners, capacity * BLOCK
    )
    got_rows, got_ids = (
        lax.all_to_all(send_rows, "vocab", split_axis=0, concat_axis=0, tiled=True),
        lax.all_to_all(send_ids, "vocab", split_axis=0, concat_axis=0, tiled=True),
    )
    flat_rows = got_rows.reshape(-1, quarter)
    flat_ids = got_ids.reshape(-1)
    one_hot = (jnp.arange(slab_rows, dtype=jnp.int32)[:, None] == flat_ids[None, :]).astype(
        jnp.bfloat16
    )
    token_sum = jnp.dot(one_hot, flat_rows, preferred_element_type=jnp.float32)
    head_grad = (
        lax.psum_scatter(
            lax.dot_general(
                hidden, dlogits, (((0,), (0,)), ((), ())), preferred_element_type=jnp.float32
            ).astype(jnp.bfloat16),
            "section",
            scatter_dimension=0,
            tiled=True,
        )
        .astype(jnp.float32)
        .T
    )
    gradient = token_sum + head_grad
    new_moment1 = beta_first * moment1 + (1.0 - beta_first) * gradient
    new_moment2 = beta_second * moment2 + (1.0 - beta_second) * gradient * gradient
    new_master = master - learn_rate * (new_moment1 / first_fix) / (
        jnp.sqrt(new_moment2 / second_fix) + adam_epsilon
    )
    refreshed = lax.all_gather(new_master.astype(jnp.bfloat16), "section", axis=1, tiled=True)
    return (new_master, new_moment1, new_moment2, refreshed)


def solution(mesh):
    placed = (
        P("vocab", "section"),
        P("vocab"),
        P("vocab", None),
        P("section", None),
        P("section", "vocab"),
        P("vocab", "section"),
        P("vocab", "section"),
        P("vocab", "section"),
    )
    return jax.shard_map(
        shards,
        mesh=mesh,
        in_specs=placed,
        out_specs=(
            P("vocab", "section"),
            P("vocab", "section"),
            P("vocab", "section"),
            P("vocab", None),
        ),
        check_vma=False,
    )
```

profile of v0, /device:TPU:25, one launch (start us, length us, event | category | flops | bytes accessed | tf_op | source)
XLA Modules:
  0.0 287.0 jit_solution(9561290510103801497)
XLA Ops:
  7.2 0.0 copy-start
  7.2 0.0 reduce-scatter.4.cloned.1.call-start
  7.2 7.5 %convolution_convert_fusion = bf16[4608,520]{0,1:T(8,128)(2,1)} fusion(bf16[512,4608]{1,0:T(8,128)(2,1)} %param.11, bf16[512,520]{0,1:T(8,128)(2,1)} %param.12), kind=kOutput, calls=%fused_computation.4 | convolution fusion | flops 2456064000 | bytes 10043392 | tf_op jit(solution)/shard_map/dot_general | solution.py:46
  14.7 8.0 %copy.22 = bf16[4608,520]{1,0:T(8,128)(2,1)} copy(bf16[4608,520]{0,1:T(8,128)(2,1)} %convolution_convert_fusion) | data formatting | bytes 9584640
  22.7 0.0 reduce-scatter.4.cloned.1.call-update
  22.7 0.6 copy-done.2
  23.4 0.1 copy.18
  23.5 0.1 reduce-window.4
  23.5 0.1 fusion.6
  23.7 0.0 copy-done.1
  23.7 0.6 gather_fusion
  24.2 0.7 bitcast_select_fusion
  24.9 8.7 %all-to-all-start = ((s32[32,1,128]{2,1,0:T(1,128)}), s32[32,1,128]{2,1,0:T(1,128)S(1)}, u32[]{:S(2)}, u32[]{:S(2)}) async-start(s32[32,1,128]{2,1,0:T(1,128)} %bitcast.6), calls=%async_computation | async-start | bytes 32768 | tf_op jit(solution)/shard_map/all_to_all | solution.py:36
  33.7 6.5 %gather_fusion.1 = bf16[32,128,1152]{2,1,0:T(8,128)(2,1)} fusion(bf16[8,128,1152]{2,1,0:T(8,128)(2,1)S(1)} %bitcast.28, s32[1024]{0:T(1024)S(1)} %pad_clamp_fusion), kind=kCustom, calls=%fused_computation.1 | custom fusion | bytes 18874496 | tf_op jit(solution)/shard_map/gather | solution.py:30
  40.1 0.0 all-to-all-done
  40.2 7.8 %all-to-all-start.1 = ((bf16[32,128,1152]{2,1,0:T(8,128)(2,1)}), bf16[32,128,1152]{2,1,0:T(8,128)(2,1)}, u32[]{:S(2)}, u32[]{:S(2)}) async-start(bf16[32,128,1152]{2,1,0:T(8,128)(2,1)} %gather_fusion.1), calls=%async_computation.1 | async-start | bytes 18874368 | tf_op jit(solution)/shard_map/all_to_all | solution.py:35
  48.0 0.0 all-gather.2.cloned.1.call-start
  48.0 72.0 %reduce-scatter.4.cloned.1.call-done = bf16[1152,520]{1,0:T(8,128)(2,1)} async-done(((bf16[4608,520]{1,0:T(8,128)(2,1)}), bf16[1152,520]{1,0:T(8,128)(2,1)}) %reduce-scatter.4.cloned.1.call-update) | async-done | bytes 1198096
  120.0 2.5 copy.23
  122.5 95.3 %all-to-all-done.1 = bf16[32,128,1152]{2,1,0:T(8,128)(2,1)} async-done(((bf16[32,128,1152]{2,1,0:T(8,128)(2,1)}), bf16[32,128,1152]{2,1,0:T(8,128)(2,1)}, u32[]{:S(2)}, u32[]{:S(2)}) %all-to-all-start.1) | async-done | bytes 9437216 | tf_op jit(solution)/shard_map/all_to_all | solution.py:35
  217.8 14.3 %fusion.7 = (bf16[520,1152]{1,0:T(8,128)(2,1)}, f32[520,1152]{1,0:T(8,128)}, f32[520,1152]{1,0:T(8,128)}, f32[520,1152]{1,0:T(8,128)}) fusion(f32[520,1152]{1,0:T(8,128)} %param.13, f32[520,1152]{1,0:T(8,128)} %param.14, f32[520,1152]{1,0:T(8,128)} %param.15, bf16[1152,520]{0,1:T(8,128)(2,1)} %copy.23, bf16[4096,1152]{1,0:T(8,128)(2,1)} %bitcast.9, ...), kind=kOutput, calls=%fused_computation.22 | convolution fusion | flops 4918451200 | bytes 26226688 | tf_op jit(solution)/shard_map/dot_general | solution.py:43
  232.1 0.0 all-gather.2.cloned.1.call-update
  232.2 43.1 %all-gather.2.cloned.1.call-done = bf16[520,4608]{1,0:T(8,128)(2,1)} async-done(((bf16[520,1152]{1,0:T(8,128)(2,1)}), bf16[520,4608]{1,0:T(8,128)(2,1)}) %all-gather.2.cloned.1.call-update) | async-done | bytes 4792336 | tf_op jit(solution)/shard_map/all_gather | solution.py:62
  275.3 4.9 %copy.25 = bf16[520,4608]{1,0:T(8,128)(2,1)} copy(bf16[520,4608]{1,0:T(8,128)(2,1)} %all-gather.2.cloned.1.call-done) | data formatting | bytes 9584640
  (7 shorter events, 0.0 us)
Async XLA Ops:
  7.2 26.5 %copy-start = (bf16[1024,1152]{1,0:T(8,128)(2,1)S(1)}, bf16[1024,1152]{1,0:T(8,128)(2,1)}, u32[]{:S(2)}) copy-start(bf16[1024,1152]{1,0:T(8,128)(2,1)} %param.8) | copy-start | bytes 7077892
  7.2 112.9 %reduce-scatter.4.cloned.1.call-start = ((), (), s32[]{:S(2)}) async-start(), calls=%async_computation.4 | async-start | bytes 7372800
  22.7 0.7 copy-start.2
  22.7 0.9 copy-start.1
  24.9 15.2 %all-to-all-start = ((s32[32,1,128]{2,1,0:T(1,128)}), s32[32,1,128]{2,1,0:T(1,128)S(1)}, u32[]{:S(2)}, u32[]{:S(2)}) async-start(s32[32,1,128]{2,1,0:T(1,128)} %bitcast.6), calls=%async_computation | async-start | bytes 32768 | tf_op jit(solution)/shard_map/all_to_all | solution.py:36
  40.2 177.6 %all-to-all-start.1 = ((bf16[32,128,1152]{2,1,0:T(8,128)(2,1)}), bf16[32,128,1152]{2,1,0:T(8,128)(2,1)}, u32[]{:S(2)}, u32[]{:S(2)}) async-start(bf16[32,128,1152]{2,1,0:T(8,128)(2,1)} %gather_fusion.1), calls=%async_computation.1 | async-start | bytes 18874368 | tf_op jit(solution)/shard_map/all_to_all | solution.py:35
  48.0 227.3 %all-gather.2.cloned.1.call-start = ((), (), s32[]{:S(2)}) async-start(), calls=%async_computation.3 | async-start | bytes 5990400 | tf_op jit(solution)/shard_map/all_gather | solution.py:62
Sparse Core Ops, SparseCore 0:
  22.9 97.1 reduce-scatter.3
  232.3 42.9 all-gather.1
where the time goes:
time: 289 us; the launch traced here: 287 us
  waiting for transfers between devices  210 us (73%)
  local copies, waits for them, and re-layouts  23.2 us (8%)
  matrix products  21.8 us (8%)
  starting transfers between devices  16.6 us (6%)
  between operations  14.1 us (5%)
    all_to_all x1, waiting for transfers between devices, shards(): lax.all_to_all(send_rows, 'vocab', split_axis=0, concat_axis=0, tiled=True)  95.3 us
    unnamed x3, waiting for transfers between devices  72 us
    all_gather x1, waiting for transfers between devices, shards(): lax.all_gather(new_master.astype(jnp.bfloat16), 'section', axis=1, tiled=...  43.1 us
    unnamed x9, local copies, waits for them, and re-layouts  16 us
    dot_general x1, matrix products, shards(): token_sum = jnp.dot(one_hot, flat_rows, preferred_element_type=jnp.float32)  14.3 us
    all_to_all x1, starting transfers between devices, shards(): lax.all_to_all(send_ids, 'vocab', split_axis=0, concat_axis=0, tiled=True)  8.73 us
    all_to_all x1, starting transfers between devices, shards(): lax.all_to_all(send_rows, 'vocab', split_axis=0, concat_axis=0, tiled=True)  7.83 us
    dot_general x1, matrix products, shards(): lax.dot_general(hidden, dlogits, (((0,), (0,)), ((), ())), preferred_elem...  7.47 us
  transfers between devices with their start and end apart: 4, of which 3 were waited for; matrix products, arithmetic and copies ran while one was open for 4% of the time, Pallas kernels for 0%

commit v1 on v0

v1 whole, which is shorter than its diff:
```python
import functools

import jax
import jax.numpy as jnp
from jax import lax
from jax.experimental import pallas as pl
from jax.experimental.pallas import tpu as pltpu
from jax.sharding import PartitionSpec as P

BLOCK = 128


beta_first = 0.9
beta_second = 0.999
learn_rate = 0.01
adam_epsilon = 1e-08
first_fix = 1.0 - 0.9**10
second_fix = 1.0 - 0.999**10

CORE = ((0, 1), (1, 0), (2, 3), (3, 2))
ACROSS = ((0, 2), (2, 0), (1, 3), (3, 1))


def head_kernel(place, dlogits_t, hidden_keep, hidden_send, keep, send):
    left = dlogits_t[...]
    keep[0] = jnp.dot(left, hidden_keep[...], preferred_element_type=jnp.float32).astype(
        jnp.bfloat16
    )
    send[0] = jnp.dot(left, hidden_send[...], preferred_element_type=jnp.float32).astype(
        jnp.bfloat16
    )


def head_parts(hidden, dlogits, section, quarter):
    tokens, rows = dlogits.shape
    shape = jax.ShapeDtypeStruct((2, rows, quarter), jnp.bfloat16)
    return pl.pallas_call(
        head_kernel,
        grid_spec=pltpu.PrefetchScalarGridSpec(
            num_scalar_prefetch=1,
            grid=(2,),
            in_specs=[
                pl.BlockSpec((rows, tokens), lambda h, place: (0, 0)),
                pl.BlockSpec((tokens, quarter), lambda h, place: (0, place[0] ^ (2 * h))),
                pl.BlockSpec((tokens, quarter), lambda h, place: (0, place[0] ^ (2 * h + 1))),
            ],
            out_specs=[
                pl.BlockSpec((1, rows, quarter), lambda h, place: (h, 0, 0)),
                pl.BlockSpec((1, rows, quarter), lambda h, place: (h, 0, 0)),
            ],
        ),
        out_shape=[shape, shape],
        compiler_params=pltpu.CompilerParams(vmem_limit_bytes=40 * 1024 * 1024),
        cost_estimate=pl.CostEstimate(
            flops=2 * tokens * rows * 4 * quarter,
            bytes_accessed=2 * (tokens * 4 * quarter + tokens * rows + 4 * rows * quarter),
            transcendentals=0,
        ),
    )(section.reshape(1), dlogits.T, hidden, hidden)


def sum_kernel(width, senders, blocks, owner, got, out, acc):
    step = pl.program_id(0)
    owners, slab_rows, packed = acc.shape

    @pl.when(step == 0)
    def _():
        acc[...] = jnp.zeros_like(acc)

    row = lax.broadcasted_iota(jnp.int32, (slab_rows, BLOCK), 0).astype(jnp.float32)
    for sender in range(senders):
        for block in range(blocks):
            part = got[sender, :, block * BLOCK : (block + 1) * BLOCK]
            ids = part[width : width + 1].astype(jnp.float32) * 32.0
            ids = ids + part[width + 1 : width + 2].astype(jnp.float32) - 1.0
            one_hot = (row == ids).astype(jnp.bfloat16)
            place = owner[(step * senders + sender) * blocks + block]
            acc[place] += lax.dot_general(
                one_hot, part, (((1,), (1,)), ((), ())), preferred_element_type=jnp.float32
            )

    @pl.when(step == pl.num_programs(0) - 1)
    def _():
        shape = (packed, packed)
        down = lax.broadcasted_iota(jnp.int32, shape, 0)
        across = lax.broadcasted_iota(jnp.int32, shape, 1)
        unit = jnp.logical_and(down == across, down < width).astype(jnp.bfloat16)

        def turn(place, carry):
            out[place] = lax.dot_general(
                unit,
                acc[place].astype(jnp.bfloat16),
                (((1,), (1,)), ((), ())),
                preferred_element_type=jnp.float32,
            ).astype(jnp.bfloat16)
            return carry

        lax.fori_loop(0, owners, turn, 0)


def owner_sums(got, owner, slab_rows, width):
    owners, packed, row_total = got.shape
    senders = 4
    blocks = row_total // BLOCK
    return pl.pallas_call(
        functools.partial(sum_kernel, width, senders, blocks),
        grid_spec=pltpu.PrefetchScalarGridSpec(
            num_scalar_prefetch=1,
            grid=(owners // senders,),
            in_specs=[
                pl.BlockSpec((senders, packed, row_total), lambda i, owner: (i, 0, 0)),
            ],
            out_specs=pl.BlockSpec((owners, packed, slab_rows), lambda i, owner: (0, 0, 0)),
            scratch_shapes=[pltpu.VMEM((owners, slab_rows, packed), jnp.float32)],
        ),
        out_shape=jax.ShapeDtypeStruct((owners, packed, slab_rows), jnp.bfloat16),
        compiler_params=pltpu.CompilerParams(vmem_limit_bytes=40 * 1024 * 1024),
        cost_estimate=pl.CostEstimate(
            flops=2 * owners * row_total * slab_rows * packed,
            bytes_accessed=2 * owners * packed * (row_total + slab_rows),
            transcendentals=0,
        ),
    )(owner, got)


def place_kernel(place, own, core, far, diagonal, out, sems):
    quarter = own.shape[1]
    copies = []
    for k, part in enumerate((own, core, far, diagonal)):
        start = pl.multiple_of((place[0] ^ k) * quarter, 128)
        copies.append(
            pltpu.make_async_copy(part, out.at[:, pl.ds(start, quarter)], sems.at[k])
        )
    for copy in copies:
        copy.start()
    for copy in copies:
        copy.wait()


def assemble(section, own, core, far, diagonal):
    rows, quarter = own.shape
    anywhere = pl.BlockSpec(memory_space=pl.ANY)
    return pl.pallas_call(
        place_kernel,
        in_specs=[pl.BlockSpec(memory_space=pltpu.SMEM)] + [anywhere] * 4,
        out_specs=anywhere,
        scratch_shapes=[pltpu.SemaphoreType.DMA((4,))],
        out_shape=jax.ShapeDtypeStruct((rows, 4 * quarter), jnp.bfloat16),
        cost_estimate=pl.CostEstimate(
            flops=0, bytes_accessed=4 * rows * quarter * 4, transcendentals=0
        ),
    )(section.reshape(1), own, core, far, diagonal)


def shards(token_grad, token_ids, block_counts, hidden, dlogits, master, moment1, moment2):
    owners = lax.axis_size("vocab")
    section = lax.axis_index("section").astype(jnp.int32)
    row_total, quarter = token_grad.shape
    blocks = row_total // BLOCK
    slab_rows = master.shape[0]
    width = quarter // owners
    packed = -(-(width + 3) // 8) * 8

    ends = jnp.cumsum(block_counts[0])
    block_owner = jnp.sum(
        (ends[None, :] <= jnp.arange(blocks, dtype=jnp.int32)[:, None]).astype(jnp.int32), axis=1
    )
    row_owner = jnp.repeat(block_owner, BLOCK)
    shifted = token_ids + 1
    line = jnp.arange(owners * packed, dtype=jnp.int32)
    chunk, within = line // packed, line % packed
    select = jnp.logical_and(
        (chunk * width + within)[:, None] == jnp.arange(quarter, dtype=jnp.int32)[None, :],
        (within < width)[:, None],
    ).astype(jnp.bfloat16)
    turned = lax.dot_general(
        select, token_grad, (((1,), (1,)), ((), ())), preferred_element_type=jnp.float32
    )
    inner = within[:, None]
    turned = jnp.where(
        inner == width,
        (shifted // 32).astype(jnp.float32)[None, :],
        jnp.where(
            inner == width + 1,
            (shifted % 32).astype(jnp.float32)[None, :],
            jnp.where(inner == width + 2, row_owner.astype(jnp.float32)[None, :], turned),
        ),
    ).astype(jnp.bfloat16)
    got = lax.all_to_all(
        turned.reshape(owners, packed, row_total), "vocab", split_axis=0, concat_axis=0, tiled=True
    )

    keep, send = head_parts(hidden, dlogits, section, quarter)
    from_core = lax.ppermute(send, "section", CORE)
    near = keep[0].astype(jnp.float32) + from_core[0].astype(jnp.float32)
    onward = (keep[1].astype(jnp.float32) + from_core[1].astype(jnp.float32)).astype(jnp.bfloat16)
    from_far = lax.ppermute(onward, "section", ACROSS)
    head_grad = near + from_far.astype(jnp.float32)

    got_owner = got[:, width + 2, ::BLOCK].astype(jnp.int32).reshape(-1)
    sums = owner_sums(got, got_owner, slab_rows, width)
    back = lax.all_to_all(sums, "vocab", split_axis=0, concat_axis=0, tiled=True)
    token_sum = lax.dot_general(
        back.reshape(owners * packed, slab_rows),
        select,
        (((0,), (0,)), ((), ())),
        preferred_element_type=jnp.float32,
    )
    gradient = token_sum + head_grad
    new_moment1 = beta_first * moment1 + (1.0 - beta_first) * gradient
    new_moment2 = beta_second * moment2 + (1.0 - beta_second) * gradient * gradient
    new_master = master - learn_rate * (new_moment1 / first_fix) / (
        jnp.sqrt(new_moment2 / second_fix) + adam_epsilon
    )
    own = new_master.astype(jnp.bfloat16)
    far = lax.ppermute(own, "section", ACROSS)
    core = lax.ppermute(own, "section", CORE)
    diagonal = lax.ppermute(far, "section", CORE)
    refreshed = assemble(section, own, core, far, diagonal)
    return (new_master, new_moment1, new_moment2, refreshed)


def solution(mesh):
    placed = (
        P("vocab", "section"),
        P("vocab"),
        P("vocab", None),
        P("section", None),
        P("section", "vocab"),
        P("vocab", "section"),
        P("vocab", "section"),
        P("vocab", "section"),
    )
    return jax.shard_map(
        shards,
        mesh=mesh,
        in_specs=placed,
        out_specs=(
            P("vocab", "section"),
            P("vocab", "section"),
            P("vocab", "section"),
            P("vocab", None),
        ),
        check_vma=False,
    )
```

time: 289 us -> 324 us (1.12)
  Pallas kernels: 0 us -> 180 us
  waiting for transfers between devices: 210 us -> 85.3 us
  local copies, waits for them, and re-layouts: 23.2 us -> 8.63 us
  between operations: 14.1 us -> 0.92 us
  other arithmetic: 0.87 us -> 11.7 us
  matrix products: 21.8 us -> 11.3 us
  starting transfers between devices: 16.6 us -> 24.2 us
    pallas_call x0 -> x3, Pallas kernels: none -> 180 us  [the longest x1 146 us: assemble(): pl.pallas_call(place_kernel, in_specs=[pl.BlockSpec(memory_space=pltpu.SM...]
    unnamed x3 -> x0, waiting for transfers between devices: 72 us -> none
    all_to_all x2, waiting for transfers between devices: 95.3 us -> 40.3 us  [the longest x1 25.1 us: shards(): lax.all_to_all(turned.reshape(owners, packed, row_total), 'vocab', split_...]
    ppermute x0 -> x5, waiting for transfers between devices: none -> 45 us  [the longest x1 23.9 us: shards(): far = lax.ppermute(own, 'section', ACROSS)]
    all_gather x1 -> x0, waiting for transfers between devices: 43.1 us -> none  [shards(): lax.all_gather(new_master.astype(jnp.bfloat16), 'section', axis=1, tiled=...]
    convert_element_type x0 -> x5, other arithmetic: none -> 11.4 us  [the longest x1 7.54 us: shards(): own = new_master.astype(jnp.bfloat16)]
    dot_general x2, matrix products: 21.8 us -> 11.3 us  [the longest x1 6.09 us: shards(): lax.dot_general(select, token_grad, (((1,), (1,)), ((), ())), preferred_e...]
    ppermute x0 -> x5, starting transfers between devices: none -> 9.53 us  [the longest x1 3.12 us: shards(): diagonal = lax.ppermute(far, 'section', CORE)]
  transfers between devices with their start and end apart: 4 -> 7, of which waited for: 3 -> 5; matrix products, arithmetic and copies ran while one was open for 4% -> 3% of each run, Pallas kernels for 0% -> 11%
where the time goes in v1:
time: 324 us; the launch traced here: 322 us
  Pallas kernels  180 us (56%)
  waiting for transfers between devices  85.3 us (26%)
  starting transfers between devices  24.2 us (7%)
  other arithmetic  11.7 us (4%)
  matrix products  11.3 us (3%)
  local copies, waits for them, and re-layouts  8.63 us (3%)
    pallas_call x1, Pallas kernels, assemble(): pl.pallas_call(place_kernel, in_specs=[pl.BlockSpec(memory_space=pltpu.SM...  146 us
    pallas_call x1, Pallas kernels, owner_sums(): pl.pallas_call(functools.partial(sum_kernel, width, senders, blocks), gri...  29.3 us
    all_to_all x1, waiting for transfers between devices, shards(): lax.all_to_all(turned.reshape(owners, packed, row_total), 'vocab', split_...  25.1 us
    ppermute x1, waiting for transfers between devices, shards(): far = lax.ppermute(own, 'section', ACROSS)  23.9 us
    ppermute x1, waiting for transfers between devices, shards(): from_far = lax.ppermute(onward, 'section', ACROSS)  19.5 us
    all_to_all x1, waiting for transfers between devices, shards(): lax.all_to_all(sums, 'vocab', split_axis=0, concat_axis=0, tiled=True)  15.2 us
    all_to_all x1, starting transfers between devices, shards(): lax.all_to_all(turned.reshape(owners, packed, row_total), 'vocab', split_...  8.91 us
    convert_element_type x1, other arithmetic, shards(): own = new_master.astype(jnp.bfloat16)  7.54 us
  transfers between devices with their start and end apart: 7, of which 5 were waited for; matrix products, arithmetic and copies ran while one was open for 3% of the time, Pallas kernels for 11%

profile of v1, /device:TPU:25, one launch (start us, length us, event | category | flops | bytes accessed | tf_op | source)
XLA Modules:
  0.0 322.2 jit_solution(11517545448276607357)
XLA Ops:
  0.7 0.9 fusion.25
  2.7 6.1 %select_convert_fusion = bf16[1280,1024]{1,0:T(8,128)(2,1)} fusion(bf16[1024,1152]{1,0:T(8,128)(2,1)S(1)} %copy-done, s32[1280]{0:T(1024)S(1)} %fusion.15, pred[1280]{0:T(1024)(128)(4,1)S(1)} %fusion.19, bf16[1024]{0:T(1024)(128)(2,1)S(1)} %broadcast_bitcast_fusion, bf16[1024]{0:T(1024)(128)(2,1)S(1)} %get-tuple-element.13, ...), kind=kOutput, calls=%fused_computation.4 | convolution fusion | flops 3026780160 | bytes 4997120 | tf_op jit(solution)/shard_map/dot_general | solution.py:176
  8.8 8.9 %all-to-all-start = ((bf16[32,40,1024]{2,1,0:T(8,128)(2,1)}), bf16[32,40,1024]{2,1,0:T(8,128)(2,1)}, u32[]{:S(2)}, u32[]{:S(2)}) async-start(bf16[32,40,1024]{2,1,0:T(8,128)(2,1)} %bitcast.22), calls=%async_computation | async-start | bytes 5242880 | tf_op jit(solution)/shard_map/all_to_all | solution.py:189
  17.7 2.3 copy-done.1
  20.0 4.6 %shard_map.112 = (bf16[2,520,1152]{2,1,0:T(8,128)(2,1)S(1)}, bf16[2,520,1152]{2,1,0:T(8,128)(2,1)}) custom-call(s32[1]{0:T(128)} %bitcast.4.place, bf16[520,512]{1,0:T(8,128)(2,1)S(1)} %bitcast.21, bf16[512,4608]{1,0:T(8,128)(2,1)S(1)} %copy-done.1, bf16[512,4608]{1,0:T(8,128)(2,1)S(1)} %copy-done.1), custom_call_target="tpu_custom_call" | custom-call | flops 2453667840 | bytes 10043392 | tf_op jit(solution)/shard_map/pallas_call | solution.py:37
  24.6 1.4 copy-done.2
  26.0 1.2 collective-permute-start
  27.3 25.1 %all-to-all-done.got = bf16[32,40,1024]{2,1,0:T(8,128)(2,1)} async-done(((bf16[32,40,1024]{2,1,0:T(8,128)(2,1)}), bf16[32,40,1024]{2,1,0:T(8,128)(2,1)}, u32[]{:S(2)}, u32[]{:S(2)}) %all-to-all-start) | async-done | bytes 2621472 | tf_op jit(solution)/shard_map/all_to_all | solution.py:189
  52.4 1.2 slice.15
  53.8 29.3 %shard_map.111 = bf16[32,40,520]{2,1,0:T(8,128)(2,1)S(1)} custom-call(s32[256]{0:T(256)S(1)} %reshape.102.owner, bf16[32,40,1024]{2,1,0:T(8,128)(2,1)} %all-to-all-done.got), custom_call_target="tpu_custom_call" | custom-call | flops 1363148800 | bytes 3952640 | tf_op jit(solution)/shard_map/pallas_call | solution.py:105
  83.1 1.2 copy-done.4
  84.2 5.8 %all-to-all-start.1 = ((bf16[32,40,520]{2,1,0:T(8,128)(2,1)}), bf16[32,40,520]{2,1,0:T(8,128)(2,1)}, u32[]{:S(2)}, u32[]{:S(2)}) async-start(bf16[32,40,520]{2,1,0:T(8,128)(2,1)} %copy-done.4), calls=%async_computation.1 | async-start | bytes 3276800 | tf_op jit(solution)/shard_map/all_to_all | solution.py:202
  90.0 2.9 fusion.13
  93.0 2.5 collective-permute-start.1
  95.4 15.2 %all-to-all-done.1 = bf16[32,40,520]{2,1,0:T(8,128)(2,1)} async-done(((bf16[32,40,520]{2,1,0:T(8,128)(2,1)}), bf16[32,40,520]{2,1,0:T(8,128)(2,1)}, u32[]{:S(2)}, u32[]{:S(2)}) %all-to-all-start.1) | async-done | bytes 1331232 | tf_op jit(solution)/shard_map/all_to_all | solution.py:202
  110.6 5.2 %fusion.1 = f32[520,1152]{1,0:T(8,128)} fusion(bf16[1280,520]{1,0:T(8,128)(2,1)} %bitcast.3, s32[1280]{0:T(1024)S(1)} %fusion.15, pred[1280]{0:T(1024)(128)(4,1)S(1)} %fusion.19), kind=kOutput, calls=%fused_computation.2 | convolution fusion | flops 1536491520 | bytes 3733760 | tf_op jit(solution)/shard_map/dot_general | solution.py:203
  115.8 19.5 %collective-permute-done.1 = bf16[520,1152]{1,0:T(8,128)(2,1)} collective-permute-done((bf16[520,1152]{1,0:T(8,128)(2,1)}, bf16[520,1152]{1,0:T(8,128)(2,1)}, u32[]{:S(2)}, u32[]{:S(2)}) %collective-permute-start.1) | collective-permute-done | bytes 1198112 | tf_op jit(solution)/shard_map/ppermute | solution.py:197
  135.3 7.5 %fusion.29 = (bf16[520,1152]{1,0:T(8,128)(2,1)S(1)}, f32[520,1152]{1,0:T(8,128)}, f32[520,1152]{1,0:T(8,128)}, f32[520,1152]{1,0:T(8,128)}) fusion(f32[520,1152]{1,0:T(8,128)S(1)} %copy-done.7, f32[520,1152]{1,0:T(8,128)} %fusion.1, bf16[520,1152]{1,0:T(8,128)(2,1)} %collective-permute-done.1, bf16[2,520,1152]{2,1,0:T(8,128)(2,1)} %collective-permute-done, ...), kind=kLoop, calls=%fused_computation.48 | loop fusion | flops 11381760 | bytes 21565440 | tf_op jit(solution)/shard_map/convert_element_type | solution.py:215
  143.9 2.2 collective-permute-start.2
  146.1 23.9 %collective-permute-done.3.far = bf16[520,1152]{1,0:T(8,128)(2,1)S(1)} collective-permute-done((bf16[520,1152]{1,0:T(8,128)(2,1)S(1)}, bf16[520,1152]{1,0:T(8,128)(2,1)S(1)}, u32[]{:S(2)}, u32[]{:S(2)}) %collective-permute-start.3) | collective-permute-done | bytes 1198112 | tf_op jit(solution)/shard_map/ppermute | solution.py:216
  170.0 3.1 collective-permute-start.4
  173.2 1.0 copy-done.10
  174.2 1.6 collective-permute-done.4.diagonal
  175.8 146.3 %shard_map.113 = bf16[520,4608]{1,0:T(8,128)(2,1)} custom-call(s32[1]{0:T(128)} %bitcast.4.place, bf16[520,1152]{1,0:T(8,128)(2,1)} %copy-done.6, bf16[520,1152]{1,0:T(8,128)(2,1)} %copy-done.10, bf16[520,1152]{1,0:T(8,128)(2,1)} %copy-done.9, bf16[520,1152]{1,0:T(8,128)(2,1)} %collective-permute-done.4.diagonal), custom_call_target="tpu_custom_call" | custom-call | bytes 9584640 | tf_op jit(solution)/shard_map/pallas_call | solution.py:143
  (33 shorter events, 2.4 us)
Async XLA Ops:
  0.6 2.0 copy-start
  8.8 8.9 %copy-start.5 = (bf16[512,520]{0,1:T(8,128)(2,1)S(1)}, bf16[512,520]{0,1:T(8,128)(2,1)}, u32[]{:S(2)}) copy-start(bf16[512,520]{0,1:T(8,128)(2,1)} %param.12) | copy-start | bytes 1597444
  8.8 43.6 %all-to-all-start = ((bf16[32,40,1024]{2,1,0:T(8,128)(2,1)}), bf16[32,40,1024]{2,1,0:T(8,128)(2,1)}, u32[]{:S(2)}, u32[]{:S(2)}) async-start(bf16[32,40,1024]{2,1,0:T(8,128)(2,1)} %bitcast.22), calls=%async_computation | async-start | bytes 5242880 | tf_op jit(solution)/shard_map/all_to_all | solution.py:189
  17.7 2.3 copy-start.1
  24.6 1.4 copy-start.2
  26.0 64.0 %collective-permute-start = (bf16[2,520,1152]{2,1,0:T(8,128)(2,1)}, bf16[2,520,1152]{2,1,0:T(8,128)(2,1)}, u32[]{:S(2)}, u32[]{:S(2)}) collective-permute-start(bf16[2,520,1152]{2,1,0:T(8,128)(2,1)} %get-tuple-element.7), channel_id=1, source_target_pairs={{0,32},{32,0},{64,96},{96,64},{1,33},{33,1},{65,97},{97,65},{2,34}... | collective-permute-start | bytes 7188488 | tf_op jit(solution)/shard_map/ppermute | solution.py:194
  83.1 1.2 copy-start.4
  84.2 26.4 %all-to-all-start.1 = ((bf16[32,40,520]{2,1,0:T(8,128)(2,1)}), bf16[32,40,520]{2,1,0:T(8,128)(2,1)}, u32[]{:S(2)}, u32[]{:S(2)}) async-start(bf16[32,40,520]{2,1,0:T(8,128)(2,1)} %copy-done.4), calls=%async_computation.1 | async-start | bytes 3276800 | tf_op jit(solution)/shard_map/all_to_all | solution.py:202
  93.0 42.3 %collective-permute-start.1 = (bf16[520,1152]{1,0:T(8,128)(2,1)}, bf16[520,1152]{1,0:T(8,128)(2,1)}, u32[]{:S(2)}, u32[]{:S(2)}) collective-permute-start(bf16[520,1152]{1,0:T(8,128)(2,1)} %fusion.13), channel_id=1, source_target_pairs={{0,64},{64,0},{32,96},{96,32},{1,65},{65,1},{33,97},{97,33},{2,66}... | collective-permute-start | bytes 3594248 | tf_op jit(solution)/shard_map/ppermute | solution.py:197
  110.6 24.7 %copy-start.3 = (bf16[2,520,1152]{2,1,0:T(8,128)(2,1)S(1)}, bf16[2,520,1152]{2,1,0:T(8,128)(2,1)}, u32[]{:S(2)}) copy-start(bf16[2,520,1152]{2,1,0:T(8,128)(2,1)} %copy-done.2) | copy-start | bytes 7188484
  110.6 24.7 %copy-start.7 = (f32[520,1152]{1,0:T(8,128)S(1)}, f32[520,1152]{1,0:T(8,128)}, u32[]{:S(2)}) copy-start(f32[520,1152]{1,0:T(8,128)} %param.13) | copy-start | bytes 7188484
  110.6 24.7 %copy-start.8 = (f32[520,1152]{1,0:T(8,128)S(1)}, f32[520,1152]{1,0:T(8,128)}, u32[]{:S(2)}) copy-start(f32[520,1152]{1,0:T(8,128)} %param.14) | copy-start | bytes 7188484
  142.9 1.0 copy-start.6
  142.9 27.2 %collective-permute-start.3 = (bf16[520,1152]{1,0:T(8,128)(2,1)S(1)}, bf16[520,1152]{1,0:T(8,128)(2,1)S(1)}, u32[]{:S(2)}, u32[]{:S(2)}) collective-permute-start(bf16[520,1152]{1,0:T(8,128)(2,1)S(1)} %get-tuple-element.8.own), channel_id=1, source_target_pairs={{0,64},{64,0},{32,96},{96,32},{1,65},{65,1},{33,97},{97,33},{2,66}... | collective-permute-start | bytes 3594248 | tf_op jit(solution)/shard_map/ppermute | solution.py:216
  143.9 29.2 %collective-permute-start.2 = (bf16[520,1152]{1,0:T(8,128)(2,1)S(1)}, bf16[520,1152]{1,0:T(8,128)(2,1)S(1)}, u32[]{:S(2)}, u32[]{:S(2)}) collective-permute-start(bf16[520,1152]{1,0:T(8,128)(2,1)S(1)} %get-tuple-element.8.own), channel_id=1, source_target_pairs={{0,32},{32,0},{64,96},{96,64},{1,33},{33,1},{65,97},{97,65},{2,34}... | collective-permute-start | bytes 3594248 | tf_op jit(solution)/shard_map/ppermute | solution.py:217
  170.0 3.1 copy-start.9
  170.0 5.8 %collective-permute-start.4 = (bf16[520,1152]{1,0:T(8,128)(2,1)S(1)}, bf16[520,1152]{1,0:T(8,128)(2,1)}, u32[]{:S(2)}, u32[]{:S(2)}) collective-permute-start(bf16[520,1152]{1,0:T(8,128)(2,1)S(1)} %collective-permute-done.3.far), channel_id=1, source_target_pairs={{0,32},{32,0},{64,96},{96,64},{1,33},{33,1},{65,97},{97,65},{2,34}... | collective-permute-start | bytes 3594248 | tf_op jit(solution)/shard_map/ppermute | solution.py:218
  173.2 1.0 copy-start.10

commit v2 on v1

v2 whole, which is shorter than its diff:
```python
import functools

import jax
import jax.numpy as jnp
from jax import lax
from jax.experimental import pallas as pl
from jax.experimental.pallas import tpu as pltpu
from jax.sharding import PartitionSpec as P

BLOCK = 128
MIB = 1024 * 1024


beta_first = 0.9
beta_second = 0.999
learn_rate = 0.01
adam_epsilon = 1e-08
first_fix = 1.0 - 0.9**10
second_fix = 1.0 - 0.999**10

CORE = ((0, 1), (1, 0), (2, 3), (3, 2))
ACROSS = ((0, 2), (2, 0), (1, 3), (3, 1))


def head_kernel(place, dlogits_t, hidden_keep, hidden_send, keep, send):
    left = dlogits_t[...]
    keep[0] = jnp.dot(left, hidden_keep[...], preferred_element_type=jnp.float32).astype(
        jnp.bfloat16
    )
    send[0] = jnp.dot(left, hidden_send[...], preferred_element_type=jnp.float32).astype(
        jnp.bfloat16
    )


def head_parts(hidden, dlogits, section, quarter):
    tokens, rows = dlogits.shape
    shape = jax.ShapeDtypeStruct((2, rows, quarter), jnp.bfloat16)
    return pl.pallas_call(
        head_kernel,
        grid_spec=pltpu.PrefetchScalarGridSpec(
            num_scalar_prefetch=1,
            grid=(2,),
            in_specs=[
                pl.BlockSpec((rows, tokens), lambda h, place: (0, 0)),
                pl.BlockSpec((tokens, quarter), lambda h, place: (0, place[0] ^ (2 * h))),
                pl.BlockSpec((tokens, quarter), lambda h, place: (0, place[0] ^ (2 * h + 1))),
            ],
            out_specs=[
                pl.BlockSpec((1, rows, quarter), lambda h, place: (h, 0, 0)),
                pl.BlockSpec((1, rows, quarter), lambda h, place: (h, 0, 0)),
            ],
        ),
        out_shape=[shape, shape],
        compiler_params=pltpu.CompilerParams(vmem_limit_bytes=40 * MIB),
        cost_estimate=pl.CostEstimate(
            flops=2 * tokens * rows * 4 * quarter,
            bytes_accessed=2 * (tokens * 4 * quarter + tokens * rows + 4 * rows * quarter),
            transcendentals=0,
        ),
    )(section.reshape(1), dlogits.T, hidden, hidden)


def sum_kernel(senders, blocks, owner, ids, got, out, acc, parts):
    step = pl.program_id(0)
    owners, _, slab_rows = acc.shape

    @pl.when(step == 0)
    def _():
        acc[...] = jnp.zeros_like(acc)

    lane = lax.broadcasted_iota(jnp.int32, (BLOCK, slab_rows), 1).astype(jnp.float32)
    for sender in range(senders):
        columns = ids[sender].T
        for block in range(blocks):
            part = got[sender, :, block * BLOCK : (block + 1) * BLOCK]
            one_hot = (lane == columns[:, block : block + 1]).astype(jnp.bfloat16)
            parts[sender * blocks + block] = jnp.dot(
                part, one_hot, preferred_element_type=jnp.float32
            )
    for at in range(senders * blocks):
        place = owner[step * senders * blocks + at]
        acc[place] += parts[at]

    @pl.when(step == pl.num_programs(0) - 1)
    def _():
        def narrow(place, carry):
            out[place] = acc[place].astype(jnp.bfloat16)
            return carry

        lax.fori_loop(0, owners, narrow, 0)


def owner_sums(got, owner, ids, slab_rows):
    owners, width, row_total = got.shape
    senders = 4
    blocks = row_total // BLOCK
    return pl.pallas_call(
        functools.partial(sum_kernel, senders, blocks),
        grid_spec=pltpu.PrefetchScalarGridSpec(
            num_scalar_prefetch=1,
            grid=(owners // senders,),
            in_specs=[
                pl.BlockSpec((senders, blocks, BLOCK), lambda i, owner: (i, 0, 0)),
                pl.BlockSpec((senders, width, row_total), lambda i, owner: (i, 0, 0)),
            ],
            out_specs=pl.BlockSpec((owners, width, slab_rows), lambda i, owner: (0, 0, 0)),
            scratch_shapes=[
                pltpu.VMEM((owners, width, slab_rows), jnp.float32),
                pltpu.VMEM((senders * blocks, width, slab_rows), jnp.float32),
            ],
        ),
        out_shape=jax.ShapeDtypeStruct((owners, width, slab_rows), jnp.bfloat16),
        compiler_params=pltpu.CompilerParams(vmem_limit_bytes=40 * MIB),
        cost_estimate=pl.CostEstimate(
            flops=2 * owners * row_total * slab_rows * 256,
            bytes_accessed=2 * owners * width * (row_total + slab_rows),
            transcendentals=0,
        ),
    )(owner, ids, got)


def adam_kernel(
    width, back, keep, core, far, master, moment1, moment2, *rest
):
    out_master, out_moment1, out_moment2, out_own, total = rest[-5:]
    step = pl.program_id(0)
    owners, packed, slab_rows = back.shape
    lanes = out_own.shape[1]

    @pl.when(step == 0)
    def _():
        shape = (owners * packed, owners * width)
        line = lax.broadcasted_iota(jnp.int32, shape, 0)
        feature = lax.broadcasted_iota(jnp.int32, shape, 1)
        within = line % packed
        select = jnp.logical_and(
            (line // packed) * width + within == feature, within < width
        ).astype(jnp.bfloat16)
        summed = lax.dot_general(
            back[...].reshape(owners * packed, slab_rows),
            select,
            (((0,), (0,)), ((), ())),
            preferred_element_type=jnp.float32,
        )
        for at in range(owners * width // lanes):
            total[at] = summed[:, at * lanes : (at + 1) * lanes]

    gradient = (
        total[step]
        + keep[0].astype(jnp.float32)
        + core[0].astype(jnp.float32)
        + far[...].astype(jnp.float32)
    )
    first = beta_first * moment1[...] + (1.0 - beta_first) * gradient
    second = beta_second * moment2[...] + (1.0 - beta_second) * gradient * gradient
    fresh = master[...] - learn_rate * (first / first_fix) / (
        jnp.sqrt(second / second_fix) + adam_epsilon
    )
    out_master[...] = fresh
    out_moment1[...] = first
    out_moment2[...] = second
    out_own[...] = fresh.astype(jnp.bfloat16)


def adam(back, width, start, keep, core, far, master, moment1, moment2, earlier=()):
    owners, packed, slab_rows = back.shape
    span = owners * width
    lanes = 128
    first = start // lanes
    tile = pl.BlockSpec((slab_rows, lanes), lambda i: (0, first + i))
    tile0 = pl.BlockSpec((1, slab_rows, lanes), lambda i: (0, 0, first + i))
    whole = jax.ShapeDtypeStruct(master.shape, jnp.float32)
    return pl.pallas_call(
        functools.partial(adam_kernel, width),
        grid=(span // lanes,),
        in_specs=[
            pl.BlockSpec((owners, packed, slab_rows), lambda i: (0, 0, 0)),
            tile0,
            tile0,
            tile,
            tile,
            tile,
            tile,
        ]
        + [pl.BlockSpec(memory_space=pl.ANY)] * len(earlier),
        out_specs=[tile, tile, tile, pl.BlockSpec((slab_rows, lanes), lambda i: (0, i))],
        out_shape=[whole, whole, whole, jax.ShapeDtypeStruct((slab_rows, span), jnp.bfloat16)],
        scratch_shapes=[pltpu.VMEM((span // lanes, slab_rows, lanes), jnp.float32)],
        input_output_aliases={7 + at: at for at in range(len(earlier))},
        compiler_params=pltpu.CompilerParams(vmem_limit_bytes=40 * MIB),
        cost_estimate=pl.CostEstimate(
            flops=2 * owners * packed * span * slab_rows,
            bytes_accessed=slab_rows * span * 32 + 2 * owners * packed * slab_rows,
            transcendentals=slab_rows * span,
        ),
    )(back, keep, core, far, master, moment1, moment2, *earlier)


def place_kernel(count, place, *refs):
    parts, out = refs[:-1], refs[-1]
    quarter = out.shape[1] // 4
    for k in range(4):
        start = (place[0] ^ k) * quarter
        for at in range(count):
            part = parts[k * count + at]
            size = part.shape[1]
            out[:, pl.ds(pl.multiple_of(start, 128), size)] = part[...]
            start = start + size


def assemble(section, pieces):
    count = len(pieces[0])
    rows = pieces[0][0].shape[0]
    quarter = sum(part.shape[1] for part in pieces[0])
    some = 176
    parts = [part for piece in pieces for part in piece]
    return pl.pallas_call(
        functools.partial(place_kernel, count),
        grid_spec=pltpu.PrefetchScalarGridSpec(
            num_scalar_prefetch=1,
            grid=(-(-rows // some),),
            in_specs=[pl.BlockSpec((some, part.shape[1]), lambda i, place: (i, 0)) for part in parts],
            out_specs=pl.BlockSpec((some, 4 * quarter), lambda i, place: (i, 0)),
        ),
        out_shape=jax.ShapeDtypeStruct((rows, 4 * quarter), jnp.bfloat16),
        compiler_params=pltpu.CompilerParams(vmem_limit_bytes=40 * MIB),
        cost_estimate=pl.CostEstimate(
            flops=0, bytes_accessed=4 * rows * quarter * 4, transcendentals=0
        ),
    )(section.reshape(1), *parts)


def exchange(rows):
    return lax.all_to_all(rows, "vocab", split_axis=0, concat_axis=0, tiled=True)


def shards(token_grad, token_ids, block_counts, hidden, dlogits, master, moment1, moment2):
    owners = lax.axis_size("vocab")
    section = lax.axis_index("section").astype(jnp.int32)
    row_total, quarter = token_grad.shape
    blocks = row_total // BLOCK
    slab_rows = master.shape[0]
    second_width = 16
    first_width = quarter // owners - second_width
    first_span = first_width * owners
    packed = -(-(first_width + 3) // 8) * 8

    ends = jnp.cumsum(block_counts[0])
    block_owner = jnp.sum(
        (ends[None, :] <= jnp.arange(blocks, dtype=jnp.int32)[:, None]).astype(jnp.int32), axis=1
    )
    row_owner = jnp.repeat(block_owner, BLOCK)
    shifted = token_ids + 1
    line = jnp.arange(owners * packed, dtype=jnp.int32)
    chunk, within = line // packed, line % packed
    select = jnp.logical_and(
        (chunk * first_width + within)[:, None]
        == jnp.arange(first_span, dtype=jnp.int32)[None, :],
        (within < first_width)[:, None],
    ).astype(jnp.bfloat16)
    turned = lax.dot_general(
        select,
        token_grad[:, :first_span],
        (((1,), (1,)), ((), ())),
        preferred_element_type=jnp.float32,
    )
    inner = within[:, None]
    turned = jnp.where(
        inner == first_width,
        (shifted // 32).astype(jnp.float32)[None, :],
        jnp.where(
            inner == first_width + 1,
            (shifted % 32).astype(jnp.float32)[None, :],
            jnp.where(inner == first_width + 2, row_owner.astype(jnp.float32)[None, :], turned),
        ),
    ).astype(jnp.bfloat16)
    got_a = exchange(turned.reshape(owners, packed, row_total))
    turned_b = token_grad[:, first_span:].T.reshape(owners, second_width, row_total)
    turned_b, got_a = lax.optimization_barrier((turned_b, got_a))
    got_b = exchange(turned_b)

    keep, send = head_parts(hidden, dlogits, section, quarter)
    core = lax.ppermute(send, "section", CORE)
    onward = (keep[1].astype(jnp.float32) + core[1].astype(jnp.float32)).astype(jnp.bfloat16)
    far = lax.ppermute(onward, "section", ACROSS)

    got_a, onward = lax.optimization_barrier((got_a, onward))
    numbers = got_a[:, first_width : first_width + 3, :].astype(jnp.float32)
    ids = (numbers[:, 0] * 32.0 + numbers[:, 1] - 1.0).reshape(owners, blocks, BLOCK)
    owner = numbers[:, 2, ::BLOCK].astype(jnp.int32).reshape(-1)

    sums_a = owner_sums(got_a, owner, ids, slab_rows)
    back_a = exchange(sums_a)
    sums_b = owner_sums(got_b, owner, ids, slab_rows)
    back_b = exchange(sums_b)

    shares = (keep, core, far, master, moment1, moment2)
    *states, own_a = adam(back_a, first_width, 0, *shares)
    far_a = lax.ppermute(own_a, "section", ACROSS)
    core_a = lax.ppermute(own_a, "section", CORE)
    *states, own_b = adam(back_b, second_width, first_span, *shares, earlier=states)
    far_b = lax.ppermute(own_b, "section", ACROSS)
    core_b = lax.ppermute(own_b, "section", CORE)
    cross_a = lax.ppermute(far_a, "section", CORE)
    cross_b = lax.ppermute(far_b, "section", CORE)
    refreshed = assemble(
        section,
        ((own_a, own_b), (core_a, core_b), (far_a, far_b), (cross_a, cross_b)),
    )
    return (*states, refreshed)


def solution(mesh):
    placed = (
        P("vocab", "section"),
        P("vocab"),
        P("vocab", None),
        P("section", None),
        P("section", "vocab"),
        P("vocab", "section"),
        P("vocab", "section"),
        P("vocab", "section"),
    )
    return jax.shard_map(
        shards,
        mesh=mesh,
        in_specs=placed,
        out_specs=(
            P("vocab", "section"),
            P("vocab", "section"),
            P("vocab", "section"),
            P("vocab", None),
        ),
        check_vma=False,
    )
```

time: 324 us -> 153 us (0.47)
  Pallas kernels: 180 us -> 44.2 us
  waiting for transfers between devices: 85.3 us -> 27.1 us
  starting transfers between devices: 24.2 us -> 46.1 us
  local copies, waits for them, and re-layouts: 8.63 us -> 21.4 us
  matrix products: 11.3 us -> 4.35 us
  other arithmetic: 11.7 us -> 6.4 us
    pallas_call x2 -> x5, Pallas kernels: 176 us -> 39.6 us  [the longest x2 24.3 us: owner_sums(): pl.pallas_call(functools.partial(sum_kernel, senders, blocks), grid_spec=...]
    ppermute x5 -> x8, waiting for transfers between devices: 45 us -> 7.26 us  [the longest x1 5.71 us: shards(): far_b = lax.ppermute(own_b, 'section', ACROSS)]
    all_to_all x2 -> x4, waiting for transfers between devices: 40.3 us -> 19.9 us  [exchange(): lax.all_to_all(rows, 'vocab', split_axis=0, concat_axis=0, tiled=True)]
    all_to_all x2 -> x4, starting transfers between devices: 14.7 us -> 28.1 us  [exchange(): lax.all_to_all(rows, 'vocab', split_axis=0, concat_axis=0, tiled=True)]
    unnamed x22 -> x30, local copies, waits for them, and re-layouts: 6.51 us -> 17.3 us
    ppermute x5 -> x8, starting transfers between devices: 9.53 us -> 18.1 us  [the longest x1 4.74 us: shards(): cross_a = lax.ppermute(far_a, 'section', CORE)]
    dot_general x2 -> x1, matrix products: 11.3 us -> 4.35 us  [shards(): lax.dot_general(select, token_grad[:, :first_span], (((1,), (1,)), ((), (...]
    convert_element_type x3, other arithmetic: 10.5 us -> 4.6 us  [the longest x1 2.58 us: shards(): (keep[1].astype(jnp.float32) + core[1].astype(jnp.float32)).astype(jnp.bf...]
  transfers between devices with their start and end apart: 7 -> 12, of which waited for: 5 -> 4; matrix products, arithmetic and copies ran while one was open for 3% -> 10% of each run, Pallas kernels for 11% -> 24%
where the time goes in v2:
time: 153 us; the launch traced here: 150 us
  starting transfers between devices  46.1 us (30%)
  Pallas kernels  44.2 us (29%)
  waiting for transfers between devices  27.1 us (18%)
  local copies, waits for them, and re-layouts  21.4 us (14%)
  other arithmetic  6.4 us (4%)
  matrix products  4.35 us (3%)
    all_to_all x4, starting transfers between devices, exchange(): lax.all_to_all(rows, 'vocab', split_axis=0, concat_axis=0, tiled=True)  28.1 us
    pallas_call x2, Pallas kernels, owner_sums(): pl.pallas_call(functools.partial(sum_kernel, senders, blocks), grid_spec=...  24.3 us
    all_to_all x4, waiting for transfers between devices, exchange(): lax.all_to_all(rows, 'vocab', split_axis=0, concat_axis=0, tiled=True)  19.9 us
    unnamed x30, local copies, waits for them, and re-layouts  17.3 us
    pallas_call x2, Pallas kernels, adam(): pl.pallas_call(functools.partial(adam_kernel, width), grid=(span // lanes...  11.8 us
    ppermute x1, waiting for transfers between devices, shards(): far_b = lax.ppermute(own_b, 'section', ACROSS)  5.71 us
    ppermute x1, starting transfers between devices, shards(): cross_a = lax.ppermute(far_a, 'section', CORE)  4.74 us
    pallas_call x1, Pallas kernels, head_parts(): pl.pallas_call(head_kernel, grid_spec=pltpu.PrefetchScalarGridSpec(num_sc...  4.58 us
  transfers between devices with their start and end apart: 12, of which 4 were waited for; matrix products, arithmetic and copies ran while one was open for 10% of the time, Pallas kernels for 24%

profile of v2, /device:TPU:25, one launch (start us, length us, event | category | flops | bytes accessed | tf_op | source)
XLA Modules:
  0.0 150.4 jit_solution(6111550339235007751)
XLA Ops:
  0.6 2.3 %copy-done = bf16[512,4608]{1,0:T(8,128)(2,1)S(1)} copy-done((bf16[512,4608]{1,0:T(8,128)(2,1)S(1)}, bf16[512,4608]{1,0:T(8,128)(2,1)}, u32[]{:S(2)}) %copy-start) | copy-done | bytes 4718616
  4.0 4.6 %shard_map.111 = (bf16[2,520,1152]{2,1,0:T(8,128)(2,1)S(1)}, bf16[2,520,1152]{2,1,0:T(8,128)(2,1)}) custom-call(s32[1]{0:T(128)} %bitcast.5.place, bf16[520,512]{1,0:T(8,128)(2,1)S(1)} %bitcast.12, bf16[512,4608]{1,0:T(8,128)(2,1)S(1)} %copy-done, bf16[512,4608]{1,0:T(8,128)(2,1)S(1)} %copy-done), custom_call_target="tpu_custom_call" | custom-call | flops 2453667840 | bytes 10043392 | tf_op jit(solution)/shard_map/pallas_call | solution.py:38
  9.8 4.3 %select_convert_fusion = bf16[768,1024]{1,0:T(8,128)(2,1)} fusion(bf16[1024]{0:T(1024)(128)(2,1)S(1)} %broadcast_bitcast_fusion, bf16[1024]{0:T(1024)(128)(2,1)S(1)} %get-tuple-element.31, bf16[1024]{0:T(1024)(128)(2,1)S(1)} %get-tuple-element.30, pred[768]{0:T(1024)(128)(4,1)S(1)} %get-tuple-element.33, pred[768]{0:T(1024)(128)(4,1)S(1)} %get-tuple-element.34, ...), kind=kOutput, calls=%fused_computation | convolution fusion | flops 1009975296 | bytes 2895872 | tf_op jit(solution)/shard_map/dot_general | solution.py:261
  14.2 8.8 %all-to-all-start = ((bf16[32,24,1024]{2,1,0:T(8,128)(2,1)}), bf16[32,24,1024]{2,1,0:T(8,128)(2,1)}, u32[]{:S(2)}, u32[]{:S(2)}) async-start(bf16[32,24,1024]{2,1,0:T(8,128)(2,1)} %bitcast.16), calls=%async_computation | async-start | bytes 3145728 | tf_op jit(solution)/shard_map/all_to_all | solution.py:234
  25.6 18.2 %all-to-all-done.got = bf16[32,24,1024]{2,1,0:T(8,128)(2,1)} async-done(((bf16[32,24,1024]{2,1,0:T(8,128)(2,1)}), bf16[32,24,1024]{2,1,0:T(8,128)(2,1)}, u32[]{:S(2)}, u32[]{:S(2)}) %all-to-all-start) | async-done | bytes 1572896 | tf_op jit(solution)/shard_map/all_to_all | solution.py:234
  43.7 5.9 %all-to-all-start.1 = ((bf16[32,16,1024]{2,1,0:T(8,128)(2,1)}), bf16[32,16,1024]{2,1,0:T(8,128)(2,1)S(1)}, u32[]{:S(2)}, u32[]{:S(2)}) async-start(bf16[32,16,1024]{2,1,0:T(8,128)(2,1)} %bitcast.15), calls=%async_computation.1 | async-start | bytes 2097152 | tf_op jit(solution)/shard_map/all_to_all | solution.py:234
  49.6 2.6 %fusion.6 = bf16[520,1152]{1,0:T(8,128)(2,1)} fusion(bf16[2,520,1152]{2,1,0:T(8,128)(2,1)} %collective-permute-done.core, bf16[2,520,1152]{2,1,0:T(8,128)(2,1)S(1)} %get-tuple-element.18.keep), kind=kLoop, calls=%fused_computation.6 | loop fusion | flops 2396160 | bytes 3594240 | tf_op jit(solution)/shard_map/convert_element_type | solution.py:284
  52.2 2.4 %collective-permute-start.1 = (bf16[520,1152]{1,0:T(8,128)(2,1)}, bf16[520,1152]{1,0:T(8,128)(2,1)}, u32[]{:S(2)}, u32[]{:S(2)}) collective-permute-start(bf16[520,1152]{1,0:T(8,128)(2,1)} %fusion.6), channel_id=1, source_target_pairs={{0,64},{64,0},{32,96},{96,32},{1,65},{65,1},{33,97},{97,33},{2,66}... | collective-permute-start | bytes 3594248 | tf_op jit(solution)/shard_map/ppermute | solution.py:285
  54.6 2.0 %slice_convert_fusion = f32[32,3,1024]{2,1,0:T(4,128)} fusion(bf16[32,24,1024]{2,1,0:T(8,128)(2,1)} %all-to-all-done.got), kind=kLoop, calls=%fused_computation.10 | loop fusion | flops 98304 | bytes 589824 | tf_op jit(solution)/shard_map/convert_element_type | solution.py:288
  59.4 12.8 %shard_map.113 = bf16[32,24,520]{2,1,0:T(8,128)(2,1)S(1)} custom-call(s32[256]{0:T(256)S(1)} %convert_element_type.60.owner, f32[32,8,128]{2,1,0:T(8,128)S(1)} %bitcast.13, bf16[32,24,1024]{2,1,0:T(8,128)(2,1)} %all-to-all-done.got), custom_call_target="tpu_custom_call" | custom-call | flops 8724152320 | bytes 2371584 | tf_op jit(solution)/shard_map/pallas_call | solution.py:97
  74.8 7.1 %all-to-all-start.3 = ((bf16[32,24,520]{2,1,0:T(8,128)(2,1)}), bf16[32,24,520]{2,1,0:T(8,128)(2,1)S(1)}, u32[]{:S(2)}, u32[]{:S(2)}) async-start(bf16[32,24,520]{2,1,0:T(8,128)(2,1)} %copy-done.8), calls=%async_computation.3 | async-start | bytes 1966080 | tf_op jit(solution)/shard_map/all_to_all | solution.py:234
  84.1 11.5 %shard_map.112 = bf16[32,16,520]{2,1,0:T(8,128)(2,1)S(1)} custom-call(s32[256]{0:T(256)S(1)} %convert_element_type.60.owner, f32[32,8,128]{2,1,0:T(8,128)S(1)} %bitcast.14, bf16[32,16,1024]{2,1,0:T(8,128)(2,1)S(1)} %copy-done.7), custom_call_target="tpu_custom_call" | custom-call | flops 8724152320 | bytes 1581056 | tf_op jit(solution)/shard_map/pallas_call | solution.py:97
  96.5 1.7 %all-to-all-done.3.back = bf16[32,24,520]{2,1,0:T(8,128)(2,1)S(1)} async-done(((bf16[32,24,520]{2,1,0:T(8,128)(2,1)}), bf16[32,24,520]{2,1,0:T(8,128)(2,1)S(1)}, u32[]{:S(2)}, u32[]{:S(2)}) %all-to-all-start.3) | async-done | bytes 798752 | tf_op jit(solution)/shard_map/all_to_all | solution.py:234
  98.2 6.3 %all-to-all-start.2 = ((bf16[32,16,520]{2,1,0:T(8,128)(2,1)}), bf16[32,16,520]{2,1,0:T(8,128)(2,1)}, u32[]{:S(2)}, u32[]{:S(2)}) async-start(bf16[32,16,520]{2,1,0:T(8,128)(2,1)} %copy-done.9), calls=%async_computation.2 | async-start | bytes 1310720 | tf_op jit(solution)/shard_map/all_to_all | solution.py:234
  106.2 1.7 %copy-done.3 = f32[520,1152]{1,0:T(8,128)S(1)} copy-done((f32[520,1152]{1,0:T(8,128)S(1)}, f32[520,1152]{1,0:T(8,128)}, u32[]{:S(2)}) %copy-start.3) | copy-done | bytes 2396184
  107.9 7.0 %shard_map.114 = (f32[520,1152]{1,0:T(8,128)}, f32[520,1152]{1,0:T(8,128)}, f32[520,1152]{1,0:T(8,128)}, bf16[520,640]{1,0:T(8,128)(2,1)}) custom-call(bf16[32,24,520]{2,1,0:T(8,128)(2,1)S(1)} %all-to-all-done.3.back, bf16[2,520,1152]{2,1,0:T(8,128)(2,1)S(1)} %get-tuple-element.18.keep, bf16[2,520,1152]{2,1,0:T(8,128)(2,1)} %collective-permute-done.core, ...), custom_call_target="tpu_custom_call" | custom-call | flops 511180800 | bytes 11448320 | tf_op jit(solution)/shard_map/pallas_call | solution.py:173
  114.8 2.5 %collective-permute-start.4 = (bf16[520,640]{1,0:T(8,128)(2,1)}, bf16[520,640]{1,0:T(8,128)(2,1)S(1)}, u32[]{:S(2)}, u32[]{:S(2)}) collective-permute-start(bf16[520,640]{1,0:T(8,128)(2,1)} %get-tuple-element.28.refs_0_), channel_id=1, source_target_pairs={{0,64},{64,0},{32,96},{96,32},{1,65},{65,1},{33,97},{97,33},{2,66}... | collective-permute-start | bytes 1996808 | tf_op jit(solution)/shard_map/ppermute | solution.py:299
  117.3 1.7 %copy-done.2 = f32[520,1152]{1,0:T(8,128)S(1)} copy-done((f32[520,1152]{1,0:T(8,128)S(1)}, f32[520,1152]{1,0:T(8,128)}, u32[]{:S(2)}) %copy-start.2) | copy-done | bytes 2396184
  122.3 4.8 %shard_map.115 = (f32[520,1152]{1,0:T(8,128)}, f32[520,1152]{1,0:T(8,128)}, f32[520,1152]{1,0:T(8,128)}, bf16[520,512]{1,0:T(8,128)(2,1)S(1)}) custom-call(bf16[32,16,520]{2,1,0:T(8,128)(2,1)} %all-to-all-done.2.back, bf16[2,520,1152]{2,1,0:T(8,128)(2,1)S(1)} %get-tuple-element.18.keep, ...), custom_call_target="tpu_custom_call", output_to_operand_aliasing={{0}: (7, {}), {1}: (8, {}), {2}: (9, {})} | custom-call | flops 272629760 | bytes 9052160 | tf_op jit(solution)/shard_map/pallas_call | solution.py:173
  127.7 4.4 %collective-permute-start.2 = (bf16[520,640]{1,0:T(8,128)(2,1)}, bf16[520,640]{1,0:T(8,128)(2,1)S(1)}, u32[]{:S(2)}, u32[]{:S(2)}) collective-permute-start(bf16[520,640]{1,0:T(8,128)(2,1)} %get-tuple-element.28.refs_0_), channel_id=1, source_target_pairs={{0,32},{32,0},{64,96},{96,64},{1,33},{33,1},{65,97},{97,65},{2,34}... | collective-permute-start | bytes 1996808 | tf_op jit(solution)/shard_map/ppermute | solution.py:300
  132.1 4.7 %collective-permute-start.6 = (bf16[520,640]{1,0:T(8,128)(2,1)S(1)}, bf16[520,640]{1,0:T(8,128)(2,1)S(1)}, u32[]{:S(2)}, u32[]{:S(2)}) collective-permute-start(bf16[520,640]{1,0:T(8,128)(2,1)S(1)} %collective-permute-done.4.refs_4_), channel_id=1, source_target_pairs={{0,32},{32,0},{64,96},{96,64},{1,33},{33,1},{65,97},{97,65},{2,34}... | collective-permute-start | bytes 1996808 | tf_op jit(solution)/shard_map/ppermute | solution.py:304
  136.8 5.7 %collective-permute-done.5.refs_5_ = bf16[520,512]{1,0:T(8,128)(2,1)S(1)} collective-permute-done((bf16[520,512]{1,0:T(8,128)(2,1)S(1)}, bf16[520,512]{1,0:T(8,128)(2,1)S(1)}, u32[]{:S(2)}, u32[]{:S(2)}) %collective-permute-start.5) | collective-permute-done | bytes 532512 | tf_op jit(solution)/shard_map/ppermute | solution.py:302
  142.5 2.8 %collective-permute-start.7 = (bf16[520,512]{1,0:T(8,128)(2,1)S(1)}, bf16[520,512]{1,0:T(8,128)(2,1)S(1)}, u32[]{:S(2)}, u32[]{:S(2)}) collective-permute-start(bf16[520,512]{1,0:T(8,128)(2,1)S(1)} %collective-permute-done.5.refs_5_), channel_id=1, source_target_pairs={{0,32},{32,0},{64,96},{96,64},{1,33},{33,1},{65,97},{97,65},{2,34}... | collective-permute-start | bytes 1597448 | tf_op jit(solution)/shard_map/ppermute | solution.py:305
  146.9 3.5 %shard_map.116 = bf16[520,4608]{1,0:T(8,128)(2,1)} custom-call(s32[1]{0:T(128)} %bitcast.5.place, bf16[520,640]{1,0:T(8,128)(2,1)} %get-tuple-element.28.refs_0_, bf16[520,512]{1,0:T(8,128)(2,1)S(1)} %get-tuple-element.29.refs_1_, bf16[520,640]{1,0:T(8,128)(2,1)S(1)} %collective-permute-done.2.refs_2_, bf16[520,512]{1,0:T(8,128)(2,1)S(1)} %collective-permute-done.3.refs_3_, ...), custom_call_target="tpu_custom_call" | custom-call | bytes 9584640 | tf_op jit(solution)/shard_map/pallas_call | solution.py:217
  (55 shorter events, 20.4 us)
Async XLA Ops:
  0.6 2.3 %copy-start = (bf16[512,4608]{1,0:T(8,128)(2,1)S(1)}, bf16[512,4608]{1,0:T(8,128)(2,1)}, u32[]{:S(2)}) copy-start(bf16[512,4608]{1,0:T(8,128)(2,1)} %hidden_send.1) | copy-start | bytes 14155780
  3.0 1.0 copy-start.10
  4.0 5.3 %copy-start.14 = (s32[1,32]{1,0:T(1,128)S(1)}, s32[1,32]{1,0:T(1,128)}, u32[]{:S(2)}) copy-start(s32[1,32]{1,0:T(1,128)} %param.10) | copy-start | bytes 388
  4.0 5.8 %copy-start.13 = (s32[1024]{0:T(1024)S(1)}, s32[1024]{0:T(1024)}, u32[]{:S(2)}) copy-start(s32[1024]{0:T(1024)} %param.9) | copy-start | bytes 12292
  8.6 41.0 %collective-permute-start = (bf16[2,520,1152]{2,1,0:T(8,128)(2,1)}, bf16[2,520,1152]{2,1,0:T(8,128)(2,1)}, u32[]{:S(2)}, u32[]{:S(2)}) collective-permute-start(bf16[2,520,1152]{2,1,0:T(8,128)(2,1)} %get-tuple-element.19), channel_id=1, source_target_pairs={{0,32},{32,0},{64,96},{96,64},{1,33},{33,1},{65,97},{97,65},{2,34}... | collective-permute-start | bytes 7188488 | tf_op jit(solution)/shard_map/ppermute | solution.py:283
  14.2 29.6 %all-to-all-start = ((bf16[32,24,1024]{2,1,0:T(8,128)(2,1)}), bf16[32,24,1024]{2,1,0:T(8,128)(2,1)}, u32[]{:S(2)}, u32[]{:S(2)}) async-start(bf16[32,24,1024]{2,1,0:T(8,128)(2,1)} %bitcast.16), calls=%async_computation | async-start | bytes 3145728 | tf_op jit(solution)/shard_map/all_to_all | solution.py:234
  43.7 30.1 %all-to-all-start.1 = ((bf16[32,16,1024]{2,1,0:T(8,128)(2,1)}), bf16[32,16,1024]{2,1,0:T(8,128)(2,1)S(1)}, u32[]{:S(2)}, u32[]{:S(2)}) async-start(bf16[32,16,1024]{2,1,0:T(8,128)(2,1)} %bitcast.15), calls=%async_computation.1 | async-start | bytes 2097152 | tf_op jit(solution)/shard_map/all_to_all | solution.py:234
  52.2 52.3 %collective-permute-start.1 = (bf16[520,1152]{1,0:T(8,128)(2,1)}, bf16[520,1152]{1,0:T(8,128)(2,1)}, u32[]{:S(2)}, u32[]{:S(2)}) collective-permute-start(bf16[520,1152]{1,0:T(8,128)(2,1)} %fusion.6), channel_id=1, source_target_pairs={{0,64},{64,0},{32,96},{96,32},{1,65},{65,1},{33,97},{97,33},{2,66}... | collective-permute-start | bytes 3594248 | tf_op jit(solution)/shard_map/ppermute | solution.py:285
  72.3 0.9 copy-start.8
  73.9 1.0 copy-start.6
  74.8 23.4 %all-to-all-start.3 = ((bf16[32,24,520]{2,1,0:T(8,128)(2,1)}), bf16[32,24,520]{2,1,0:T(8,128)(2,1)S(1)}, u32[]{:S(2)}, u32[]{:S(2)}) async-start(bf16[32,24,520]{2,1,0:T(8,128)(2,1)} %copy-done.8), calls=%async_computation.3 | async-start | bytes 1966080 | tf_op jit(solution)/shard_map/all_to_all | solution.py:234
  82.0 1.2 copy-start.7
  98.2 19.1 %all-to-all-start.2 = ((bf16[32,16,520]{2,1,0:T(8,128)(2,1)}), bf16[32,16,520]{2,1,0:T(8,128)(2,1)}, u32[]{:S(2)}, u32[]{:S(2)}) async-start(bf16[32,16,520]{2,1,0:T(8,128)(2,1)} %copy-done.9), calls=%async_computation.2 | async-start | bytes 1310720 | tf_op jit(solution)/shard_map/all_to_all | solution.py:234
  104.5 1.7 %copy-start.1 = (f32[520,1152]{1,0:T(8,128)S(1)}, f32[520,1152]{1,0:T(8,128)}, u32[]{:S(2)}) copy-start(f32[520,1152]{1,0:T(8,128)} %master.3) | copy-start | bytes 7188484
  106.2 1.7 %copy-start.3 = (f32[520,1152]{1,0:T(8,128)S(1)}, f32[520,1152]{1,0:T(8,128)}, u32[]{:S(2)}) copy-start(f32[520,1152]{1,0:T(8,128)} %moment1.3) | copy-start | bytes 7188484
  114.8 17.2 %collective-permute-start.4 = (bf16[520,640]{1,0:T(8,128)(2,1)}, bf16[520,640]{1,0:T(8,128)(2,1)S(1)}, u32[]{:S(2)}, u32[]{:S(2)}) collective-permute-start(bf16[520,640]{1,0:T(8,128)(2,1)} %get-tuple-element.28.refs_0_), channel_id=1, source_target_pairs={{0,64},{64,0},{32,96},{96,32},{1,65},{65,1},{33,97},{97,33},{2,66}... | collective-permute-start | bytes 1996808 | tf_op jit(solution)/shard_map/ppermute | solution.py:299
  117.3 1.7 %copy-start.2 = (f32[520,1152]{1,0:T(8,128)S(1)}, f32[520,1152]{1,0:T(8,128)}, u32[]{:S(2)}) copy-start(f32[520,1152]{1,0:T(8,128)} %master.3) | copy-start | bytes 7188484
  119.0 1.7 %copy-start.4 = (f32[520,1152]{1,0:T(8,128)S(1)}, f32[520,1152]{1,0:T(8,128)}, u32[]{:S(2)}) copy-start(f32[520,1152]{1,0:T(8,128)} %moment1.3) | copy-start | bytes 7188484
  120.6 1.7 %copy-start.5 = (f32[520,1152]{1,0:T(8,128)S(1)}, f32[520,1152]{1,0:T(8,128)}, u32[]{:S(2)}) copy-start(f32[520,1152]{1,0:T(8,128)} %moment2.3) | copy-start | bytes 7188484
  127.2 15.4 %collective-permute-start.5 = (bf16[520,512]{1,0:T(8,128)(2,1)S(1)}, bf16[520,512]{1,0:T(8,128)(2,1)S(1)}, u32[]{:S(2)}, u32[]{:S(2)}) collective-permute-start(bf16[520,512]{1,0:T(8,128)(2,1)S(1)} %get-tuple-element.29.refs_1_), channel_id=1, source_target_pairs={{0,64},{64,0},{32,96},{96,32},{1,65},{65,1},{33,97},{97,33},{2,66}... | collective-permute-start | bytes 1597448 | tf_op jit(solution)/shard_map/ppermute | solution.py:302
  127.7 17.7 %collective-permute-start.2 = (bf16[520,640]{1,0:T(8,128)(2,1)}, bf16[520,640]{1,0:T(8,128)(2,1)S(1)}, u32[]{:S(2)}, u32[]{:S(2)}) collective-permute-start(bf16[520,640]{1,0:T(8,128)(2,1)} %get-tuple-element.28.refs_0_), channel_id=1, source_target_pairs={{0,32},{32,0},{64,96},{96,64},{1,33},{33,1},{65,97},{97,65},{2,34}... | collective-permute-start | bytes 1996808 | tf_op jit(solution)/shard_map/ppermute | solution.py:300
  132.1 14.8 %collective-permute-start.6 = (bf16[520,640]{1,0:T(8,128)(2,1)S(1)}, bf16[520,640]{1,0:T(8,128)(2,1)S(1)}, u32[]{:S(2)}, u32[]{:S(2)}) collective-permute-start(bf16[520,640]{1,0:T(8,128)(2,1)S(1)} %collective-permute-done.4.refs_4_), channel_id=1, source_target_pairs={{0,32},{32,0},{64,96},{96,64},{1,33},{33,1},{65,97},{97,65},{2,34}... | collective-permute-start | bytes 1996808 | tf_op jit(solution)/shard_map/ppermute | solution.py:304
  136.8 8.5 %collective-permute-start.3 = (bf16[520,512]{1,0:T(8,128)(2,1)S(1)}, bf16[520,512]{1,0:T(8,128)(2,1)S(1)}, u32[]{:S(2)}, u32[]{:S(2)}) collective-permute-start(bf16[520,512]{1,0:T(8,128)(2,1)S(1)} %get-tuple-element.29.refs_1_), channel_id=1, source_target_pairs={{0,32},{32,0},{64,96},{96,64},{1,33},{33,1},{65,97},{97,65},{2,34}... | collective-permute-start | bytes 1597448 | tf_op jit(solution)/shard_map/ppermute | solution.py:303
  142.5 4.4 %collective-permute-start.7 = (bf16[520,512]{1,0:T(8,128)(2,1)S(1)}, bf16[520,512]{1,0:T(8,128)(2,1)S(1)}, u32[]{:S(2)}, u32[]{:S(2)}) collective-permute-start(bf16[520,512]{1,0:T(8,128)(2,1)S(1)} %collective-permute-done.5.refs_5_), channel_id=1, source_target_pairs={{0,32},{32,0},{64,96},{96,64},{1,33},{33,1},{65,97},{97,65},{2,34}... | collective-permute-start | bytes 1597448 | tf_op jit(solution)/shard_map/ppermute | solution.py:305
  (3 other events, 2.4 us)

commit v3 on v0

v3 whole, which is shorter than its diff:
```python
import functools

import jax
import jax.numpy as jnp
from jax import lax
from jax.experimental import pallas as pl
from jax.experimental.pallas import tpu as pltpu
from jax.sharding import PartitionSpec as P

BLOCK = 128
MIB = 1024 * 1024


beta_first = 0.9
beta_second = 0.999
learn_rate = 0.01
adam_epsilon = 1e-08
first_fix = 1.0 - 0.9**10
second_fix = 1.0 - 0.999**10

CORE = ((0, 1), (1, 0), (2, 3), (3, 2))
ACROSS = ((0, 2), (2, 0), (1, 3), (3, 1))


def head_kernel(place, mine, theirs, hidden, hidden_theirs, own, early, late):
    half = pl.program_id(0)

    def product():
        return jnp.dot(mine[...], hidden[...], preferred_element_type=jnp.float32) + jnp.dot(
            theirs[...], hidden_theirs[...], preferred_element_type=jnp.float32
        )

    @pl.when(half == 0)
    def _():
        both = product().astype(jnp.bfloat16)
        early[...] = both[:, :512]
        late[...] = both[:, 512:]

    @pl.when(half == 1)
    def _():
        own[...] = product()


def head_parts(section, hidden, dlogits, hidden_theirs, dlogits_theirs):
    tokens, rows = dlogits.shape
    quarter = hidden.shape[1] // 4
    left = pl.BlockSpec((rows, tokens), lambda h, place: (0, 0))
    right = pl.BlockSpec((tokens, quarter), lambda h, place: (0, place[0] ^ (2 - 2 * h)))
    shapes = [
        jax.ShapeDtypeStruct((rows, quarter), jnp.float32),
        jax.ShapeDtypeStruct((rows, 512), jnp.bfloat16),
        jax.ShapeDtypeStruct((rows, quarter - 512), jnp.bfloat16),
    ]
    return pl.pallas_call(
        head_kernel,
        grid_spec=pltpu.PrefetchScalarGridSpec(
            num_scalar_prefetch=1,
            grid=(2,),
            in_specs=[left, left, right, right],
            out_specs=[pl.BlockSpec(shape.shape, lambda h, place: (0, 0)) for shape in shapes],
        ),
        out_shape=shapes,
        compiler_params=pltpu.CompilerParams(vmem_limit_bytes=58 * MIB),
        cost_estimate=pl.CostEstimate(
            flops=4 * tokens * rows * 2 * quarter,
            bytes_accessed=4 * tokens * (2 * quarter + rows) + 8 * rows * quarter,
            transcendentals=0,
        ),
    )(section.reshape(1), dlogits.T, dlogits_theirs.T, hidden, hidden_theirs)


SENDERS = 4


def sum_kernel(marks, got, out, acc, parts, ids, place, place_smem, sem):
    step = pl.program_id(0)
    members, _, slab_rows = acc.shape
    senders = got.shape[0]
    blocks = got.shape[2] // BLOCK

    @pl.when(step == 0)
    def _():
        lane = lax.broadcasted_iota(jnp.int32, (1, BLOCK), 1)
        for member in range(members):
            mark = marks[member].astype(jnp.float32)
            numbers = mark[4:5] * 32.0 + mark[5:6] - 1.0
            owner = mark[6:7].astype(jnp.int32)
            spots = jnp.zeros((1, BLOCK), jnp.int32)
            for block in range(blocks):
                lanes = slice(block * BLOCK, (block + 1) * BLOCK)
                ids[member, block : block + 1] = numbers[:, lanes]
                spots = jnp.where(lane == block, owner[:, lanes], spots)
            place[member : member + 1] = spots
        copy = pltpu.make_async_copy(place, place_smem, sem)
        copy.start()
        acc[...] = jnp.zeros_like(acc)
        copy.wait()

    lane = lax.broadcasted_iota(jnp.int32, (BLOCK, slab_rows), 1).astype(jnp.float32)

    def add(sender):
        for block in range(blocks):
            spot = place_smem[step * senders + sender, block]
            acc[spot] += parts[sender * blocks + block]

    for sender in range(senders):
        columns = ids[step * senders + sender].T
        for block in range(blocks):
            part = got[sender, :, block * BLOCK : (block + 1) * BLOCK]
            one_hot = (lane == columns[:, block : block + 1]).astype(jnp.bfloat16)
            parts[sender * blocks + block] = jnp.dot(
                part, one_hot, preferred_element_type=jnp.float32
            )
        if sender > 0:
            add(sender - 1)
    add(senders - 1)

    @pl.when(step == pl.num_programs(0) - 1)
    def _():
        def narrow(spot, carry):
            out[spot] = acc[spot].astype(jnp.bfloat16)
            return carry

        lax.fori_loop(0, members, narrow, 0)


def owner_sums(got, slab_rows):
    members, rows, row_total = got.shape
    blocks = row_total // BLOCK
    shape = (members, rows, slab_rows)
    return pl.pallas_call(
        sum_kernel,
        grid=(members // SENDERS,),
        in_specs=[
            pl.BlockSpec((members, 8, row_total), lambda i: (0, rows // 8 - 1, 0)),
            pl.BlockSpec((SENDERS, rows, row_total), lambda i: (i, 0, 0)),
        ],
        out_specs=pl.BlockSpec(shape, lambda i: (0, 0, 0)),
        out_shape=jax.ShapeDtypeStruct(shape, jnp.bfloat16),
        scratch_shapes=[
            pltpu.VMEM((members, rows, slab_rows), jnp.float32),
            pltpu.VMEM((SENDERS * blocks, rows, slab_rows), jnp.float32),
            pltpu.VMEM((members, blocks, BLOCK), jnp.float32),
            pltpu.VMEM((members, BLOCK), jnp.int32),
            pltpu.SMEM((members, BLOCK), jnp.int32),
            pltpu.SemaphoreType.DMA,
        ],
        compiler_params=pltpu.CompilerParams(vmem_limit_bytes=20 * MIB),
        cost_estimate=pl.CostEstimate(
            flops=2 * members * row_total * slab_rows * 400,
            bytes_accessed=2 * members * rows * (row_total + slab_rows),
            transcendentals=0,
        ),
    )(got, got)


def turned(block):
    size = block.shape[1]
    down = lax.broadcasted_iota(jnp.int32, (size, size), 0)
    unit = (down == lax.broadcasted_iota(jnp.int32, (size, size), 1)).astype(jnp.bfloat16)
    return lax.dot_general(
        unit, block, (((1,), (1,)), ((), ())), preferred_element_type=jnp.float32
    ).astype(jnp.bfloat16)


def message_kernel(counts, ids, first, second, third, out, rest, marks):
    step = pl.program_id(0)
    blocks = ids.shape[0]

    @pl.when(step == 0)
    def _():
        owners = counts.shape[1]
        shape = (owners, owners)
        before = lax.broadcasted_iota(jnp.int32, shape, 0) <= lax.broadcasted_iota(
            jnp.int32, shape, 1
        )
        ends = jnp.dot(
            jnp.broadcast_to(counts[...].astype(jnp.float32), (8, owners)).astype(jnp.bfloat16),
            before.astype(jnp.bfloat16),
            preferred_element_type=jnp.float32,
        )
        at = lax.broadcasted_iota(jnp.int32, ends.shape, 0).astype(jnp.float32)
        owner = jnp.sum((ends <= at).astype(jnp.float32), axis=1, keepdims=True)
        owner = jnp.broadcast_to(owner, ids.shape)
        shifted = ids[...] + 1
        high = (shifted >> 5).astype(jnp.float32)
        low = (shifted & 31).astype(jnp.float32)
        marks[...] = jnp.zeros_like(marks)
        for block in range(blocks):
            lanes = slice(block * BLOCK, (block + 1) * BLOCK)
            row = slice(block, block + 1)
            marks[0:1, lanes] = high[row]
            marks[1:2, lanes] = low[row]
            marks[2:3, lanes] = owner[row]
        tail = turned(third[...]).astype(jnp.float32)
        for member in range(rest.shape[0]):
            both = jnp.concatenate([tail[member * 4 : member * 4 + 4], marks[0:4]], axis=0)
            rest[member] = both.astype(jnp.bfloat16)

    a = turned(first[...])
    b = turned(second[...])
    for member in range(8):
        out[member, :16] = a[member * 16 : member * 16 + 16]
        out[member, 16:32] = b[member * 16 : member * 16 + 16]
        out[member, 32:] = rest[step * 8 + member]


def messages(block_counts, token_ids, token_grad):
    row_total = token_grad.shape[0]
    blocks = row_total // BLOCK
    return pl.pallas_call(
        message_kernel,
        grid=(4,),
        in_specs=[
            pl.BlockSpec(block_counts.shape, lambda i: (0, 0)),
            pl.BlockSpec((blocks, BLOCK), lambda i: (0, 0)),
            pl.BlockSpec((row_total, 128), lambda i: (0, i)),
            pl.BlockSpec((row_total, 128), lambda i: (0, 4 + i)),
            pl.BlockSpec((row_total, 128), lambda i: (0, 8)),
        ],
        out_specs=pl.BlockSpec((8, 40, row_total), lambda i: (i, 0, 0)),
        out_shape=jax.ShapeDtypeStruct((32, 40, row_total), jnp.bfloat16),
        scratch_shapes=[
            pltpu.VMEM((32, 8, row_total), jnp.bfloat16),
            pltpu.VMEM((8, row_total), jnp.float32),
        ],
        compiler_params=pltpu.CompilerParams(vmem_limit_bytes=58 * MIB),
        cost_estimate=pl.CostEstimate(
            flops=2 * row_total * 1152 * 128,
            bytes_accessed=2 * row_total * (1152 + 1280),
            transcendentals=0,
        ),
    )(block_counts, token_ids.reshape(blocks, BLOCK), token_grad, token_grad, token_grad)


def adam_kernel(tail, back, rest, head, far, master, moment1, moment2, *more):
    out_master, out_moment1, out_moment2, out_own, unit, total = more[-6:]
    step = pl.program_id(0)
    _, _, slab_rows = back.shape
    lanes = out_own.shape[1]

    @pl.when(step == 0)
    def _():
        down = lax.broadcasted_iota(jnp.int32, unit.shape, 0)
        unit[...] = (down == lax.broadcasted_iota(jnp.int32, unit.shape, 1)).astype(jnp.bfloat16)

    def upright(part):
        return lax.dot_general(
            unit[...], part, (((1,), (1,)), ((), ())), preferred_element_type=jnp.float32
        )

    if tail:

        @pl.when(step < 4)
        def _():
            total[...] = upright(back[...].reshape(lanes, slab_rows))

        @pl.when(step == 4)
        def _():
            shape = (lanes, 2 * lanes)
            feature = lax.broadcasted_iota(jnp.int32, shape, 0)
            line = lax.broadcasted_iota(jnp.int32, shape, 1)
            select = jnp.logical_and((line // 8) * 4 + line % 8 == feature, line % 8 < 4)
            part = jnp.dot(
                select.astype(jnp.bfloat16),
                rest[...].reshape(2 * lanes, slab_rows),
                preferred_element_type=jnp.float32,
            )
            total[...] = upright(part.astype(jnp.bfloat16))
    else:
        total[...] = upright(back[...].reshape(lanes, slab_rows))

    gradient = total[...] + head[...] + far[...].astype(jnp.float32)
    first = beta_first * moment1[...] + (1.0 - beta_first) * gradient
    second = beta_second * moment2[...] + (1.0 - beta_second) * gradient * gradient
    fresh = master[...] - (learn_rate / first_fix) * first / (
        jnp.sqrt(second * (1.0 / second_fix)) + adam_epsilon
    )
    out_master[...] = fresh
    out_moment1[...] = first
    out_moment2[...] = second
    out_own[...] = fresh.astype(jnp.bfloat16)


def adam(back, group, span, head, far, master, moment1, moment2, earlier=()):
    members, rows, slab_rows = back.shape
    lanes = 128
    first = 4 * group
    tile = pl.BlockSpec((slab_rows, lanes), lambda i: (0, first + i))
    whole = jax.ShapeDtypeStruct(master.shape, jnp.float32)
    return pl.pallas_call(
        functools.partial(adam_kernel, span > 512),
        grid=(span // lanes,),
        in_specs=[
            pl.BlockSpec((8, 16, slab_rows), lambda i: (jnp.minimum(i, 3), group, 0)),
            pl.BlockSpec((members, 8, slab_rows), lambda i: (0, rows // 8 - 1, 0)),
            tile,
            pl.BlockSpec((slab_rows, lanes), lambda i: (0, i)),
            tile,
            tile,
            tile,
        ]
        + [pl.BlockSpec(memory_space=pl.ANY)] * len(earlier),
        out_specs=[tile, tile, tile, pl.BlockSpec((slab_rows, lanes), lambda i: (0, i))],
        out_shape=[whole, whole, whole, jax.ShapeDtypeStruct((slab_rows, span), jnp.bfloat16)],
        scratch_shapes=[
            pltpu.VMEM((slab_rows, slab_rows), jnp.bfloat16),
            pltpu.VMEM((slab_rows, lanes), jnp.float32),
        ],
        input_output_aliases={7 + at: at for at in range(len(earlier))},
        compiler_params=pltpu.CompilerParams(vmem_limit_bytes=58 * MIB),
        cost_estimate=pl.CostEstimate(
            flops=4 * lanes * span * slab_rows,
            bytes_accessed=slab_rows * span * 36,
            transcendentals=slab_rows * span,
        ),
    )(back, back, head, far, master, moment1, moment2, *earlier)


def place_kernel(count, place, *refs):
    parts, out = refs[:-1], refs[-1]
    quarter = out.shape[1] // 4
    for k in range(4):
        start = (place[0] ^ k) * quarter
        for at in range(count):
            part = parts[k * count + at]
            size = part.shape[1]
            out[:, pl.ds(pl.multiple_of(start, 128), size)] = part[...]
            start = start + size


def assemble(section, pieces):
    count = len(pieces[0])
    rows = pieces[0][0].shape[0]
    quarter = sum(part.shape[1] for part in pieces[0])
    some = 176
    parts = [part for piece in pieces for part in piece]
    return pl.pallas_call(
        functools.partial(place_kernel, count),
        grid_spec=pltpu.PrefetchScalarGridSpec(
            num_scalar_prefetch=1,
            grid=(-(-rows // some),),
            in_specs=[pl.BlockSpec((some, part.shape[1]), lambda i, place: (i, 0)) for part in parts],
            out_specs=pl.BlockSpec((some, 4 * quarter), lambda i, place: (i, 0)),
        ),
        out_shape=jax.ShapeDtypeStruct((rows, 4 * quarter), jnp.bfloat16),
        compiler_params=pltpu.CompilerParams(vmem_limit_bytes=20 * MIB),
        cost_estimate=pl.CostEstimate(
            flops=0, bytes_accessed=4 * rows * quarter * 4, transcendentals=0
        ),
    )(section.reshape(1), *parts)


def exchange(rows):
    return lax.all_to_all(rows, "vocab", split_axis=0, concat_axis=0, tiled=True)


def shards(token_grad, token_ids, block_counts, hidden, dlogits, master, moment1, moment2):
    section = lax.axis_index("section").astype(jnp.int32)
    quarter = token_grad.shape[1]
    slab_rows = master.shape[0]
    hidden_theirs = lax.ppermute(hidden, "section", CORE)
    dlogits_theirs = lax.ppermute(dlogits, "section", CORE)
    got = exchange(messages(block_counts, token_ids, token_grad))

    head, early, late = head_parts(section, hidden, dlogits, hidden_theirs, dlogits_theirs)
    got, early, late = lax.optimization_barrier((got, early, late))
    early = lax.ppermute(early, "section", ACROSS)
    late = lax.ppermute(late, "section", ACROSS)
    sums, early = lax.optimization_barrier((owner_sums(got, slab_rows), early))
    back = exchange(sums)

    states = (master, moment1, moment2)
    *states, own_a = adam(back, 0, 512, head, early, *states)
    far_a = lax.ppermute(own_a, "section", ACROSS)
    core_a = lax.ppermute(own_a, "section", CORE)
    *states, own_b = adam(
        back, 1, quarter - 512, head, late, master, moment1, moment2, earlier=states
    )
    turn_b, far_a = lax.optimization_barrier((own_b, far_a))
    far_b = lax.ppermute(turn_b, "section", ACROSS)
    core_b = lax.ppermute(own_b, "section", CORE)
    cross_a = lax.ppermute(far_a, "section", CORE)
    cross_b = lax.ppermute(far_b, "section", CORE)
    refreshed = assemble(
        section,
        ((own_a, own_b), (core_a, core_b), (far_a, far_b), (cross_a, cross_b)),
    )
    return (*states, refreshed)


def solution(mesh):
    placed = (
        P("vocab", "section"),
        P("vocab"),
        P("vocab", None),
        P("section", None),
        P("section", "vocab"),
        P("vocab", "section"),
        P("vocab", "section"),
        P("vocab", "section"),
    )
    return jax.shard_map(
        shards,
        mesh=mesh,
        in_specs=placed,
        out_specs=(
            P("vocab", "section"),
            P("vocab", "section"),
            P("vocab", "section"),
            P("vocab", None),
        ),
        check_vma=False,
    )
```

time: 289 us -> 144 us (0.50)
  waiting for transfers between devices: 210 us -> 68.4 us
  Pallas kernels: 0 us -> 41.3 us
  matrix products: 21.8 us -> 0 us
  local copies, waits for them, and re-layouts: 23.2 us -> 4.27 us
  between operations: 14.1 us -> 0.69 us
  starting transfers between devices: 16.6 us -> 27.6 us
    unnamed x3 -> x0, waiting for transfers between devices: 72 us -> none
    all_to_all x2, waiting for transfers between devices: 95.3 us -> 46.2 us  [exchange(): lax.all_to_all(rows, 'vocab', split_axis=0, concat_axis=0, tiled=True)]
    all_gather x1 -> x0, waiting for transfers between devices: 43.1 us -> none  [shards(): lax.all_gather(new_master.astype(jnp.bfloat16), 'section', axis=1, tiled=...]
    pallas_call x0 -> x6, Pallas kernels: none -> 41.3 us  [the longest x1 13.6 us: owner_sums(): pl.pallas_call(sum_kernel, grid=(members // SENDERS,), in_specs=[pl.Block...]
    ppermute x0 -> x10, waiting for transfers between devices: none -> 22.2 us  [the longest x1 11.2 us: shards(): far_b = lax.ppermute(turn_b, 'section', ACROSS)]
    dot_general x2 -> x0, matrix products: 21.8 us -> none  [the longest x1 14.3 us: shards(): token_sum = jnp.dot(one_hot, flat_rows, preferred_element_type=jnp.float32)]
    ppermute x0 -> x10, starting transfers between devices: none -> 13.9 us  [the longest x1 3.27 us: shards(): cross_b = lax.ppermute(far_b, 'section', CORE)]
    unnamed x9 -> x14, local copies, waits for them, and re-layouts: 16 us -> 4.27 us
  transfers between devices with their start and end apart: 4 -> 12, of which waited for: 3 -> 8; matrix products, arithmetic and copies ran while one was open for 4% -> 0% of each run, Pallas kernels for 0% -> 27%
where the time goes in v3:
time: 144 us; the launch traced here: 142 us
  waiting for transfers between devices  68.4 us (48%)
  Pallas kernels  41.3 us (29%)
  starting transfers between devices  27.6 us (19%)
  local copies, waits for them, and re-layouts  4.27 us (3%)
    all_to_all x2, waiting for transfers between devices, exchange(): lax.all_to_all(rows, 'vocab', split_axis=0, concat_axis=0, tiled=True)  46.2 us
    all_to_all x2, starting transfers between devices, exchange(): lax.all_to_all(rows, 'vocab', split_axis=0, concat_axis=0, tiled=True)  13.7 us
    pallas_call x1, Pallas kernels, owner_sums(): pl.pallas_call(sum_kernel, grid=(members // SENDERS,), in_specs=[pl.Block...  13.6 us
    pallas_call x2, Pallas kernels, adam(): pl.pallas_call(functools.partial(adam_kernel, span > 512), grid=(span //...  13.5 us
    ppermute x1, waiting for transfers between devices, shards(): far_b = lax.ppermute(turn_b, 'section', ACROSS)  11.2 us
    pallas_call x1, Pallas kernels, head_parts(): pl.pallas_call(head_kernel, grid_spec=pltpu.PrefetchScalarGridSpec(num_sc...  6.93 us
    pallas_call x1, Pallas kernels, messages(): pl.pallas_call(message_kernel, grid=(4,), in_specs=[pl.BlockSpec(block_co...  4.8 us
    unnamed x14, local copies, waits for them, and re-layouts  4.27 us
  transfers between devices with their start and end apart: 12, of which 8 were waited for; matrix products, arithmetic and copies ran while one was open for 0% of the time, Pallas kernels for 27%

profile of v3, /device:TPU:25, one launch (start us, length us, event | category | flops | bytes accessed | tf_op | source)
XLA Modules:
  0.0 142.3 jit_solution(18386123484362266260)
XLA Ops:
  1.4 4.8 %shard_map.111 = bf16[32,40,1024]{2,1,0:T(8,128)(2,1)} custom-call(s32[1,32]{1,0:T(1,128)} %counts.1, s32[8,128]{1,0:T(8,128)} %bitcast.5, bf16[1024,1152]{1,0:T(8,128)(2,1)} %third.1, bf16[1024,1152]{1,0:T(8,128)(2,1)} %third.1, bf16[1024,1152]{1,0:T(8,128)(2,1)} %third.1), custom_call_target="tpu_custom_call" | custom-call | flops 301989888 | bytes 4980736 | tf_op jit(solution)/shard_map/pallas_call | solution.py:211
  6.2 8.9 %all-to-all-start = ((bf16[32,40,1024]{2,1,0:T(8,128)(2,1)}), bf16[32,40,1024]{2,1,0:T(8,128)(2,1)S(1)}, u32[]{:S(2)}, u32[]{:S(2)}) async-start(bf16[32,40,1024]{2,1,0:T(8,128)(2,1)} %shard_map.111), calls=%async_computation | async-start | bytes 5242880 | tf_op jit(solution)/shard_map/all_to_all | solution.py:355
  15.8 1.7 %collective-permute-done = bf16[512,520]{0,1:T(8,128)(2,1)} collective-permute-done((bf16[512,520]{0,1:T(8,128)(2,1)S(1)}, bf16[512,520]{0,1:T(8,128)(2,1)}, u32[]{:S(2)}, u32[]{:S(2)}) %collective-permute-start) | collective-permute-done | bytes 532512 | tf_op jit(solution)/shard_map/ppermute | solution.py:363
  17.4 6.9 %shard_map.112 = (f32[520,1152]{1,0:T(8,128)}, bf16[520,512]{1,0:T(8,128)(2,1)}, bf16[520,640]{1,0:T(8,128)(2,1)}) custom-call(s32[1]{0:T(128)} %bitcast.1.place, bf16[520,512]{1,0:T(8,128)(2,1)} %bitcast.4, bf16[520,512]{1,0:T(8,128)(2,1)} %bitcast.3.theirs, bf16[512,4608]{1,0:T(8,128)(2,1)} %hidden.1, bf16[512,4608]{1,0:T(8,128)(2,1)} %collective-permute-done.1.hidden_theirs), custom_call_target="tpu_custom_call" | custom-call | flops 2453667840 | bytes 10575872 | tf_op jit(solution)/shard_map/pallas_call | solution.py:54
  24.4 26.3 %all-to-all-done.marks.got = bf16[32,40,1024]{2,1,0:T(8,128)(2,1)S(1)} async-done(((bf16[32,40,1024]{2,1,0:T(8,128)(2,1)}), bf16[32,40,1024]{2,1,0:T(8,128)(2,1)S(1)}, u32[]{:S(2)}, u32[]{:S(2)}) %all-to-all-start) | async-done | bytes 2621472 | tf_op jit(solution)/shard_map/all_to_all | solution.py:355
  50.6 2.4 %collective-permute-start.2 = (bf16[520,512]{1,0:T(8,128)(2,1)}, bf16[520,512]{1,0:T(8,128)(2,1)S(1)}, u32[]{:S(2)}, u32[]{:S(2)}) collective-permute-start(bf16[520,512]{1,0:T(8,128)(2,1)} %get-tuple-element.25), channel_id=1, source_target_pairs={{0,64},{64,0},{32,96},{96,32},{1,65},{65,1},{33,97},{97,33},{2,66}... | collective-permute-start | bytes 1597448 | tf_op jit(solution)/shard_map/ppermute | solution.py:368
  53.1 13.6 %shard_map.113 = bf16[32,40,520]{2,1,0:T(8,128)(2,1)S(1)} custom-call(bf16[32,40,1024]{2,1,0:T(8,128)(2,1)S(1)} %all-to-all-done.marks.got, bf16[32,40,1024]{2,1,0:T(8,128)(2,1)S(1)} %all-to-all-done.marks.got), custom_call_target="tpu_custom_call" | custom-call | flops 13631488000 | bytes 3952640 | tf_op jit(solution)/shard_map/pallas_call | solution.py:131
  66.6 1.2 copy-done
  67.8 4.8 %all-to-all-start.1 = ((bf16[32,40,520]{2,1,0:T(8,128)(2,1)}), bf16[32,40,520]{2,1,0:T(8,128)(2,1)S(1)}, u32[]{:S(2)}, u32[]{:S(2)}) async-start(bf16[32,40,520]{2,1,0:T(8,128)(2,1)} %copy-done), calls=%async_computation.1 | async-start | bytes 3276800 | tf_op jit(solution)/shard_map/all_to_all | solution.py:355
  72.6 1.1 collective-permute-start.3
  73.7 19.9 %all-to-all-done.1.back.rest = bf16[32,40,520]{2,1,0:T(8,128)(2,1)S(1)} async-done(((bf16[32,40,520]{2,1,0:T(8,128)(2,1)}), bf16[32,40,520]{2,1,0:T(8,128)(2,1)S(1)}, u32[]{:S(2)}, u32[]{:S(2)}) %all-to-all-start.1) | async-done | bytes 1331232 | tf_op jit(solution)/shard_map/all_to_all | solution.py:355
  93.7 1.2 copy-done.3
  94.8 6.0 %shard_map.114 = (f32[520,1152]{1,0:T(8,128)}, f32[520,1152]{1,0:T(8,128)}, f32[520,1152]{1,0:T(8,128)}, bf16[520,512]{1,0:T(8,128)(2,1)}) custom-call(bf16[32,40,520]{2,1,0:T(8,128)(2,1)} %copy-done.3, bf16[32,40,520]{2,1,0:T(8,128)(2,1)} %copy-done.3, f32[520,1152]{1,0:T(8,128)} %get-tuple-element.27.head, bf16[520,512]{1,0:T(8,128)(2,1)} %copy-done.6, ...), custom_call_target="tpu_custom_call" | custom-call | flops 136314880 | bytes 9584640 | tf_op jit(solution)/shard_map/pallas_call | solution.py:291
  101.4 3.7 %collective-permute-done.3.far = bf16[520,640]{1,0:T(8,128)(2,1)S(1)} collective-permute-done((bf16[520,640]{1,0:T(8,128)(2,1)}, bf16[520,640]{1,0:T(8,128)(2,1)S(1)}, u32[]{:S(2)}, u32[]{:S(2)}) %collective-permute-start.3) | collective-permute-done | bytes 665632 | tf_op jit(solution)/shard_map/ppermute | solution.py:369
  105.0 0.8 copy-done.4
  105.9 7.6 %shard_map.115 = (f32[520,1152]{1,0:T(8,128)}, f32[520,1152]{1,0:T(8,128)}, f32[520,1152]{1,0:T(8,128)}, bf16[520,640]{1,0:T(8,128)(2,1)}) custom-call(bf16[32,40,520]{2,1,0:T(8,128)(2,1)} %copy-done.3, bf16[32,40,520]{2,1,0:T(8,128)(2,1)} %copy-done.3, ...), custom_call_target="tpu_custom_call", output_to_operand_aliasing={{0}: (7, {}), {1}: (8, {}), {2}: (9, {})} | custom-call | flops 170393600 | bytes 11980800 | tf_op jit(solution)/shard_map/pallas_call | solution.py:291
  113.5 2.8 %collective-permute-done.6.refs_4_ = bf16[520,512]{1,0:T(8,128)(2,1)S(1)} collective-permute-done((bf16[520,512]{1,0:T(8,128)(2,1)}, bf16[520,512]{1,0:T(8,128)(2,1)S(1)}, u32[]{:S(2)}, u32[]{:S(2)}) %collective-permute-start.6) | collective-permute-done | bytes 532512 | tf_op jit(solution)/shard_map/ppermute | solution.py:375
  116.3 1.6 %collective-permute-start.7 = (bf16[520,640]{1,0:T(8,128)(2,1)}, bf16[520,640]{1,0:T(8,128)(2,1)S(1)}, u32[]{:S(2)}, u32[]{:S(2)}) collective-permute-start(bf16[520,640]{1,0:T(8,128)(2,1)} %get-tuple-element.39.refs_1_), channel_id=1, source_target_pairs={{0,64},{64,0},{32,96},{96,32},{1,65},{65,1},{33,97},{97,33},{2,66}... | collective-permute-start | bytes 1996808 | tf_op jit(solution)/shard_map/ppermute | solution.py:381
  117.9 3.0 %collective-permute-start.5 = (bf16[520,640]{1,0:T(8,128)(2,1)}, bf16[520,640]{1,0:T(8,128)(2,1)S(1)}, u32[]{:S(2)}, u32[]{:S(2)}) collective-permute-start(bf16[520,640]{1,0:T(8,128)(2,1)} %get-tuple-element.39.refs_1_), channel_id=1, source_target_pairs={{0,32},{32,0},{64,96},{96,64},{1,33},{33,1},{65,97},{97,65},{2,34}... | collective-permute-start | bytes 1996808 | tf_op jit(solution)/shard_map/ppermute | solution.py:382
  120.9 11.2 %collective-permute-done.7.refs_5_ = bf16[520,640]{1,0:T(8,128)(2,1)S(1)} collective-permute-done((bf16[520,640]{1,0:T(8,128)(2,1)}, bf16[520,640]{1,0:T(8,128)(2,1)S(1)}, u32[]{:S(2)}, u32[]{:S(2)}) %collective-permute-start.7) | collective-permute-done | bytes 665632 | tf_op jit(solution)/shard_map/ppermute | solution.py:381
  132.1 3.3 %collective-permute-start.9 = (bf16[520,640]{1,0:T(8,128)(2,1)S(1)}, bf16[520,640]{1,0:T(8,128)(2,1)S(1)}, u32[]{:S(2)}, u32[]{:S(2)}) collective-permute-start(bf16[520,640]{1,0:T(8,128)(2,1)S(1)} %collective-permute-done.7.refs_5_), channel_id=1, source_target_pairs={{0,32},{32,0},{64,96},{96,64},{1,33},{33,1},{65,97},{97,65},{2,34}... | collective-permute-start | bytes 1996808 | tf_op jit(solution)/shard_map/ppermute | solution.py:384
  135.9 2.0 %collective-permute-done.4.refs_2_ = bf16[520,512]{1,0:T(8,128)(2,1)S(1)} collective-permute-done((bf16[520,512]{1,0:T(8,128)(2,1)S(1)}, bf16[520,512]{1,0:T(8,128)(2,1)S(1)}, u32[]{:S(2)}, u32[]{:S(2)}) %collective-permute-start.4) | collective-permute-done | bytes 532512 | tf_op jit(solution)/shard_map/ppermute | solution.py:376
  138.6 1.1 copy-done.1
  139.7 2.5 %shard_map.116 = bf16[520,4608]{1,0:T(8,128)(2,1)} custom-call(s32[1]{0:T(128)} %bitcast.1.place, bf16[520,512]{1,0:T(8,128)(2,1)S(1)} %copy-done.2, bf16[520,640]{1,0:T(8,128)(2,1)S(1)} %copy-done.1, bf16[520,512]{1,0:T(8,128)(2,1)S(1)} %collective-permute-done.4.refs_2_, bf16[520,640]{1,0:T(8,128)(2,1)S(1)} %collective-permute-done.5.refs_3_, ...), custom_call_target="tpu_custom_call" | custom-call | bytes 9584640 | tf_op jit(solution)/shard_map/pallas_call | solution.py:338
  (20 shorter events, 3.3 us)
Async XLA Ops:
  0.6 16.8 %collective-permute-start.1 = (bf16[512,4608]{1,0:T(8,128)(2,1)}, bf16[512,4608]{1,0:T(8,128)(2,1)}, u32[]{:S(2)}, u32[]{:S(2)}) collective-permute-start(bf16[512,4608]{1,0:T(8,128)(2,1)} %hidden.1), channel_id=1, source_target_pairs={{0,32},{32,0},{64,96},{96,64},{1,33},{33,1},{65,97},{97,65},{2,34}... | collective-permute-start | bytes 14155784 | tf_op jit(solution)/shard_map/ppermute | solution.py:362
  6.2 8.9 %copy-start.5 = (bf16[512,520]{0,1:T(8,128)(2,1)S(1)}, bf16[512,520]{0,1:T(8,128)(2,1)}, u32[]{:S(2)}) copy-start(bf16[512,520]{0,1:T(8,128)(2,1)} %param.12) | copy-start | bytes 1597444
  6.2 44.4 %all-to-all-start = ((bf16[32,40,1024]{2,1,0:T(8,128)(2,1)}), bf16[32,40,1024]{2,1,0:T(8,128)(2,1)S(1)}, u32[]{:S(2)}, u32[]{:S(2)}) async-start(bf16[32,40,1024]{2,1,0:T(8,128)(2,1)} %shard_map.111), calls=%async_computation | async-start | bytes 5242880 | tf_op jit(solution)/shard_map/all_to_all | solution.py:355
  15.1 2.4 %collective-permute-start = (bf16[512,520]{0,1:T(8,128)(2,1)S(1)}, bf16[512,520]{0,1:T(8,128)(2,1)}, u32[]{:S(2)}, u32[]{:S(2)}) collective-permute-start(bf16[512,520]{0,1:T(8,128)(2,1)S(1)} %copy-done.5), channel_id=1, source_target_pairs={{0,32},{32,0},{64,96},{96,64},{1,33},{33,1},{65,97},{97,65},{2,34}... | collective-permute-start | bytes 1597448 | tf_op jit(solution)/shard_map/ppermute | solution.py:363
  50.6 17.2 %collective-permute-start.2 = (bf16[520,512]{1,0:T(8,128)(2,1)}, bf16[520,512]{1,0:T(8,128)(2,1)S(1)}, u32[]{:S(2)}, u32[]{:S(2)}) collective-permute-start(bf16[520,512]{1,0:T(8,128)(2,1)} %get-tuple-element.25), channel_id=1, source_target_pairs={{0,64},{64,0},{32,96},{96,32},{1,65},{65,1},{33,97},{97,33},{2,66}... | collective-permute-start | bytes 1597448 | tf_op jit(solution)/shard_map/ppermute | solution.py:368
  66.6 1.2 copy-start
  67.8 25.9 %copy-start.6 = (bf16[520,512]{1,0:T(8,128)(2,1)}, bf16[520,512]{1,0:T(8,128)(2,1)S(1)}, u32[]{:S(2)}) copy-start(bf16[520,512]{1,0:T(8,128)(2,1)S(1)} %collective-permute-done.2.far) | copy-start | bytes 1597444
  67.8 25.9 %all-to-all-start.1 = ((bf16[32,40,520]{2,1,0:T(8,128)(2,1)}), bf16[32,40,520]{2,1,0:T(8,128)(2,1)S(1)}, u32[]{:S(2)}, u32[]{:S(2)}) async-start(bf16[32,40,520]{2,1,0:T(8,128)(2,1)} %copy-done), calls=%async_computation.1 | async-start | bytes 3276800 | tf_op jit(solution)/shard_map/all_to_all | solution.py:355
  72.6 32.4 %collective-permute-start.3 = (bf16[520,640]{1,0:T(8,128)(2,1)}, bf16[520,640]{1,0:T(8,128)(2,1)S(1)}, u32[]{:S(2)}, u32[]{:S(2)}) collective-permute-start(bf16[520,640]{1,0:T(8,128)(2,1)} %get-tuple-element.28), channel_id=1, source_target_pairs={{0,64},{64,0},{32,96},{96,32},{1,65},{65,1},{33,97},{97,33},{2,66}... | collective-permute-start | bytes 1996808 | tf_op jit(solution)/shard_map/ppermute | solution.py:369
  93.7 1.2 copy-start.3
  100.8 15.5 %collective-permute-start.6 = (bf16[520,512]{1,0:T(8,128)(2,1)}, bf16[520,512]{1,0:T(8,128)(2,1)S(1)}, u32[]{:S(2)}, u32[]{:S(2)}) collective-permute-start(bf16[520,512]{1,0:T(8,128)(2,1)} %get-tuple-element.36.refs_0_), channel_id=1, source_target_pairs={{0,64},{64,0},{32,96},{96,32},{1,65},{65,1},{33,97},{97,33},{2,66}... | collective-permute-start | bytes 1597448 | tf_op jit(solution)/shard_map/ppermute | solution.py:375
  105.0 0.9 copy-start.4
  105.9 29.5 %copy-start.2 = (bf16[520,512]{1,0:T(8,128)(2,1)S(1)}, bf16[520,512]{1,0:T(8,128)(2,1)}, u32[]{:S(2)}) copy-start(bf16[520,512]{1,0:T(8,128)(2,1)} %get-tuple-element.36.refs_0_) | copy-start | bytes 1597444
  116.3 15.8 %collective-permute-start.7 = (bf16[520,640]{1,0:T(8,128)(2,1)}, bf16[520,640]{1,0:T(8,128)(2,1)S(1)}, u32[]{:S(2)}, u32[]{:S(2)}) collective-permute-start(bf16[520,640]{1,0:T(8,128)(2,1)} %get-tuple-element.39.refs_1_), channel_id=1, source_target_pairs={{0,64},{64,0},{32,96},{96,32},{1,65},{65,1},{33,97},{97,33},{2,66}... | collective-permute-start | bytes 1996808 | tf_op jit(solution)/shard_map/ppermute | solution.py:381
  117.9 20.0 %collective-permute-start.5 = (bf16[520,640]{1,0:T(8,128)(2,1)}, bf16[520,640]{1,0:T(8,128)(2,1)S(1)}, u32[]{:S(2)}, u32[]{:S(2)}) collective-permute-start(bf16[520,640]{1,0:T(8,128)(2,1)} %get-tuple-element.39.refs_1_), channel_id=1, source_target_pairs={{0,32},{32,0},{64,96},{96,64},{1,33},{33,1},{65,97},{97,65},{2,34}... | collective-permute-start | bytes 1996808 | tf_op jit(solution)/shard_map/ppermute | solution.py:382
  132.1 6.5 %collective-permute-start.9 = (bf16[520,640]{1,0:T(8,128)(2,1)S(1)}, bf16[520,640]{1,0:T(8,128)(2,1)S(1)}, u32[]{:S(2)}, u32[]{:S(2)}) collective-permute-start(bf16[520,640]{1,0:T(8,128)(2,1)S(1)} %collective-permute-done.7.refs_5_), channel_id=1, source_target_pairs={{0,32},{32,0},{64,96},{96,64},{1,33},{33,1},{65,97},{97,65},{2,34}... | collective-permute-start | bytes 1996808 | tf_op jit(solution)/shard_map/ppermute | solution.py:384
  135.4 2.5 %collective-permute-start.4 = (bf16[520,512]{1,0:T(8,128)(2,1)S(1)}, bf16[520,512]{1,0:T(8,128)(2,1)S(1)}, u32[]{:S(2)}, u32[]{:S(2)}) collective-permute-start(bf16[520,512]{1,0:T(8,128)(2,1)S(1)} %copy-done.2), channel_id=1, source_target_pairs={{0,32},{32,0},{64,96},{96,64},{1,33},{33,1},{65,97},{97,65},{2,34}... | collective-permute-start | bytes 1597448 | tf_op jit(solution)/shard_map/ppermute | solution.py:376
  135.4 3.3 %collective-permute-start.8 = (bf16[520,512]{1,0:T(8,128)(2,1)S(1)}, bf16[520,512]{1,0:T(8,128)(2,1)S(1)}, u32[]{:S(2)}, u32[]{:S(2)}) collective-permute-start(bf16[520,512]{1,0:T(8,128)(2,1)S(1)} %collective-permute-done.6.refs_4_), channel_id=1, source_target_pairs={{0,32},{32,0},{64,96},{96,64},{1,33},{33,1},{65,97},{97,65},{2,34}... | collective-permute-start | bytes 1597448 | tf_op jit(solution)/shard_map/ppermute | solution.py:383
  138.6 1.1 copy-start.1

commit v4 on v3

--- a/solution.py
+++ b/solution.py
@@ -33,12 +33,12 @@
     @pl.when(half == 0)
     def _():
         both = product().astype(jnp.bfloat16)
-        early[...] = both[:, :512]
-        late[...] = both[:, 512:]
+        early[...] = both[:, :640]
+        late[...] = both[:, 640:]
 
     @pl.when(half == 1)
     def _():
-        own[...] = product()
+        own[...] = product().astype(jnp.bfloat16)
 
 
 def head_parts(section, hidden, dlogits, hidden_theirs, dlogits_theirs):
@@ -47,9 +47,9 @@
     left = pl.BlockSpec((rows, tokens), lambda h, place: (0, 0))
     right = pl.BlockSpec((tokens, quarter), lambda h, place: (0, place[0] ^ (2 - 2 * h)))
     shapes = [
-        jax.ShapeDtypeStruct((rows, quarter), jnp.float32),
-        jax.ShapeDtypeStruct((rows, 512), jnp.bfloat16),
-        jax.ShapeDtypeStruct((rows, quarter - 512), jnp.bfloat16),
+        jax.ShapeDtypeStruct((rows, quarter), jnp.bfloat16),
+        jax.ShapeDtypeStruct((rows, 640), jnp.bfloat16),
+        jax.ShapeDtypeStruct((rows, quarter - 640), jnp.bfloat16),
     ]
     return pl.pallas_call(
         head_kernel,
@@ -233,11 +233,11 @@
     )(block_counts, token_ids.reshape(blocks, BLOCK), token_grad, token_grad, token_grad)
 
 
-def adam_kernel(tail, back, rest, head, far, master, moment1, moment2, *more):
+def adam_kernel(early, tail, back, rest, head, *more):
+    far, (master, moment1, moment2) = more[: len(early)], more[len(early) : len(early) + 3]
     out_master, out_moment1, out_moment2, out_own, unit, total = more[-6:]
     step = pl.program_id(0)
-    _, _, slab_rows = back.shape
-    lanes = out_own.shape[1]
+    slab_rows, lanes = out_own.shape
 
     @pl.when(step == 0)
     def _():
@@ -270,7 +270,10 @@
     else:
         total[...] = upright(back[...].reshape(lanes, slab_rows))
 
-    gradient = total[...] + head[...] + far[...].astype(jnp.float32)
+    from_far = far[0][...].astype(jnp.float32)
+    if len(early) == 2:
+        from_far = jnp.where(step < early[1], from_far, far[1][...].astype(jnp.float32))
+    gradient = total[...] + head[...].astype(jnp.float32) + from_far
     first = beta_first * moment1[...] + (1.0 - beta_first) * gradient
     second = beta_second * moment2[...] + (1.0 - beta_second) * gradient * gradient
     fresh = master[...] - (learn_rate / first_fix) * first / (
@@ -282,20 +285,29 @@
     out_own[...] = fresh.astype(jnp.bfloat16)
 
 
-def adam(back, group, span, head, far, master, moment1, moment2, earlier=()):
+def adam(back, group, lanes, head, far, master, moment1, moment2, earlier=()):
     members, rows, slab_rows = back.shape
-    lanes = 128
-    first = 4 * group
+    quarter = master.shape[1]
+    span = 512 if group == 0 else quarter - 512
+    first = 512 * group // lanes
     tile = pl.BlockSpec((slab_rows, lanes), lambda i: (0, first + i))
+
+    def far_spec(begin, array):
+        last = array.shape[1] // lanes - 1
+        return pl.BlockSpec((slab_rows, lanes), lambda i: (0, jnp.clip(first + i - begin, 0, last)))
+
+    begins = [0, far[0].shape[1] // lanes][: len(far)]
     whole = jax.ShapeDtypeStruct(master.shape, jnp.float32)
     return pl.pallas_call(
-        functools.partial(adam_kernel, span > 512),
+        functools.partial(adam_kernel, [begin - first for begin in begins], span > 512),
         grid=(span // lanes,),
         in_specs=[
-            pl.BlockSpec((8, 16, slab_rows), lambda i: (jnp.minimum(i, 3), group, 0)),
+            pl.BlockSpec(
+                (lanes // 16, 16, slab_rows), lambda i: (jnp.minimum(i, 512 // lanes - 1), group, 0)
+            ),
             pl.BlockSpec((members, 8, slab_rows), lambda i: (0, rows // 8 - 1, 0)),
             tile,
-            pl.BlockSpec((slab_rows, lanes), lambda i: (0, i)),
+            *[far_spec(*pair) for pair in zip(begins, far)],
             tile,
             tile,
             tile,
@@ -307,14 +319,14 @@
             pltpu.VMEM((slab_rows, slab_rows), jnp.bfloat16),
             pltpu.VMEM((slab_rows, lanes), jnp.float32),
         ],
-        input_output_aliases={7 + at: at for at in range(len(earlier))},
-        compiler_params=pltpu.CompilerParams(vmem_limit_bytes=58 * MIB),
+        input_output_aliases={6 + len(far) + at: at for at in range(len(earlier))},
+        compiler_params=pltpu.CompilerParams(vmem_limit_bytes=52 * MIB),
         cost_estimate=pl.CostEstimate(
-            flops=4 * lanes * span * slab_rows,
+            flops=4 * 128 * span * slab_rows,
             bytes_accessed=slab_rows * span * 36,
             transcendentals=slab_rows * span,
         ),
-    )(back, back, head, far, master, moment1, moment2, *earlier)
+    )(back, back, head, *far, master, moment1, moment2, *earlier)
 
 
 def place_kernel(count, place, *refs):
@@ -370,12 +382,11 @@
     sums, early = lax.optimization_barrier((owner_sums(got, slab_rows), early))
     back = exchange(sums)
 
-    states = (master, moment1, moment2)
-    *states, own_a = adam(back, 0, 512, head, early, *states)
+    *states, own_a = adam(back, 0, 256, head, [early], master, moment1, moment2)
     far_a = lax.ppermute(own_a, "section", ACROSS)
     core_a = lax.ppermute(own_a, "section", CORE)
     *states, own_b = adam(
-        back, 1, quarter - 512, head, late, master, moment1, moment2, earlier=states
+        back, 1, 128, head, [early, late], master, moment1, moment2, earlier=states
     )
     turn_b, far_a = lax.optimization_barrier((own_b, far_a))
     far_b = lax.ppermute(turn_b, "section", ACROSS)

time: 144 us -> 141 us (0.979)
  Pallas kernels: 41.3 us -> 39 us
  local copies, waits for them, and re-layouts: 4.27 us -> 2.33 us
  starting transfers between devices: 27.6 us -> 29.5 us
    ppermute x1, waiting for transfers between devices: 3.66 us -> 1.42 us  [shards(): late = lax.ppermute(late, 'section', ACROSS)]
    pallas_call x2, Pallas kernels: 13.5 us -> 11.5 us  [adam(): pl.pallas_call(functools.partial(adam_kernel, [begin - first for begin in...]
    unnamed x14 -> x6, local copies, waits for them, and re-layouts: 4.27 us -> 2.33 us
    ppermute x1, starting transfers between devices: 0.57 us -> 2.49 us  [shards(): far_a = lax.ppermute(own_a, 'section', ACROSS)]
    ppermute x1, waiting for transfers between devices: 2.82 us -> 4.71 us  [shards(): far_a = lax.ppermute(own_a, 'section', ACROSS)]
    ppermute x1, starting transfers between devices: 1.61 us -> 0.01 us  [shards(): far_b = lax.ppermute(turn_b, 'section', ACROSS)]
    ppermute x1, starting transfers between devices: 1.09 us -> 2.57 us  [shards(): late = lax.ppermute(late, 'section', ACROSS)]
    ppermute x1, waiting for transfers between devices: 11.2 us -> 12.7 us  [shards(): far_b = lax.ppermute(turn_b, 'section', ACROSS)]
  transfers between devices with their start and end apart: 12 -> 12, of which waited for: 8 -> 9; matrix products, arithmetic and copies ran while one was open for 0% -> 0% of each run, Pallas kernels for 27% -> 26%
where the time goes in v4:
time: 141 us; the launch traced here: 140 us
  waiting for transfers between devices  68.7 us (49%)
  Pallas kernels  39 us (28%)
  starting transfers between devices  29.5 us (21%)
  local copies, waits for them, and re-layouts  2.33 us (2%)
    all_to_all x2, waiting for transfers between devices, exchange(): lax.all_to_all(rows, 'vocab', split_axis=0, concat_axis=0, tiled=True)  45.2 us
    all_to_all x2, starting transfers between devices, exchange(): lax.all_to_all(rows, 'vocab', split_axis=0, concat_axis=0, tiled=True)  13.9 us
    pallas_call x1, Pallas kernels, owner_sums(): pl.pallas_call(sum_kernel, grid=(members // SENDERS,), in_specs=[pl.Block...  13.6 us
    ppermute x1, waiting for transfers between devices, shards(): far_b = lax.ppermute(turn_b, 'section', ACROSS)  12.7 us
    pallas_call x2, Pallas kernels, adam(): pl.pallas_call(functools.partial(adam_kernel, [begin - first for begin in...  11.5 us
    pallas_call x1, Pallas kernels, head_parts(): pl.pallas_call(head_kernel, grid_spec=pltpu.PrefetchScalarGridSpec(num_sc...  6.56 us
    pallas_call x1, Pallas kernels, messages(): pl.pallas_call(message_kernel, grid=(4,), in_specs=[pl.BlockSpec(block_co...  4.8 us
    ppermute x1, waiting for transfers between devices, shards(): far_a = lax.ppermute(own_a, 'section', ACROSS)  4.71 us
  transfers between devices with their start and end apart: 12, of which 9 were waited for; matrix products, arithmetic and copies ran while one was open for 0% of the time, Pallas kernels for 26%

profile of v4, /device:TPU:25, one launch (start us, length us, event | category | flops | bytes accessed | tf_op | source)
XLA Modules:
  0.0 140.2 jit_solution(5351016179037555046)
XLA Ops:
  0.6 0.8 collective-permute-start.1
  1.4 4.8 %shard_map.111 = bf16[32,40,1024]{2,1,0:T(8,128)(2,1)} custom-call(s32[1,32]{1,0:T(1,128)} %counts.1, s32[8,128]{1,0:T(8,128)} %bitcast.5, bf16[1024,1152]{1,0:T(8,128)(2,1)} %third.1, bf16[1024,1152]{1,0:T(8,128)(2,1)} %third.1, bf16[1024,1152]{1,0:T(8,128)(2,1)} %third.1), custom_call_target="tpu_custom_call" | custom-call | flops 301989888 | bytes 4980736 | tf_op jit(solution)/shard_map/pallas_call | solution.py:211
  6.2 8.9 %all-to-all-start = ((bf16[32,40,1024]{2,1,0:T(8,128)(2,1)}), bf16[32,40,1024]{2,1,0:T(8,128)(2,1)S(1)}, u32[]{:S(2)}, u32[]{:S(2)}) async-start(bf16[32,40,1024]{2,1,0:T(8,128)(2,1)} %shard_map.111), calls=%async_computation | async-start | bytes 5242880 | tf_op jit(solution)/shard_map/all_to_all | solution.py:367
  15.8 1.7 %collective-permute-done = bf16[512,520]{0,1:T(8,128)(2,1)} collective-permute-done((bf16[512,520]{0,1:T(8,128)(2,1)S(1)}, bf16[512,520]{0,1:T(8,128)(2,1)}, u32[]{:S(2)}, u32[]{:S(2)}) %collective-permute-start) | collective-permute-done | bytes 532512 | tf_op jit(solution)/shard_map/ppermute | solution.py:375
  17.4 6.6 %shard_map.112 = (bf16[520,1152]{1,0:T(8,128)(2,1)}, bf16[520,640]{1,0:T(8,128)(2,1)}, bf16[520,512]{1,0:T(8,128)(2,1)}) custom-call(s32[1]{0:T(128)} %bitcast.1.place, bf16[520,512]{1,0:T(8,128)(2,1)} %bitcast.4, bf16[520,512]{1,0:T(8,128)(2,1)} %bitcast.3.theirs, bf16[512,4608]{1,0:T(8,128)(2,1)} %hidden.1, ...), custom_call_target="tpu_custom_call" | custom-call | flops 2453667840 | bytes 10575872 | tf_op jit(solution)/shard_map/pallas_call | solution.py:54
  24.0 26.6 %all-to-all-done.marks.got = bf16[32,40,1024]{2,1,0:T(8,128)(2,1)S(1)} async-done(((bf16[32,40,1024]{2,1,0:T(8,128)(2,1)}), bf16[32,40,1024]{2,1,0:T(8,128)(2,1)S(1)}, u32[]{:S(2)}, u32[]{:S(2)}) %all-to-all-start) | async-done | bytes 2621472 | tf_op jit(solution)/shard_map/all_to_all | solution.py:367
  50.6 2.4 %collective-permute-start.2 = (bf16[520,640]{1,0:T(8,128)(2,1)}, bf16[520,640]{1,0:T(8,128)(2,1)S(1)}, u32[]{:S(2)}, u32[]{:S(2)}) collective-permute-start(bf16[520,640]{1,0:T(8,128)(2,1)} %get-tuple-element.25), channel_id=1, source_target_pairs={{0,64},{64,0},{32,96},{96,32},{1,65},{65,1},{33,97},{97,33},{2,66}... | collective-permute-start | bytes 1996808 | tf_op jit(solution)/shard_map/ppermute | solution.py:380
  53.1 13.6 %shard_map.113 = bf16[32,40,520]{2,1,0:T(8,128)(2,1)S(1)} custom-call(bf16[32,40,1024]{2,1,0:T(8,128)(2,1)S(1)} %all-to-all-done.marks.got, bf16[32,40,1024]{2,1,0:T(8,128)(2,1)S(1)} %all-to-all-done.marks.got), custom_call_target="tpu_custom_call" | custom-call | flops 13631488000 | bytes 3952640 | tf_op jit(solution)/shard_map/pallas_call | solution.py:131
  66.7 1.2 copy-done
  68.1 5.0 %all-to-all-start.1 = ((bf16[32,40,520]{2,1,0:T(8,128)(2,1)}), bf16[32,40,520]{2,1,0:T(8,128)(2,1)S(1)}, u32[]{:S(2)}, u32[]{:S(2)}) async-start(bf16[32,40,520]{2,1,0:T(8,128)(2,1)} %copy-done), calls=%async_computation.1 | async-start | bytes 3276800 | tf_op jit(solution)/shard_map/all_to_all | solution.py:367
  73.1 2.6 %collective-permute-start.3 = (bf16[520,512]{1,0:T(8,128)(2,1)}, bf16[520,512]{1,0:T(8,128)(2,1)S(1)}, u32[]{:S(2)}, u32[]{:S(2)}) collective-permute-start(bf16[520,512]{1,0:T(8,128)(2,1)} %get-tuple-element.29), channel_id=1, source_target_pairs={{0,64},{64,0},{32,96},{96,32},{1,65},{65,1},{33,97},{97,33},{2,66}... | collective-permute-start | bytes 1597448 | tf_op jit(solution)/shard_map/ppermute | solution.py:381
  75.7 18.6 %all-to-all-done.1.back.rest = bf16[32,40,520]{2,1,0:T(8,128)(2,1)S(1)} async-done(((bf16[32,40,520]{2,1,0:T(8,128)(2,1)}), bf16[32,40,520]{2,1,0:T(8,128)(2,1)S(1)}, u32[]{:S(2)}, u32[]{:S(2)}) %all-to-all-start.1) | async-done | bytes 1331232 | tf_op jit(solution)/shard_map/all_to_all | solution.py:367
  94.2 1.2 copy-done.1
  95.4 4.5 %shard_map.114 = (f32[520,1152]{1,0:T(8,128)}, f32[520,1152]{1,0:T(8,128)}, f32[520,1152]{1,0:T(8,128)}, bf16[520,512]{1,0:T(8,128)(2,1)S(1)}) custom-call(bf16[32,40,520]{2,1,0:T(8,128)(2,1)} %copy-done.1, bf16[32,40,520]{2,1,0:T(8,128)(2,1)} %copy-done.1, bf16[520,1152]{1,0:T(8,128)(2,1)} %get-tuple-element.27.head, ...), custom_call_target="tpu_custom_call" | custom-call | flops 136314880 | bytes 9584640 | tf_op jit(solution)/shard_map/pallas_call | solution.py:301
  99.9 2.5 %collective-permute-start.6 = (bf16[520,512]{1,0:T(8,128)(2,1)S(1)}, bf16[520,512]{1,0:T(8,128)(2,1)S(1)}, u32[]{:S(2)}, u32[]{:S(2)}) collective-permute-start(bf16[520,512]{1,0:T(8,128)(2,1)S(1)} %get-tuple-element.36.refs_0_), channel_id=1, source_target_pairs={{0,64},{64,0},{32,96},{96,32},{1,65},{65,1},{33,97},{97,33},{2,66}... | collective-permute-start | bytes 1597448 | tf_op jit(solution)/shard_map/ppermute | solution.py:386
  102.4 1.4 %collective-permute-done.3.more_1_ = bf16[520,512]{1,0:T(8,128)(2,1)S(1)} collective-permute-done((bf16[520,512]{1,0:T(8,128)(2,1)}, bf16[520,512]{1,0:T(8,128)(2,1)S(1)}, u32[]{:S(2)}, u32[]{:S(2)}) %collective-permute-start.3) | collective-permute-done | bytes 532512 | tf_op jit(solution)/shard_map/ppermute | solution.py:381
  103.8 7.1 %shard_map.115 = (f32[520,1152]{1,0:T(8,128)}, f32[520,1152]{1,0:T(8,128)}, f32[520,1152]{1,0:T(8,128)}, bf16[520,640]{1,0:T(8,128)(2,1)S(1)}) custom-call(bf16[32,40,520]{2,1,0:T(8,128)(2,1)} %copy-done.1, bf16[32,40,520]{2,1,0:T(8,128)(2,1)} %copy-done.1, ...), custom_call_target="tpu_custom_call", output_to_operand_aliasing={{0}: (8, {}), {1}: (9, {}), {2}: (10, {})} | custom-call | flops 170393600 | bytes 11980800 | tf_op jit(solution)/shard_map/pallas_call | solution.py:301
  110.9 4.7 %collective-permute-done.6.refs_4_ = bf16[520,512]{1,0:T(8,128)(2,1)S(1)} collective-permute-done((bf16[520,512]{1,0:T(8,128)(2,1)S(1)}, bf16[520,512]{1,0:T(8,128)(2,1)S(1)}, u32[]{:S(2)}, u32[]{:S(2)}) %collective-permute-start.6) | collective-permute-done | bytes 532512 | tf_op jit(solution)/shard_map/ppermute | solution.py:386
  115.6 3.1 %collective-permute-start.5 = (bf16[520,640]{1,0:T(8,128)(2,1)S(1)}, bf16[520,640]{1,0:T(8,128)(2,1)S(1)}, u32[]{:S(2)}, u32[]{:S(2)}) collective-permute-start(bf16[520,640]{1,0:T(8,128)(2,1)S(1)} %get-tuple-element.39.refs_1_), channel_id=1, source_target_pairs={{0,32},{32,0},{64,96},{96,64},{1,33},{33,1},{65,97},{97,65},{2,34}... | collective-permute-start | bytes 1996808 | tf_op jit(solution)/shard_map/ppermute | solution.py:393
  118.7 12.7 %collective-permute-done.7.refs_5_ = bf16[520,640]{1,0:T(8,128)(2,1)S(1)} collective-permute-done((bf16[520,640]{1,0:T(8,128)(2,1)S(1)}, bf16[520,640]{1,0:T(8,128)(2,1)S(1)}, u32[]{:S(2)}, u32[]{:S(2)}) %collective-permute-start.7) | collective-permute-done | bytes 665632 | tf_op jit(solution)/shard_map/ppermute | solution.py:392
  131.4 3.1 %collective-permute-start.9 = (bf16[520,640]{1,0:T(8,128)(2,1)S(1)}, bf16[520,640]{1,0:T(8,128)(2,1)S(1)}, u32[]{:S(2)}, u32[]{:S(2)}) collective-permute-start(bf16[520,640]{1,0:T(8,128)(2,1)S(1)} %collective-permute-done.7.refs_5_), channel_id=1, source_target_pairs={{0,32},{32,0},{64,96},{96,64},{1,33},{33,1},{65,97},{97,65},{2,34}... | collective-permute-start | bytes 1996808 | tf_op jit(solution)/shard_map/ppermute | solution.py:395
  135.0 2.0 %collective-permute-done.4.refs_2_ = bf16[520,512]{1,0:T(8,128)(2,1)S(1)} collective-permute-done((bf16[520,512]{1,0:T(8,128)(2,1)S(1)}, bf16[520,512]{1,0:T(8,128)(2,1)S(1)}, u32[]{:S(2)}, u32[]{:S(2)}) %collective-permute-start.4) | collective-permute-done | bytes 532512 | tf_op jit(solution)/shard_map/ppermute | solution.py:387
  136.9 0.8 collective-permute-done.8.refs_6_
  137.7 2.5 %shard_map.116 = bf16[520,4608]{1,0:T(8,128)(2,1)} custom-call(s32[1]{0:T(128)} %bitcast.1.place, bf16[520,512]{1,0:T(8,128)(2,1)S(1)} %get-tuple-element.36.refs_0_, bf16[520,640]{1,0:T(8,128)(2,1)S(1)} %get-tuple-element.39.refs_1_, bf16[520,512]{1,0:T(8,128)(2,1)S(1)} %collective-permute-done.4.refs_2_, ...), custom_call_target="tpu_custom_call" | custom-call | bytes 9584640 | tf_op jit(solution)/shard_map/pallas_call | solution.py:350
  (12 shorter events, 1.5 us)
Async XLA Ops:
  0.6 16.8 %collective-permute-start.1 = (bf16[512,4608]{1,0:T(8,128)(2,1)}, bf16[512,4608]{1,0:T(8,128)(2,1)}, u32[]{:S(2)}, u32[]{:S(2)}) collective-permute-start(bf16[512,4608]{1,0:T(8,128)(2,1)} %hidden.1), channel_id=1, source_target_pairs={{0,32},{32,0},{64,96},{96,64},{1,33},{33,1},{65,97},{97,65},{2,34}... | collective-permute-start | bytes 14155784 | tf_op jit(solution)/shard_map/ppermute | solution.py:374
  6.2 8.9 %copy-start.2 = (bf16[512,520]{0,1:T(8,128)(2,1)S(1)}, bf16[512,520]{0,1:T(8,128)(2,1)}, u32[]{:S(2)}) copy-start(bf16[512,520]{0,1:T(8,128)(2,1)} %param.12) | copy-start | bytes 1597444
  6.2 44.4 %all-to-all-start = ((bf16[32,40,1024]{2,1,0:T(8,128)(2,1)}), bf16[32,40,1024]{2,1,0:T(8,128)(2,1)S(1)}, u32[]{:S(2)}, u32[]{:S(2)}) async-start(bf16[32,40,1024]{2,1,0:T(8,128)(2,1)} %shard_map.111), calls=%async_computation | async-start | bytes 5242880 | tf_op jit(solution)/shard_map/all_to_all | solution.py:367
  15.1 2.4 %collective-permute-start = (bf16[512,520]{0,1:T(8,128)(2,1)S(1)}, bf16[512,520]{0,1:T(8,128)(2,1)}, u32[]{:S(2)}, u32[]{:S(2)}) collective-permute-start(bf16[512,520]{0,1:T(8,128)(2,1)S(1)} %copy-done.2), channel_id=1, source_target_pairs={{0,32},{32,0},{64,96},{96,64},{1,33},{33,1},{65,97},{97,65},{2,34}... | collective-permute-start | bytes 1597448 | tf_op jit(solution)/shard_map/ppermute | solution.py:375
  50.6 17.5 %collective-permute-start.2 = (bf16[520,640]{1,0:T(8,128)(2,1)}, bf16[520,640]{1,0:T(8,128)(2,1)S(1)}, u32[]{:S(2)}, u32[]{:S(2)}) collective-permute-start(bf16[520,640]{1,0:T(8,128)(2,1)} %get-tuple-element.25), channel_id=1, source_target_pairs={{0,64},{64,0},{32,96},{96,32},{1,65},{65,1},{33,97},{97,33},{2,66}... | collective-permute-start | bytes 1996808 | tf_op jit(solution)/shard_map/ppermute | solution.py:380
  66.7 1.2 copy-start
  68.1 26.1 %all-to-all-start.1 = ((bf16[32,40,520]{2,1,0:T(8,128)(2,1)}), bf16[32,40,520]{2,1,0:T(8,128)(2,1)S(1)}, u32[]{:S(2)}, u32[]{:S(2)}) async-start(bf16[32,40,520]{2,1,0:T(8,128)(2,1)} %copy-done), calls=%async_computation.1 | async-start | bytes 3276800 | tf_op jit(solution)/shard_map/all_to_all | solution.py:367
  73.1 30.7 %collective-permute-start.3 = (bf16[520,512]{1,0:T(8,128)(2,1)}, bf16[520,512]{1,0:T(8,128)(2,1)S(1)}, u32[]{:S(2)}, u32[]{:S(2)}) collective-permute-start(bf16[520,512]{1,0:T(8,128)(2,1)} %get-tuple-element.29), channel_id=1, source_target_pairs={{0,64},{64,0},{32,96},{96,32},{1,65},{65,1},{33,97},{97,33},{2,66}... | collective-permute-start | bytes 1597448 | tf_op jit(solution)/shard_map/ppermute | solution.py:381
  94.2 1.2 copy-start.1
  99.9 15.7 %collective-permute-start.6 = (bf16[520,512]{1,0:T(8,128)(2,1)S(1)}, bf16[520,512]{1,0:T(8,128)(2,1)S(1)}, u32[]{:S(2)}, u32[]{:S(2)}) collective-permute-start(bf16[520,512]{1,0:T(8,128)(2,1)S(1)} %get-tuple-element.36.refs_0_), channel_id=1, source_target_pairs={{0,64},{64,0},{32,96},{96,32},{1,65},{65,1},{33,97},{97,33},{2,66}... | collective-permute-start | bytes 1597448 | tf_op jit(solution)/shard_map/ppermute | solution.py:386
  115.6 15.8 %collective-permute-start.7 = (bf16[520,640]{1,0:T(8,128)(2,1)S(1)}, bf16[520,640]{1,0:T(8,128)(2,1)S(1)}, u32[]{:S(2)}, u32[]{:S(2)}) collective-permute-start(bf16[520,640]{1,0:T(8,128)(2,1)S(1)} %get-tuple-element.39.refs_1_), channel_id=1, source_target_pairs={{0,64},{64,0},{32,96},{96,32},{1,65},{65,1},{33,97},{97,33},{2,66}... | collective-permute-start | bytes 1996808 | tf_op jit(solution)/shard_map/ppermute | solution.py:392
  115.6 21.4 %collective-permute-start.5 = (bf16[520,640]{1,0:T(8,128)(2,1)S(1)}, bf16[520,640]{1,0:T(8,128)(2,1)S(1)}, u32[]{:S(2)}, u32[]{:S(2)}) collective-permute-start(bf16[520,640]{1,0:T(8,128)(2,1)S(1)} %get-tuple-element.39.refs_1_), channel_id=1, source_target_pairs={{0,32},{32,0},{64,96},{96,64},{1,33},{33,1},{65,97},{97,65},{2,34}... | collective-permute-start | bytes 1996808 | tf_op jit(solution)/shard_map/ppermute | solution.py:393
  131.4 6.3 %collective-permute-start.9 = (bf16[520,640]{1,0:T(8,128)(2,1)S(1)}, bf16[520,640]{1,0:T(8,128)(2,1)S(1)}, u32[]{:S(2)}, u32[]{:S(2)}) collective-permute-start(bf16[520,640]{1,0:T(8,128)(2,1)S(1)} %collective-permute-done.7.refs_5_), channel_id=1, source_target_pairs={{0,32},{32,0},{64,96},{96,64},{1,33},{33,1},{65,97},{97,65},{2,34}... | collective-permute-start | bytes 1996808 | tf_op jit(solution)/shard_map/ppermute | solution.py:395
  134.4 2.5 %collective-permute-start.4 = (bf16[520,512]{1,0:T(8,128)(2,1)S(1)}, bf16[520,512]{1,0:T(8,128)(2,1)S(1)}, u32[]{:S(2)}, u32[]{:S(2)}) collective-permute-start(bf16[520,512]{1,0:T(8,128)(2,1)S(1)} %get-tuple-element.36.refs_0_), channel_id=1, source_target_pairs={{0,32},{32,0},{64,96},{96,64},{1,33},{33,1},{65,97},{97,65},{2,34}... | collective-permute-start | bytes 1597448 | tf_op jit(solution)/shard_map/ppermute | solution.py:387
  134.4 3.3 %collective-permute-start.8 = (bf16[520,512]{1,0:T(8,128)(2,1)S(1)}, bf16[520,512]{1,0:T(8,128)(2,1)S(1)}, u32[]{:S(2)}, u32[]{:S(2)}) collective-permute-start(bf16[520,512]{1,0:T(8,128)(2,1)S(1)} %collective-permute-done.6.refs_4_), channel_id=1, source_target_pairs={{0,32},{32,0},{64,96},{96,64},{1,33},{33,1},{65,97},{97,65},{2,34}... | collective-permute-start | bytes 1597448 | tf_op jit(solution)/shard_map/ppermute | solution.py:394

commit v5 on v4

--- a/solution.py
+++ b/solution.py
@@ -146,11 +146,7 @@
             pltpu.SemaphoreType.DMA,
         ],
         compiler_params=pltpu.CompilerParams(vmem_limit_bytes=20 * MIB),
-        cost_estimate=pl.CostEstimate(
-            flops=2 * members * row_total * slab_rows * 400,
-            bytes_accessed=2 * members * rows * (row_total + slab_rows),
-            transcendentals=0,
-        ),
+        cost_estimate=pl.CostEstimate(flops=0, bytes_accessed=0, transcendentals=0),
     )(got, got)
 
 
@@ -376,7 +372,7 @@
     got = exchange(messages(block_counts, token_ids, token_grad))
 
     head, early, late = head_parts(section, hidden, dlogits, hidden_theirs, dlogits_theirs)
-    got, early, late = lax.optimization_barrier((got, early, late))
+    got, late = lax.optimization_barrier((got, late))
     early = lax.ppermute(early, "section", ACROSS)
     late = lax.ppermute(late, "section", ACROSS)
     sums, early = lax.optimization_barrier((owner_sums(got, slab_rows), early))

time: 141 us -> 138 us (0.979)
  waiting for transfers between devices: 68.7 us -> 62.2 us
  starting transfers between devices: 29.5 us -> 32.6 us
    all_to_all x2, waiting for transfers between devices: 45.2 us -> 40.6 us  [exchange(): lax.all_to_all(rows, 'vocab', split_axis=0, concat_axis=0, tiled=True)]
    ppermute x1, starting transfers between devices: 2.49 us -> 4.49 us  [shards(): far_a = lax.ppermute(own_a, 'section', ACROSS)]
  transfers between devices with their start and end apart: 12 -> 12, of which waited for: 9 -> 8; matrix products, arithmetic and copies ran while one was open for 0% -> 0% of each run, Pallas kernels for 26% -> 27%
where the time goes in v5:
time: 138 us; the launch traced here: 137 us
  waiting for transfers between devices  62.2 us (45%)
  Pallas kernels  39 us (28%)
  starting transfers between devices  32.6 us (24%)
  local copies, waits for them, and re-layouts  2.33 us (2%)
    all_to_all x2, waiting for transfers between devices, exchange(): lax.all_to_all(rows, 'vocab', split_axis=0, concat_axis=0, tiled=True)  40.6 us
    all_to_all x2, starting transfers between devices, exchange(): lax.all_to_all(rows, 'vocab', split_axis=0, concat_axis=0, tiled=True)  13.8 us
    pallas_call x1, Pallas kernels, owner_sums(): pl.pallas_call(sum_kernel, grid=(members // SENDERS,), in_specs=[pl.Block...  13.6 us
    pallas_call x2, Pallas kernels, adam(): pl.pallas_call(functools.partial(adam_kernel, [begin - first for begin in...  11.5 us
    ppermute x1, waiting for transfers between devices, shards(): far_b = lax.ppermute(turn_b, 'section', ACROSS)  11.5 us
    pallas_call x1, Pallas kernels, head_parts(): pl.pallas_call(head_kernel, grid_spec=pltpu.PrefetchScalarGridSpec(num_sc...  6.53 us
    pallas_call x1, Pallas kernels, messages(): pl.pallas_call(message_kernel, grid=(4,), in_specs=[pl.BlockSpec(block_co...  4.8 us
    ppermute x1, starting transfers between devices, shards(): far_a = lax.ppermute(own_a, 'section', ACROSS)  4.49 us
  transfers between devices with their start and end apart: 12, of which 8 were waited for; matrix products, arithmetic and copies ran while one was open for 0% of the time, Pallas kernels for 27%

profile of v5, /device:TPU:25, one launch (start us, length us, event | category | flops | bytes accessed | tf_op | source)
XLA Modules:
  0.0 136.8 jit_solution(16197655153638459422)
XLA Ops:
  0.6 0.8 collective-permute-start.1
  1.4 4.8 %shard_map.111 = bf16[32,40,1024]{2,1,0:T(8,128)(2,1)} custom-call(s32[1,32]{1,0:T(1,128)} %counts.1, s32[8,128]{1,0:T(8,128)} %bitcast.5, bf16[1024,1152]{1,0:T(8,128)(2,1)} %third.1, bf16[1024,1152]{1,0:T(8,128)(2,1)} %third.1, bf16[1024,1152]{1,0:T(8,128)(2,1)} %third.1), custom_call_target="tpu_custom_call" | custom-call | flops 301989888 | bytes 4980736 | tf_op jit(solution)/shard_map/pallas_call | solution.py:207
  6.2 8.9 %all-to-all-start = ((bf16[32,40,1024]{2,1,0:T(8,128)(2,1)}), bf16[32,40,1024]{2,1,0:T(8,128)(2,1)S(1)}, u32[]{:S(2)}, u32[]{:S(2)}) async-start(bf16[32,40,1024]{2,1,0:T(8,128)(2,1)} %shard_map.111), calls=%async_computation | async-start | bytes 5242880 | tf_op jit(solution)/shard_map/all_to_all | solution.py:363
  15.8 1.7 %collective-permute-done = bf16[512,520]{0,1:T(8,128)(2,1)} collective-permute-done((bf16[512,520]{0,1:T(8,128)(2,1)S(1)}, bf16[512,520]{0,1:T(8,128)(2,1)}, u32[]{:S(2)}, u32[]{:S(2)}) %collective-permute-start) | collective-permute-done | bytes 532512 | tf_op jit(solution)/shard_map/ppermute | solution.py:371
  17.4 6.5 %shard_map.112 = (bf16[520,1152]{1,0:T(8,128)(2,1)}, bf16[520,640]{1,0:T(8,128)(2,1)}, bf16[520,512]{1,0:T(8,128)(2,1)}) custom-call(s32[1]{0:T(128)} %bitcast.1.place, bf16[520,512]{1,0:T(8,128)(2,1)} %bitcast.4, bf16[520,512]{1,0:T(8,128)(2,1)} %bitcast.3.theirs, bf16[512,4608]{1,0:T(8,128)(2,1)} %hidden.1, ...), custom_call_target="tpu_custom_call" | custom-call | flops 2453667840 | bytes 10575872 | tf_op jit(solution)/shard_map/pallas_call | solution.py:54
  24.0 2.4 %collective-permute-start.2 = (bf16[520,640]{1,0:T(8,128)(2,1)}, bf16[520,640]{1,0:T(8,128)(2,1)S(1)}, u32[]{:S(2)}, u32[]{:S(2)}) collective-permute-start(bf16[520,640]{1,0:T(8,128)(2,1)} %get-tuple-element.23), channel_id=1, source_target_pairs={{0,64},{64,0},{32,96},{96,32},{1,65},{65,1},{33,97},{97,33},{2,66}... | collective-permute-start | bytes 1996808 | tf_op jit(solution)/shard_map/ppermute | solution.py:376
  26.4 24.2 %all-to-all-done.marks.got = bf16[32,40,1024]{2,1,0:T(8,128)(2,1)S(1)} async-done(((bf16[32,40,1024]{2,1,0:T(8,128)(2,1)}), bf16[32,40,1024]{2,1,0:T(8,128)(2,1)S(1)}, u32[]{:S(2)}, u32[]{:S(2)}) %all-to-all-start) | async-done | bytes 2621472 | tf_op jit(solution)/shard_map/all_to_all | solution.py:363
  50.6 13.6 %shard_map.113 = bf16[32,40,520]{2,1,0:T(8,128)(2,1)S(1)} custom-call(bf16[32,40,1024]{2,1,0:T(8,128)(2,1)S(1)} %all-to-all-done.marks.got, bf16[32,40,1024]{2,1,0:T(8,128)(2,1)S(1)} %all-to-all-done.marks.got), custom_call_target="tpu_custom_call" | custom-call | tf_op jit(solution)/shard_map/pallas_call | solution.py:131
  64.2 1.2 copy-done
  65.4 5.0 %all-to-all-start.1 = ((bf16[32,40,520]{2,1,0:T(8,128)(2,1)}), bf16[32,40,520]{2,1,0:T(8,128)(2,1)S(1)}, u32[]{:S(2)}, u32[]{:S(2)}) async-start(bf16[32,40,520]{2,1,0:T(8,128)(2,1)} %copy-done), calls=%async_computation.1 | async-start | bytes 3276800 | tf_op jit(solution)/shard_map/all_to_all | solution.py:363
  70.4 2.5 %collective-permute-start.3 = (bf16[520,512]{1,0:T(8,128)(2,1)S(1)}, bf16[520,512]{1,0:T(8,128)(2,1)S(1)}, u32[]{:S(2)}, u32[]{:S(2)}) collective-permute-start(bf16[520,512]{1,0:T(8,128)(2,1)S(1)} %copy-done.3), channel_id=1, source_target_pairs={{0,64},{64,0},{32,96},{96,32},{1,65},{65,1},{33,97},{97,33},{2,66}... | collective-permute-start | bytes 1597448 | tf_op jit(solution)/shard_map/ppermute | solution.py:377
  72.9 16.4 %all-to-all-done.1.back.rest = bf16[32,40,520]{2,1,0:T(8,128)(2,1)S(1)} async-done(((bf16[32,40,520]{2,1,0:T(8,128)(2,1)}), bf16[32,40,520]{2,1,0:T(8,128)(2,1)S(1)}, u32[]{:S(2)}, u32[]{:S(2)}) %all-to-all-start.1) | async-done | bytes 1331232 | tf_op jit(solution)/shard_map/all_to_all | solution.py:363
  89.3 1.2 copy-done.1
  90.4 4.5 %shard_map.114 = (f32[520,1152]{1,0:T(8,128)}, f32[520,1152]{1,0:T(8,128)}, f32[520,1152]{1,0:T(8,128)}, bf16[520,512]{1,0:T(8,128)(2,1)S(1)}) custom-call(bf16[32,40,520]{2,1,0:T(8,128)(2,1)} %copy-done.1, bf16[32,40,520]{2,1,0:T(8,128)(2,1)} %copy-done.1, bf16[520,1152]{1,0:T(8,128)(2,1)} %get-tuple-element.25.head, ...), custom_call_target="tpu_custom_call" | custom-call | flops 136314880 | bytes 9584640 | tf_op jit(solution)/shard_map/pallas_call | solution.py:297
  94.9 4.5 %collective-permute-start.6 = (bf16[520,512]{1,0:T(8,128)(2,1)S(1)}, bf16[520,512]{1,0:T(8,128)(2,1)S(1)}, u32[]{:S(2)}, u32[]{:S(2)}) collective-permute-start(bf16[520,512]{1,0:T(8,128)(2,1)S(1)} %get-tuple-element.34.refs_0_), channel_id=1, source_target_pairs={{0,64},{64,0},{32,96},{96,32},{1,65},{65,1},{33,97},{97,33},{2,66}... | collective-permute-start | bytes 1597448 | tf_op jit(solution)/shard_map/ppermute | solution.py:382
  99.4 1.3 collective-permute-done.3.more_1_
  100.7 7.0 %shard_map.115 = (f32[520,1152]{1,0:T(8,128)}, f32[520,1152]{1,0:T(8,128)}, f32[520,1152]{1,0:T(8,128)}, bf16[520,640]{1,0:T(8,128)(2,1)S(1)}) custom-call(bf16[32,40,520]{2,1,0:T(8,128)(2,1)} %copy-done.1, bf16[32,40,520]{2,1,0:T(8,128)(2,1)} %copy-done.1, ...), custom_call_target="tpu_custom_call", output_to_operand_aliasing={{0}: (8, {}), {1}: (9, {}), {2}: (10, {})} | custom-call | flops 170393600 | bytes 11980800 | tf_op jit(solution)/shard_map/pallas_call | solution.py:297
  107.7 4.4 %collective-permute-done.6.refs_4_ = bf16[520,512]{1,0:T(8,128)(2,1)S(1)} collective-permute-done((bf16[520,512]{1,0:T(8,128)(2,1)S(1)}, bf16[520,512]{1,0:T(8,128)(2,1)S(1)}, u32[]{:S(2)}, u32[]{:S(2)}) %collective-permute-start.6) | collective-permute-done | bytes 532512 | tf_op jit(solution)/shard_map/ppermute | solution.py:382
  112.1 3.6 %collective-permute-start.5 = (bf16[520,640]{1,0:T(8,128)(2,1)S(1)}, bf16[520,640]{1,0:T(8,128)(2,1)S(1)}, u32[]{:S(2)}, u32[]{:S(2)}) collective-permute-start(bf16[520,640]{1,0:T(8,128)(2,1)S(1)} %get-tuple-element.37.refs_1_), channel_id=1, source_target_pairs={{0,32},{32,0},{64,96},{96,64},{1,33},{33,1},{65,97},{97,65},{2,34}... | collective-permute-start | bytes 1996808 | tf_op jit(solution)/shard_map/ppermute | solution.py:389
  115.7 11.5 %collective-permute-done.7.refs_5_ = bf16[520,640]{1,0:T(8,128)(2,1)S(1)} collective-permute-done((bf16[520,640]{1,0:T(8,128)(2,1)S(1)}, bf16[520,640]{1,0:T(8,128)(2,1)S(1)}, u32[]{:S(2)}, u32[]{:S(2)}) %collective-permute-start.7) | collective-permute-done | bytes 665632 | tf_op jit(solution)/shard_map/ppermute | solution.py:388
  127.2 3.7 %collective-permute-start.9 = (bf16[520,640]{1,0:T(8,128)(2,1)S(1)}, bf16[520,640]{1,0:T(8,128)(2,1)S(1)}, u32[]{:S(2)}, u32[]{:S(2)}) collective-permute-start(bf16[520,640]{1,0:T(8,128)(2,1)S(1)} %collective-permute-done.7.refs_5_), channel_id=1, source_target_pairs={{0,32},{32,0},{64,96},{96,64},{1,33},{33,1},{65,97},{97,65},{2,34}... | collective-permute-start | bytes 1996808 | tf_op jit(solution)/shard_map/ppermute | solution.py:391
  131.5 2.0 %collective-permute-done.4.refs_2_ = bf16[520,512]{1,0:T(8,128)(2,1)S(1)} collective-permute-done((bf16[520,512]{1,0:T(8,128)(2,1)S(1)}, bf16[520,512]{1,0:T(8,128)(2,1)S(1)}, u32[]{:S(2)}, u32[]{:S(2)}) %collective-permute-start.4) | collective-permute-done | bytes 532512 | tf_op jit(solution)/shard_map/ppermute | solution.py:383
  133.5 0.8 collective-permute-done.8.refs_6_
  134.2 2.5 %shard_map.116 = bf16[520,4608]{1,0:T(8,128)(2,1)} custom-call(s32[1]{0:T(128)} %bitcast.1.place, bf16[520,512]{1,0:T(8,128)(2,1)S(1)} %get-tuple-element.34.refs_0_, bf16[520,640]{1,0:T(8,128)(2,1)S(1)} %get-tuple-element.37.refs_1_, bf16[520,512]{1,0:T(8,128)(2,1)S(1)} %collective-permute-done.4.refs_2_, ...), custom_call_target="tpu_custom_call" | custom-call | bytes 9584640 | tf_op jit(solution)/shard_map/pallas_call | solution.py:346
  (14 shorter events, 1.2 us)
Async XLA Ops:
  0.6 16.8 %collective-permute-start.1 = (bf16[512,4608]{1,0:T(8,128)(2,1)}, bf16[512,4608]{1,0:T(8,128)(2,1)}, u32[]{:S(2)}, u32[]{:S(2)}) collective-permute-start(bf16[512,4608]{1,0:T(8,128)(2,1)} %hidden.1), channel_id=1, source_target_pairs={{0,32},{32,0},{64,96},{96,64},{1,33},{33,1},{65,97},{97,65},{2,34}... | collective-permute-start | bytes 14155784 | tf_op jit(solution)/shard_map/ppermute | solution.py:370
  6.2 8.9 %copy-start.2 = (bf16[512,520]{0,1:T(8,128)(2,1)S(1)}, bf16[512,520]{0,1:T(8,128)(2,1)}, u32[]{:S(2)}) copy-start(bf16[512,520]{0,1:T(8,128)(2,1)} %param.12) | copy-start | bytes 1597444
  6.2 44.4 %all-to-all-start = ((bf16[32,40,1024]{2,1,0:T(8,128)(2,1)}), bf16[32,40,1024]{2,1,0:T(8,128)(2,1)S(1)}, u32[]{:S(2)}, u32[]{:S(2)}) async-start(bf16[32,40,1024]{2,1,0:T(8,128)(2,1)} %shard_map.111), calls=%async_computation | async-start | bytes 5242880 | tf_op jit(solution)/shard_map/all_to_all | solution.py:363
  15.1 2.4 %collective-permute-start = (bf16[512,520]{0,1:T(8,128)(2,1)S(1)}, bf16[512,520]{0,1:T(8,128)(2,1)}, u32[]{:S(2)}, u32[]{:S(2)}) collective-permute-start(bf16[512,520]{0,1:T(8,128)(2,1)S(1)} %copy-done.2), channel_id=1, source_target_pairs={{0,32},{32,0},{64,96},{96,64},{1,33},{33,1},{65,97},{97,65},{2,34}... | collective-permute-start | bytes 1597448 | tf_op jit(solution)/shard_map/ppermute | solution.py:371
  24.0 41.4 %collective-permute-start.2 = (bf16[520,640]{1,0:T(8,128)(2,1)}, bf16[520,640]{1,0:T(8,128)(2,1)S(1)}, u32[]{:S(2)}, u32[]{:S(2)}) collective-permute-start(bf16[520,640]{1,0:T(8,128)(2,1)} %get-tuple-element.23), channel_id=1, source_target_pairs={{0,64},{64,0},{32,96},{96,32},{1,65},{65,1},{33,97},{97,33},{2,66}... | collective-permute-start | bytes 1996808 | tf_op jit(solution)/shard_map/ppermute | solution.py:376
  64.2 1.2 copy-start
  65.4 5.0 %copy-start.3 = (bf16[520,512]{1,0:T(8,128)(2,1)S(1)}, bf16[520,512]{1,0:T(8,128)(2,1)}, u32[]{:S(2)}) copy-start(bf16[520,512]{1,0:T(8,128)(2,1)} %get-tuple-element.27) | copy-start | bytes 1597444
  65.4 23.9 %all-to-all-start.1 = ((bf16[32,40,520]{2,1,0:T(8,128)(2,1)}), bf16[32,40,520]{2,1,0:T(8,128)(2,1)S(1)}, u32[]{:S(2)}, u32[]{:S(2)}) async-start(bf16[32,40,520]{2,1,0:T(8,128)(2,1)} %copy-done), calls=%async_computation.1 | async-start | bytes 3276800 | tf_op jit(solution)/shard_map/all_to_all | solution.py:363
  70.4 30.3 %collective-permute-start.3 = (bf16[520,512]{1,0:T(8,128)(2,1)S(1)}, bf16[520,512]{1,0:T(8,128)(2,1)S(1)}, u32[]{:S(2)}, u32[]{:S(2)}) collective-permute-start(bf16[520,512]{1,0:T(8,128)(2,1)S(1)} %copy-done.3), channel_id=1, source_target_pairs={{0,64},{64,0},{32,96},{96,32},{1,65},{65,1},{33,97},{97,33},{2,66}... | collective-permute-start | bytes 1597448 | tf_op jit(solution)/shard_map/ppermute | solution.py:377
  89.3 1.2 copy-start.1
  94.9 17.2 %collective-permute-start.6 = (bf16[520,512]{1,0:T(8,128)(2,1)S(1)}, bf16[520,512]{1,0:T(8,128)(2,1)S(1)}, u32[]{:S(2)}, u32[]{:S(2)}) collective-permute-start(bf16[520,512]{1,0:T(8,128)(2,1)S(1)} %get-tuple-element.34.refs_0_), channel_id=1, source_target_pairs={{0,64},{64,0},{32,96},{96,32},{1,65},{65,1},{33,97},{97,33},{2,66}... | collective-permute-start | bytes 1597448 | tf_op jit(solution)/shard_map/ppermute | solution.py:382
  112.1 15.1 %collective-permute-start.7 = (bf16[520,640]{1,0:T(8,128)(2,1)S(1)}, bf16[520,640]{1,0:T(8,128)(2,1)S(1)}, u32[]{:S(2)}, u32[]{:S(2)}) collective-permute-start(bf16[520,640]{1,0:T(8,128)(2,1)S(1)} %get-tuple-element.37.refs_1_), channel_id=1, source_target_pairs={{0,64},{64,0},{32,96},{96,32},{1,65},{65,1},{33,97},{97,33},{2,66}... | collective-permute-start | bytes 1996808 | tf_op jit(solution)/shard_map/ppermute | solution.py:388
  112.1 21.4 %collective-permute-start.5 = (bf16[520,640]{1,0:T(8,128)(2,1)S(1)}, bf16[520,640]{1,0:T(8,128)(2,1)S(1)}, u32[]{:S(2)}, u32[]{:S(2)}) collective-permute-start(bf16[520,640]{1,0:T(8,128)(2,1)S(1)} %get-tuple-element.37.refs_1_), channel_id=1, source_target_pairs={{0,32},{32,0},{64,96},{96,64},{1,33},{33,1},{65,97},{97,65},{2,34}... | collective-permute-start | bytes 1996808 | tf_op jit(solution)/shard_map/ppermute | solution.py:389
  127.2 7.0 %collective-permute-start.9 = (bf16[520,640]{1,0:T(8,128)(2,1)S(1)}, bf16[520,640]{1,0:T(8,128)(2,1)S(1)}, u32[]{:S(2)}, u32[]{:S(2)}) collective-permute-start(bf16[520,640]{1,0:T(8,128)(2,1)S(1)} %collective-permute-done.7.refs_5_), channel_id=1, source_target_pairs={{0,32},{32,0},{64,96},{96,64},{1,33},{33,1},{65,97},{97,65},{2,34}... | collective-permute-start | bytes 1996808 | tf_op jit(solution)/shard_map/ppermute | solution.py:391
  131.0 2.5 %collective-permute-start.4 = (bf16[520,512]{1,0:T(8,128)(2,1)S(1)}, bf16[520,512]{1,0:T(8,128)(2,1)S(1)}, u32[]{:S(2)}, u32[]{:S(2)}) collective-permute-start(bf16[520,512]{1,0:T(8,128)(2,1)S(1)} %get-tuple-element.34.refs_0_), channel_id=1, source_target_pairs={{0,32},{32,0},{64,96},{96,64},{1,33},{33,1},{65,97},{97,65},{2,34}... | collective-permute-start | bytes 1597448 | tf_op jit(solution)/shard_map/ppermute | solution.py:383
  131.0 3.3 %collective-permute-start.8 = (bf16[520,512]{1,0:T(8,128)(2,1)S(1)}, bf16[520,512]{1,0:T(8,128)(2,1)S(1)}, u32[]{:S(2)}, u32[]{:S(2)}) collective-permute-start(bf16[520,512]{1,0:T(8,128)(2,1)S(1)} %collective-permute-done.6.refs_4_), channel_id=1, source_target_pairs={{0,32},{32,0},{64,96},{96,64},{1,33},{33,1},{65,97},{97,65},{2,34}... | collective-permute-start | bytes 1597448 | tf_op jit(solution)/shard_map/ppermute | solution.py:390

commit v6 on v5

--- a/solution.py
+++ b/solution.py
@@ -72,31 +72,39 @@
 SENDERS = 4
 
 
-def sum_kernel(marks, got, out, acc, parts, ids, place, place_smem, sem):
+MAIN = 512
+
+
+def sum_kernel(
+    marks, got, out, acc, parts, tails, last, ids, keys, place, place_smem, sem
+):
     step = pl.program_id(0)
-    members, _, slab_rows = acc.shape
+    members, rows, _ = acc.shape
     senders = got.shape[0]
     blocks = got.shape[2] // BLOCK
+    lane = lax.broadcasted_iota(jnp.int32, (1, BLOCK), 1)
 
     @pl.when(step == 0)
     def _():
-        lane = lax.broadcasted_iota(jnp.int32, (1, BLOCK), 1)
         for member in range(members):
             mark = marks[member].astype(jnp.float32)
             numbers = mark[4:5] * 32.0 + mark[5:6] - 1.0
             owner = mark[6:7].astype(jnp.int32)
             spots = jnp.zeros((1, BLOCK), jnp.int32)
+            key = jnp.full((1, BLOCK), -1, jnp.int32)
             for block in range(blocks):
                 lanes = slice(block * BLOCK, (block + 1) * BLOCK)
                 ids[member, block : block + 1] = numbers[:, lanes]
                 spots = jnp.where(lane == block, owner[:, lanes], spots)
+                key = jnp.where(lane // 8 == block, owner[:, lanes] * 8 + lane % 8, key)
             place[member : member + 1] = spots
+            keys[member : member + 1] = key
         copy = pltpu.make_async_copy(place, place_smem, sem)
         copy.start()
         acc[...] = jnp.zeros_like(acc)
         copy.wait()
 
-    lane = lax.broadcasted_iota(jnp.int32, (BLOCK, slab_rows), 1).astype(jnp.float32)
+    slot = lax.broadcasted_iota(jnp.int32, (BLOCK, MAIN), 1).astype(jnp.float32)
 
     def add(sender):
         for block in range(blocks):
@@ -105,29 +113,56 @@
 
     for sender in range(senders):
         columns = ids[step * senders + sender].T
+        ends = []
         for block in range(blocks):
             part = got[sender, :, block * BLOCK : (block + 1) * BLOCK]
-            one_hot = (lane == columns[:, block : block + 1]).astype(jnp.bfloat16)
+            column = columns[:, block : block + 1]
+            one_hot = (slot == column).astype(jnp.bfloat16)
             parts[sender * blocks + block] = jnp.dot(
                 part, one_hot, preferred_element_type=jnp.float32
             )
+            end = jnp.where(lane // 8 == block, MAIN + lane % 8, -7).astype(jnp.float32)
+            ends.append((end == column).astype(jnp.bfloat16))
+        tails[step * senders + sender] = jnp.dot(
+            got[sender], jnp.concatenate(ends, axis=0), preferred_element_type=jnp.float32
+        ).astype(jnp.bfloat16)
         if sender > 0:
             add(sender - 1)
     add(senders - 1)
 
     @pl.when(step == pl.num_programs(0) - 1)
     def _():
-        def narrow(spot, carry):
-            out[spot] = acc[spot].astype(jnp.bfloat16)
+        line = lax.broadcasted_iota(jnp.int32, (8 * members, BLOCK), 0)
+        total = jnp.zeros((8 * members, rows), jnp.float32)
+        for member in range(members):
+            total += lax.dot_general(
+                (line == keys[member : member + 1]).astype(jnp.bfloat16),
+                tails[member],
+                (((1,), (1,)), ((), ())),
+                preferred_element_type=jnp.float32,
+            )
+        last[...] = jnp.zeros_like(last)
+        last[:, :rows] = total
+        upper = lax.broadcasted_iota(jnp.int32, (8, BLOCK), 0) < 4
+
+        def leave(spot, carry):
+            out[spot, :32] = acc[spot, :32].astype(jnp.bfloat16)
+            tail = last[pl.ds(pl.multiple_of(8 * spot, 8), 8)]
+            under = [pltpu.roll(tail, 4, 0), tail, jnp.zeros_like(tail), jnp.zeros_like(tail)]
+            for at in range(4):
+                lanes = slice(at * BLOCK, (at + 1) * BLOCK)
+                out[spot, 32:, lanes] = jnp.where(upper, acc[spot, 32:, lanes], under[at]).astype(
+                    jnp.bfloat16
+                )
             return carry
 
-        lax.fori_loop(0, members, narrow, 0)
-
-
-def owner_sums(got, slab_rows):
+        lax.fori_loop(0, members, leave, 0)
+
+
+def owner_sums(got):
     members, rows, row_total = got.shape
     blocks = row_total // BLOCK
-    shape = (members, rows, slab_rows)
+    shape = (members, rows, MAIN)
     return pl.pallas_call(
         sum_kernel,
         grid=(members // SENDERS,),
@@ -138,9 +173,12 @@
         out_specs=pl.BlockSpec(shape, lambda i: (0, 0, 0)),
         out_shape=jax.ShapeDtypeStruct(shape, jnp.bfloat16),
         scratch_shapes=[
-            pltpu.VMEM((members, rows, slab_rows), jnp.float32),
-            pltpu.VMEM((SENDERS * blocks, rows, slab_rows), jnp.float32),
+            pltpu.VMEM((members, rows, MAIN), jnp.float32),
+            pltpu.VMEM((SENDERS * blocks, rows, MAIN), jnp.float32),
+            pltpu.VMEM((members, rows, BLOCK), jnp.bfloat16),
+            pltpu.VMEM((8 * members, BLOCK), jnp.float32),
             pltpu.VMEM((members, blocks, BLOCK), jnp.float32),
+            pltpu.VMEM((members, BLOCK), jnp.int32),
             pltpu.VMEM((members, BLOCK), jnp.int32),
             pltpu.SMEM((members, BLOCK), jnp.int32),
             pltpu.SemaphoreType.DMA,
@@ -229,11 +267,13 @@
     )(block_counts, token_ids.reshape(blocks, BLOCK), token_grad, token_grad, token_grad)
 
 
-def adam_kernel(early, tail, back, rest, head, *more):
+def adam_kernel(early, group, tail, back, rest, head, *more):
     far, (master, moment1, moment2) = more[: len(early)], more[len(early) : len(early) + 3]
     out_master, out_moment1, out_moment2, out_own, unit, total = more[-6:]
     step = pl.program_id(0)
-    slab_rows, lanes = out_own.shape
+    lanes = out_own.shape[1]
+    upper = lax.broadcasted_iota(jnp.int32, (8, 128), 0) < 4
+    lane = lax.broadcasted_iota(jnp.int32, (8, 128), 1)
 
     @pl.when(step == 0)
     def _():
@@ -245,11 +285,30 @@
             unit[...], part, (((1,), (1,)), ((), ())), preferred_element_type=jnp.float32
         )
 
+    def end(member):
+        ends = rest[member].astype(jnp.float32)
+        return jnp.where(upper, pltpu.roll(ends[:, :128], 4, 0), ends[:, 128:256])
+
+    def gather(members, width, start):
+        found = jnp.zeros((8, 128), jnp.float32)
+        for at, member in enumerate(members):
+            turned_end = pltpu.roll(end(member), (width * at - start) % 128, 1)
+            found = jnp.where(lane // width == at, turned_end, found)
+        return found
+
+    def whole_rows():
+        total[:MAIN] = upright(back[...].reshape(lanes, MAIN))
+        for at in range(lanes // 128):
+            first = step * (lanes // 16) + 8 * at
+            total[MAIN:, 128 * at : 128 * at + 128] = gather(
+                [first + j for j in range(8)], 16, 16 * group
+            )
+
     if tail:
 
         @pl.when(step < 4)
         def _():
-            total[...] = upright(back[...].reshape(lanes, slab_rows))
+            whole_rows()
 
         @pl.when(step == 4)
         def _():
@@ -259,12 +318,13 @@
             select = jnp.logical_and((line // 8) * 4 + line % 8 == feature, line % 8 < 4)
             part = jnp.dot(
                 select.astype(jnp.bfloat16),
-                rest[...].reshape(2 * lanes, slab_rows),
+                rest[...].reshape(2 * lanes, MAIN),
                 preferred_element_type=jnp.float32,
             )
-            total[...] = upright(part.astype(jnp.bfloat16))
+            total[:MAIN] = upright(part.astype(jnp.bfloat16))
+            total[MAIN:] = gather(range(32), 4, 32)
     else:
-        total[...] = upright(back[...].reshape(lanes, slab_rows))
+        whole_rows()
 
     from_far = far[0][...].astype(jnp.float32)
     if len(early) == 2:
@@ -282,8 +342,8 @@
 
 
 def adam(back, group, lanes, head, far, master, moment1, moment2, earlier=()):
-    members, rows, slab_rows = back.shape
-    quarter = master.shape[1]
+    members, rows, _ = back.shape
+    slab_rows, quarter = master.shape
     span = 512 if group == 0 else quarter - 512
     first = 512 * group // lanes
     tile = pl.BlockSpec((slab_rows, lanes), lambda i: (0, first + i))
@@ -295,13 +355,13 @@
     begins = [0, far[0].shape[1] // lanes][: len(far)]
     whole = jax.ShapeDtypeStruct(master.shape, jnp.float32)
     return pl.pallas_call(
-        functools.partial(adam_kernel, [begin - first for begin in begins], span > 512),
+        functools.partial(adam_kernel, [begin - first for begin in begins], group, span > 512),
         grid=(span // lanes,),
         in_specs=[
             pl.BlockSpec(
-                (lanes // 16, 16, slab_rows), lambda i: (jnp.minimum(i, 512 // lanes - 1), group, 0)
+                (lanes // 16, 16, MAIN), lambda i: (jnp.minimum(i, 512 // lanes - 1), group, 0)
             ),
-            pl.BlockSpec((members, 8, slab_rows), lambda i: (0, rows // 8 - 1, 0)),
+            pl.BlockSpec((members, 8, MAIN), lambda i: (0, rows // 8 - 1, 0)),
             tile,
             *[far_spec(*pair) for pair in zip(begins, far)],
             tile,
@@ -312,7 +372,7 @@
         out_specs=[tile, tile, tile, pl.BlockSpec((slab_rows, lanes), lambda i: (0, i))],
         out_shape=[whole, whole, whole, jax.ShapeDtypeStruct((slab_rows, span), jnp.bfloat16)],
         scratch_shapes=[
-            pltpu.VMEM((slab_rows, slab_rows), jnp.bfloat16),
+            pltpu.VMEM((MAIN, MAIN), jnp.bfloat16),
             pltpu.VMEM((slab_rows, lanes), jnp.float32),
         ],
         input_output_aliases={6 + len(far) + at: at for at in range(len(earlier))},
@@ -365,8 +425,6 @@
 
 def shards(token_grad, token_ids, block_counts, hidden, dlogits, master, moment1, moment2):
     section = lax.axis_index("section").astype(jnp.int32)
-    quarter = token_grad.shape[1]
-    slab_rows = master.shape[0]
     hidden_theirs = lax.ppermute(hidden, "section", CORE)
     dlogits_theirs = lax.ppermute(dlogits, "section", CORE)
     got = exchange(messages(block_counts, token_ids, token_grad))
@@ -375,7 +433,7 @@
     got, late = lax.optimization_barrier((got, late))
     early = lax.ppermute(early, "section", ACROSS)
     late = lax.ppermute(late, "section", ACROSS)
-    sums, early = lax.optimization_barrier((owner_sums(got, slab_rows), early))
+    sums, early = lax.optimization_barrier((owner_sums(got), early))
     back = exchange(sums)
 
     *states, own_a = adam(back, 0, 256, head, [early], master, moment1, moment2)

time: 138 us -> 134 us (0.971)
  starting transfers between devices: 32.6 us -> 30.5 us
    all_to_all x2, waiting for transfers between devices: 40.6 us -> 37.6 us  [exchange(): lax.all_to_all(rows, 'vocab', split_axis=0, concat_axis=0, tiled=True)]
    ppermute x1, starting transfers between devices: 4.49 us -> 2.42 us  [shards(): far_a = lax.ppermute(own_a, 'section', ACROSS)]
    ppermute x1, waiting for transfers between devices: 1.26 us -> 3.04 us  [shards(): late = lax.ppermute(late, 'section', ACROSS)]
where the time goes in v6:
time: 134 us; the launch traced here: 133 us
  waiting for transfers between devices  61.3 us (46%)
  Pallas kernels  38.8 us (29%)
  starting transfers between devices  30.5 us (23%)
  local copies, waits for them, and re-layouts  2.11 us (2%)
    all_to_all x2, waiting for transfers between devices, exchange(): lax.all_to_all(rows, 'vocab', split_axis=0, concat_axis=0, tiled=True)  37.6 us
    pallas_call x1, Pallas kernels, owner_sums(): pl.pallas_call(sum_kernel, grid=(members // SENDERS,), in_specs=[pl.Block...  13.9 us
    all_to_all x2, starting transfers between devices, exchange(): lax.all_to_all(rows, 'vocab', split_axis=0, concat_axis=0, tiled=True)  13.8 us
    ppermute x1, waiting for transfers between devices, shards(): far_b = lax.ppermute(turn_b, 'section', ACROSS)  11.5 us
    pallas_call x2, Pallas kernels, adam(): pl.pallas_call(functools.partial(adam_kernel, [begin - first for begin in...  11.1 us
    pallas_call x1, Pallas kernels, head_parts(): pl.pallas_call(head_kernel, grid_spec=pltpu.PrefetchScalarGridSpec(num_sc...  6.53 us
    pallas_call x1, Pallas kernels, messages(): pl.pallas_call(message_kernel, grid=(4,), in_specs=[pl.BlockSpec(block_co...  4.8 us
    ppermute x1, waiting for transfers between devices, shards(): far_a = lax.ppermute(own_a, 'section', ACROSS)  4.68 us
  transfers between devices with their start and end apart: 12, of which 8 were waited for; matrix products, arithmetic and copies ran while one was open for 0% of the time, Pallas kernels for 27%

profile of v6, /device:TPU:25, one launch (start us, length us, event | category | flops | bytes accessed | tf_op | source)
XLA Modules:
  0.0 133.4 jit_solution(2759380163702793154)
XLA Ops:
  0.6 0.8 collective-permute-start.1
  1.4 4.8 %shard_map.111 = bf16[32,40,1024]{2,1,0:T(8,128)(2,1)} custom-call(s32[1,32]{1,0:T(1,128)} %counts.1, s32[8,128]{1,0:T(8,128)} %bitcast.5, bf16[1024,1152]{1,0:T(8,128)(2,1)} %third.1, bf16[1024,1152]{1,0:T(8,128)(2,1)} %third.1, bf16[1024,1152]{1,0:T(8,128)(2,1)} %third.1), custom_call_target="tpu_custom_call" | custom-call | flops 301989888 | bytes 4980736 | tf_op jit(solution)/shard_map/pallas_call | solution.py:245
  6.2 8.9 %all-to-all-start = ((bf16[32,40,1024]{2,1,0:T(8,128)(2,1)}), bf16[32,40,1024]{2,1,0:T(8,128)(2,1)S(1)}, u32[]{:S(2)}, u32[]{:S(2)}) async-start(bf16[32,40,1024]{2,1,0:T(8,128)(2,1)} %shard_map.111), calls=%async_computation | async-start | bytes 5242880 | tf_op jit(solution)/shard_map/all_to_all | solution.py:423
  15.8 1.7 %collective-permute-done = bf16[512,520]{0,1:T(8,128)(2,1)} collective-permute-done((bf16[512,520]{0,1:T(8,128)(2,1)S(1)}, bf16[512,520]{0,1:T(8,128)(2,1)}, u32[]{:S(2)}, u32[]{:S(2)}) %collective-permute-start) | collective-permute-done | bytes 532512 | tf_op jit(solution)/shard_map/ppermute | solution.py:429
  17.4 6.5 %shard_map.112 = (bf16[520,1152]{1,0:T(8,128)(2,1)}, bf16[520,640]{1,0:T(8,128)(2,1)}, bf16[520,512]{1,0:T(8,128)(2,1)}) custom-call(s32[1]{0:T(128)} %bitcast.1.place, bf16[520,512]{1,0:T(8,128)(2,1)} %bitcast.4, bf16[520,512]{1,0:T(8,128)(2,1)} %bitcast.3.theirs, bf16[512,4608]{1,0:T(8,128)(2,1)} %hidden.1, ...), custom_call_target="tpu_custom_call" | custom-call | flops 2453667840 | bytes 10575872 | tf_op jit(solution)/shard_map/pallas_call | solution.py:54
  24.0 2.4 %collective-permute-start.2 = (bf16[520,640]{1,0:T(8,128)(2,1)}, bf16[520,640]{1,0:T(8,128)(2,1)S(1)}, u32[]{:S(2)}, u32[]{:S(2)}) collective-permute-start(bf16[520,640]{1,0:T(8,128)(2,1)} %get-tuple-element.23), channel_id=1, source_target_pairs={{0,64},{64,0},{32,96},{96,32},{1,65},{65,1},{33,97},{97,33},{2,66}... | collective-permute-start | bytes 1996808 | tf_op jit(solution)/shard_map/ppermute | solution.py:434
  26.4 24.2 %all-to-all-done.marks.got = bf16[32,40,1024]{2,1,0:T(8,128)(2,1)S(1)} async-done(((bf16[32,40,1024]{2,1,0:T(8,128)(2,1)}), bf16[32,40,1024]{2,1,0:T(8,128)(2,1)S(1)}, u32[]{:S(2)}, u32[]{:S(2)}) %all-to-all-start) | async-done | bytes 2621472 | tf_op jit(solution)/shard_map/all_to_all | solution.py:423
  50.6 13.9 %shard_map.113 = bf16[32,40,512]{2,1,0:T(8,128)(2,1)S(1)} custom-call(bf16[32,40,1024]{2,1,0:T(8,128)(2,1)S(1)} %all-to-all-done.marks.got, bf16[32,40,1024]{2,1,0:T(8,128)(2,1)S(1)} %all-to-all-done.marks.got), custom_call_target="tpu_custom_call" | custom-call | tf_op jit(solution)/shard_map/pallas_call | solution.py:166
  64.6 1.0 copy-done
  65.6 4.9 %all-to-all-start.1 = ((bf16[32,40,512]{2,1,0:T(8,128)(2,1)}), bf16[32,40,512]{2,1,0:T(8,128)(2,1)S(1)}, u32[]{:S(2)}, u32[]{:S(2)}) async-start(bf16[32,40,512]{2,1,0:T(8,128)(2,1)} %copy-done), calls=%async_computation.1 | async-start | bytes 2621440 | tf_op jit(solution)/shard_map/all_to_all | solution.py:423
  70.6 2.5 %collective-permute-start.3 = (bf16[520,512]{1,0:T(8,128)(2,1)S(1)}, bf16[520,512]{1,0:T(8,128)(2,1)S(1)}, u32[]{:S(2)}, u32[]{:S(2)}) collective-permute-start(bf16[520,512]{1,0:T(8,128)(2,1)S(1)} %copy-done.3), channel_id=1, source_target_pairs={{0,64},{64,0},{32,96},{96,32},{1,65},{65,1},{33,97},{97,33},{2,66}... | collective-permute-start | bytes 1597448 | tf_op jit(solution)/shard_map/ppermute | solution.py:435
  73.1 13.4 %all-to-all-done.1.back.rest = bf16[32,40,512]{2,1,0:T(8,128)(2,1)S(1)} async-done(((bf16[32,40,512]{2,1,0:T(8,128)(2,1)}), bf16[32,40,512]{2,1,0:T(8,128)(2,1)S(1)}, u32[]{:S(2)}, u32[]{:S(2)}) %all-to-all-start.1) | async-done | bytes 1310752 | tf_op jit(solution)/shard_map/all_to_all | solution.py:423
  86.5 1.1 copy-done.1
  87.6 4.3 %shard_map.114 = (f32[520,1152]{1,0:T(8,128)}, f32[520,1152]{1,0:T(8,128)}, f32[520,1152]{1,0:T(8,128)}, bf16[520,512]{1,0:T(8,128)(2,1)S(1)}) custom-call(bf16[32,40,512]{2,1,0:T(8,128)(2,1)} %copy-done.1, bf16[32,40,512]{2,1,0:T(8,128)(2,1)} %copy-done.1, bf16[520,1152]{1,0:T(8,128)(2,1)} %get-tuple-element.25.head, ...), custom_call_target="tpu_custom_call" | custom-call | flops 136314880 | bytes 9584640 | tf_op jit(solution)/shard_map/pallas_call | solution.py:357
  91.9 2.4 %collective-permute-start.6 = (bf16[520,512]{1,0:T(8,128)(2,1)S(1)}, bf16[520,512]{1,0:T(8,128)(2,1)S(1)}, u32[]{:S(2)}, u32[]{:S(2)}) collective-permute-start(bf16[520,512]{1,0:T(8,128)(2,1)S(1)} %get-tuple-element.34.refs_0_), channel_id=1, source_target_pairs={{0,64},{64,0},{32,96},{96,32},{1,65},{65,1},{33,97},{97,33},{2,66}... | collective-permute-start | bytes 1597448 | tf_op jit(solution)/shard_map/ppermute | solution.py:440
  94.3 3.0 %collective-permute-done.3.more_1_ = bf16[520,512]{1,0:T(8,128)(2,1)S(1)} collective-permute-done((bf16[520,512]{1,0:T(8,128)(2,1)S(1)}, bf16[520,512]{1,0:T(8,128)(2,1)S(1)}, u32[]{:S(2)}, u32[]{:S(2)}) %collective-permute-start.3) | collective-permute-done | bytes 532512 | tf_op jit(solution)/shard_map/ppermute | solution.py:435
  97.4 6.7 %shard_map.115 = (f32[520,1152]{1,0:T(8,128)}, f32[520,1152]{1,0:T(8,128)}, f32[520,1152]{1,0:T(8,128)}, bf16[520,640]{1,0:T(8,128)(2,1)S(1)}) custom-call(bf16[32,40,512]{2,1,0:T(8,128)(2,1)} %copy-done.1, bf16[32,40,512]{2,1,0:T(8,128)(2,1)} %copy-done.1, ...), custom_call_target="tpu_custom_call", output_to_operand_aliasing={{0}: (8, {}), {1}: (9, {}), {2}: (10, {})} | custom-call | flops 170393600 | bytes 11980800 | tf_op jit(solution)/shard_map/pallas_call | solution.py:357
  104.1 4.7 %collective-permute-done.6.refs_4_ = bf16[520,512]{1,0:T(8,128)(2,1)S(1)} collective-permute-done((bf16[520,512]{1,0:T(8,128)(2,1)S(1)}, bf16[520,512]{1,0:T(8,128)(2,1)S(1)}, u32[]{:S(2)}, u32[]{:S(2)}) %collective-permute-start.6) | collective-permute-done | bytes 532512 | tf_op jit(solution)/shard_map/ppermute | solution.py:440
  108.8 3.6 %collective-permute-start.5 = (bf16[520,640]{1,0:T(8,128)(2,1)S(1)}, bf16[520,640]{1,0:T(8,128)(2,1)S(1)}, u32[]{:S(2)}, u32[]{:S(2)}) collective-permute-start(bf16[520,640]{1,0:T(8,128)(2,1)S(1)} %get-tuple-element.37.refs_1_), channel_id=1, source_target_pairs={{0,32},{32,0},{64,96},{96,64},{1,33},{33,1},{65,97},{97,65},{2,34}... | collective-permute-start | bytes 1996808 | tf_op jit(solution)/shard_map/ppermute | solution.py:447
  112.4 11.5 %collective-permute-done.7.refs_5_ = bf16[520,640]{1,0:T(8,128)(2,1)S(1)} collective-permute-done((bf16[520,640]{1,0:T(8,128)(2,1)S(1)}, bf16[520,640]{1,0:T(8,128)(2,1)S(1)}, u32[]{:S(2)}, u32[]{:S(2)}) %collective-permute-start.7) | collective-permute-done | bytes 665632 | tf_op jit(solution)/shard_map/ppermute | solution.py:446
  123.9 3.7 %collective-permute-start.9 = (bf16[520,640]{1,0:T(8,128)(2,1)S(1)}, bf16[520,640]{1,0:T(8,128)(2,1)S(1)}, u32[]{:S(2)}, u32[]{:S(2)}) collective-permute-start(bf16[520,640]{1,0:T(8,128)(2,1)S(1)} %collective-permute-done.7.refs_5_), channel_id=1, source_target_pairs={{0,32},{32,0},{64,96},{96,64},{1,33},{33,1},{65,97},{97,65},{2,34}... | collective-permute-start | bytes 1996808 | tf_op jit(solution)/shard_map/ppermute | solution.py:449
  128.2 2.0 %collective-permute-done.4.refs_2_ = bf16[520,512]{1,0:T(8,128)(2,1)S(1)} collective-permute-done((bf16[520,512]{1,0:T(8,128)(2,1)S(1)}, bf16[520,512]{1,0:T(8,128)(2,1)S(1)}, u32[]{:S(2)}, u32[]{:S(2)}) %collective-permute-start.4) | collective-permute-done | bytes 532512 | tf_op jit(solution)/shard_map/ppermute | solution.py:441
  130.1 0.8 collective-permute-done.8.refs_6_
  130.9 2.5 %shard_map.116 = bf16[520,4608]{1,0:T(8,128)(2,1)} custom-call(s32[1]{0:T(128)} %bitcast.1.place, bf16[520,512]{1,0:T(8,128)(2,1)S(1)} %get-tuple-element.34.refs_0_, bf16[520,640]{1,0:T(8,128)(2,1)S(1)} %get-tuple-element.37.refs_1_, bf16[520,512]{1,0:T(8,128)(2,1)S(1)} %collective-permute-done.4.refs_2_, ...), custom_call_target="tpu_custom_call" | custom-call | bytes 9584640 | tf_op jit(solution)/shard_map/pallas_call | solution.py:406
  (14 shorter events, 1.2 us)
Async XLA Ops:
  0.6 16.8 %collective-permute-start.1 = (bf16[512,4608]{1,0:T(8,128)(2,1)}, bf16[512,4608]{1,0:T(8,128)(2,1)}, u32[]{:S(2)}, u32[]{:S(2)}) collective-permute-start(bf16[512,4608]{1,0:T(8,128)(2,1)} %hidden.1), channel_id=1, source_target_pairs={{0,32},{32,0},{64,96},{96,64},{1,33},{33,1},{65,97},{97,65},{2,34}... | collective-permute-start | bytes 14155784 | tf_op jit(solution)/shard_map/ppermute | solution.py:428
  6.2 8.9 %copy-start.2 = (bf16[512,520]{0,1:T(8,128)(2,1)S(1)}, bf16[512,520]{0,1:T(8,128)(2,1)}, u32[]{:S(2)}) copy-start(bf16[512,520]{0,1:T(8,128)(2,1)} %param.12) | copy-start | bytes 1597444
  6.2 44.4 %all-to-all-start = ((bf16[32,40,1024]{2,1,0:T(8,128)(2,1)}), bf16[32,40,1024]{2,1,0:T(8,128)(2,1)S(1)}, u32[]{:S(2)}, u32[]{:S(2)}) async-start(bf16[32,40,1024]{2,1,0:T(8,128)(2,1)} %shard_map.111), calls=%async_computation | async-start | bytes 5242880 | tf_op jit(solution)/shard_map/all_to_all | solution.py:423
  15.1 2.4 %collective-permute-start = (bf16[512,520]{0,1:T(8,128)(2,1)S(1)}, bf16[512,520]{0,1:T(8,128)(2,1)}, u32[]{:S(2)}, u32[]{:S(2)}) collective-permute-start(bf16[512,520]{0,1:T(8,128)(2,1)S(1)} %copy-done.2), channel_id=1, source_target_pairs={{0,32},{32,0},{64,96},{96,64},{1,33},{33,1},{65,97},{97,65},{2,34}... | collective-permute-start | bytes 1597448 | tf_op jit(solution)/shard_map/ppermute | solution.py:429
  24.0 41.6 %collective-permute-start.2 = (bf16[520,640]{1,0:T(8,128)(2,1)}, bf16[520,640]{1,0:T(8,128)(2,1)S(1)}, u32[]{:S(2)}, u32[]{:S(2)}) collective-permute-start(bf16[520,640]{1,0:T(8,128)(2,1)} %get-tuple-element.23), channel_id=1, source_target_pairs={{0,64},{64,0},{32,96},{96,32},{1,65},{65,1},{33,97},{97,33},{2,66}... | collective-permute-start | bytes 1996808 | tf_op jit(solution)/shard_map/ppermute | solution.py:434
  64.6 1.1 copy-start
  65.6 5.0 %copy-start.3 = (bf16[520,512]{1,0:T(8,128)(2,1)S(1)}, bf16[520,512]{1,0:T(8,128)(2,1)}, u32[]{:S(2)}) copy-start(bf16[520,512]{1,0:T(8,128)(2,1)} %get-tuple-element.27) | copy-start | bytes 1597444
  65.6 20.9 %all-to-all-start.1 = ((bf16[32,40,512]{2,1,0:T(8,128)(2,1)}), bf16[32,40,512]{2,1,0:T(8,128)(2,1)S(1)}, u32[]{:S(2)}, u32[]{:S(2)}) async-start(bf16[32,40,512]{2,1,0:T(8,128)(2,1)} %copy-done), calls=%async_computation.1 | async-start | bytes 2621440 | tf_op jit(solution)/shard_map/all_to_all | solution.py:423
  70.6 26.8 %collective-permute-start.3 = (bf16[520,512]{1,0:T(8,128)(2,1)S(1)}, bf16[520,512]{1,0:T(8,128)(2,1)S(1)}, u32[]{:S(2)}, u32[]{:S(2)}) collective-permute-start(bf16[520,512]{1,0:T(8,128)(2,1)S(1)} %copy-done.3), channel_id=1, source_target_pairs={{0,64},{64,0},{32,96},{96,32},{1,65},{65,1},{33,97},{97,33},{2,66}... | collective-permute-start | bytes 1597448 | tf_op jit(solution)/shard_map/ppermute | solution.py:435
  86.5 1.1 copy-start.1
  91.9 16.9 %collective-permute-start.6 = (bf16[520,512]{1,0:T(8,128)(2,1)S(1)}, bf16[520,512]{1,0:T(8,128)(2,1)S(1)}, u32[]{:S(2)}, u32[]{:S(2)}) collective-permute-start(bf16[520,512]{1,0:T(8,128)(2,1)S(1)} %get-tuple-element.34.refs_0_), channel_id=1, source_target_pairs={{0,64},{64,0},{32,96},{96,32},{1,65},{65,1},{33,97},{97,33},{2,66}... | collective-permute-start | bytes 1597448 | tf_op jit(solution)/shard_map/ppermute | solution.py:440
  108.8 15.1 %collective-permute-start.7 = (bf16[520,640]{1,0:T(8,128)(2,1)S(1)}, bf16[520,640]{1,0:T(8,128)(2,1)S(1)}, u32[]{:S(2)}, u32[]{:S(2)}) collective-permute-start(bf16[520,640]{1,0:T(8,128)(2,1)S(1)} %get-tuple-element.37.refs_1_), channel_id=1, source_target_pairs={{0,64},{64,0},{32,96},{96,32},{1,65},{65,1},{33,97},{97,33},{2,66}... | collective-permute-start | bytes 1996808 | tf_op jit(solution)/shard_map/ppermute | solution.py:446
  108.8 21.4 %collective-permute-start.5 = (bf16[520,640]{1,0:T(8,128)(2,1)S(1)}, bf16[520,640]{1,0:T(8,128)(2,1)S(1)}, u32[]{:S(2)}, u32[]{:S(2)}) collective-permute-start(bf16[520,640]{1,0:T(8,128)(2,1)S(1)} %get-tuple-element.37.refs_1_), channel_id=1, source_target_pairs={{0,32},{32,0},{64,96},{96,64},{1,33},{33,1},{65,97},{97,65},{2,34}... | collective-permute-start | bytes 1996808 | tf_op jit(solution)/shard_map/ppermute | solution.py:447
  123.9 7.0 %collective-permute-start.9 = (bf16[520,640]{1,0:T(8,128)(2,1)S(1)}, bf16[520,640]{1,0:T(8,128)(2,1)S(1)}, u32[]{:S(2)}, u32[]{:S(2)}) collective-permute-start(bf16[520,640]{1,0:T(8,128)(2,1)S(1)} %collective-permute-done.7.refs_5_), channel_id=1, source_target_pairs={{0,32},{32,0},{64,96},{96,64},{1,33},{33,1},{65,97},{97,65},{2,34}... | collective-permute-start | bytes 1996808 | tf_op jit(solution)/shard_map/ppermute | solution.py:449
  127.6 2.5 %collective-permute-start.4 = (bf16[520,512]{1,0:T(8,128)(2,1)S(1)}, bf16[520,512]{1,0:T(8,128)(2,1)S(1)}, u32[]{:S(2)}, u32[]{:S(2)}) collective-permute-start(bf16[520,512]{1,0:T(8,128)(2,1)S(1)} %get-tuple-element.34.refs_0_), channel_id=1, source_target_pairs={{0,32},{32,0},{64,96},{96,64},{1,33},{33,1},{65,97},{97,65},{2,34}... | collective-permute-start | bytes 1597448 | tf_op jit(solution)/shard_map/ppermute | solution.py:441
  127.6 3.3 %collective-permute-start.8 = (bf16[520,512]{1,0:T(8,128)(2,1)S(1)}, bf16[520,512]{1,0:T(8,128)(2,1)S(1)}, u32[]{:S(2)}, u32[]{:S(2)}) collective-permute-start(bf16[520,512]{1,0:T(8,128)(2,1)S(1)} %collective-permute-done.6.refs_4_), channel_id=1, source_target_pairs={{0,32},{32,0},{64,96},{96,64},{1,33},{33,1},{65,97},{97,65},{2,34}... | collective-permute-start | bytes 1597448 | tf_op jit(solution)/shard_map/ppermute | solution.py:448

commit v7 on v6

--- a/solution.py
+++ b/solution.py
@@ -69,42 +69,41 @@
     )(section.reshape(1), dlogits.T, dlogits_theirs.T, hidden, hidden_theirs)
 
 
-SENDERS = 4
+SENDERS = 8
 
 
 MAIN = 512
-
-
-def sum_kernel(
-    marks, got, out, acc, parts, tails, last, ids, keys, place, place_smem, sem
-):
+SLOTS, SHIFT = 256, 8
+
+
+def sum_kernel(marks, got, out, acc, parts, last, ids, highs, place, place_smem, sem):
     step = pl.program_id(0)
-    members, rows, _ = acc.shape
+    members, rows = acc.shape[0], got.shape[1]
     senders = got.shape[0]
     blocks = got.shape[2] // BLOCK
-    lane = lax.broadcasted_iota(jnp.int32, (1, BLOCK), 1)
+    groups = acc.shape[1] // rows
 
     @pl.when(step == 0)
     def _():
+        lane = lax.broadcasted_iota(jnp.int32, (1, BLOCK), 1)
         for member in range(members):
             mark = marks[member].astype(jnp.float32)
-            numbers = mark[4:5] * 32.0 + mark[5:6] - 1.0
+            numbers = (mark[4:5] * 32.0 + mark[5:6] - 1.0).astype(jnp.int32)
             owner = mark[6:7].astype(jnp.int32)
+            low = jnp.where(numbers < 0, -1, numbers & (SLOTS - 1)).astype(jnp.float32)
+            highs[member] = numbers >> SHIFT
             spots = jnp.zeros((1, BLOCK), jnp.int32)
-            key = jnp.full((1, BLOCK), -1, jnp.int32)
             for block in range(blocks):
                 lanes = slice(block * BLOCK, (block + 1) * BLOCK)
-                ids[member, block : block + 1] = numbers[:, lanes]
+                ids[member, block : block + 1] = low[:, lanes]
                 spots = jnp.where(lane == block, owner[:, lanes], spots)
-                key = jnp.where(lane // 8 == block, owner[:, lanes] * 8 + lane % 8, key)
             place[member : member + 1] = spots
-            keys[member : member + 1] = key
         copy = pltpu.make_async_copy(place, place_smem, sem)
         copy.start()
         acc[...] = jnp.zeros_like(acc)
         copy.wait()
 
-    slot = lax.broadcasted_iota(jnp.int32, (BLOCK, MAIN), 1).astype(jnp.float32)
+    slot = lax.broadcasted_iota(jnp.int32, (SLOTS, BLOCK), 0).astype(jnp.float32)
 
     def add(sender):
         for block in range(blocks):
@@ -112,48 +111,50 @@
             acc[spot] += parts[sender * blocks + block]
 
     for sender in range(senders):
-        columns = ids[step * senders + sender].T
-        ends = []
+        low = ids[step * senders + sender]
+        high = highs[step * senders + sender]
+        values = got[sender].astype(jnp.float32)
+        masked = jnp.concatenate(
+            [jnp.where(high == group, values, 0.0) for group in range(groups)], axis=0
+        ).astype(jnp.bfloat16)
         for block in range(blocks):
-            part = got[sender, :, block * BLOCK : (block + 1) * BLOCK]
-            column = columns[:, block : block + 1]
-            one_hot = (slot == column).astype(jnp.bfloat16)
-            parts[sender * blocks + block] = jnp.dot(
-                part, one_hot, preferred_element_type=jnp.float32
+            one_hot = (slot == low[block : block + 1]).astype(jnp.bfloat16)
+            parts[sender * blocks + block] = lax.dot_general(
+                masked[:, block * BLOCK : (block + 1) * BLOCK],
+                one_hot,
+                (((1,), (1,)), ((), ())),
+                preferred_element_type=jnp.float32,
             )
-            end = jnp.where(lane // 8 == block, MAIN + lane % 8, -7).astype(jnp.float32)
-            ends.append((end == column).astype(jnp.bfloat16))
-        tails[step * senders + sender] = jnp.dot(
-            got[sender], jnp.concatenate(ends, axis=0), preferred_element_type=jnp.float32
-        ).astype(jnp.bfloat16)
         if sender > 0:
             add(sender - 1)
     add(senders - 1)
 
     @pl.when(step == pl.num_programs(0) - 1)
     def _():
-        line = lax.broadcasted_iota(jnp.int32, (8 * members, BLOCK), 0)
-        total = jnp.zeros((8 * members, rows), jnp.float32)
+        shape = (8, BLOCK)
+        down = lax.broadcasted_iota(jnp.int32, shape, 0)
+        unit = (down == lax.broadcasted_iota(jnp.int32, shape, 1)).astype(jnp.bfloat16)
+        last[...] = jnp.zeros_like(last)
         for member in range(members):
-            total += lax.dot_general(
-                (line == keys[member : member + 1]).astype(jnp.bfloat16),
-                tails[member],
+            last[8 * member : 8 * member + 8, :rows] = lax.dot_general(
+                unit,
+                acc[member, (groups - 1) * rows :, :BLOCK].astype(jnp.bfloat16),
                 (((1,), (1,)), ((), ())),
                 preferred_element_type=jnp.float32,
             )
-        last[...] = jnp.zeros_like(last)
-        last[:, :rows] = total
-        upper = lax.broadcasted_iota(jnp.int32, (8, BLOCK), 0) < 4
+        upper = down < 4
 
         def leave(spot, carry):
-            out[spot, :32] = acc[spot, :32].astype(jnp.bfloat16)
             tail = last[pl.ds(pl.multiple_of(8 * spot, 8), 8)]
             under = [pltpu.roll(tail, 4, 0), tail, jnp.zeros_like(tail), jnp.zeros_like(tail)]
             for at in range(4):
                 lanes = slice(at * BLOCK, (at + 1) * BLOCK)
-                out[spot, 32:, lanes] = jnp.where(upper, acc[spot, 32:, lanes], under[at]).astype(
-                    jnp.bfloat16
-                )
+                first = at * BLOCK // SLOTS * rows
+                held = slice(at * BLOCK % SLOTS, at * BLOCK % SLOTS + BLOCK)
+                top = acc[spot, first : first + 32, held]
+                end = acc[spot, first + 32 : first + rows, held]
+                out[spot, :32, lanes] = top.astype(jnp.bfloat16)
+                out[spot, 32:, lanes] = jnp.where(upper, end, under[at]).astype(jnp.bfloat16)
             return carry
 
         lax.fori_loop(0, members, leave, 0)
@@ -163,6 +164,7 @@
     members, rows, row_total = got.shape
     blocks = row_total // BLOCK
     shape = (members, rows, MAIN)
+    groups = MAIN // SLOTS + 1
     return pl.pallas_call(
         sum_kernel,
         grid=(members // SENDERS,),
@@ -173,12 +175,11 @@
         out_specs=pl.BlockSpec(shape, lambda i: (0, 0, 0)),
         out_shape=jax.ShapeDtypeStruct(shape, jnp.bfloat16),
         scratch_shapes=[
-            pltpu.VMEM((members, rows, MAIN), jnp.float32),
-            pltpu.VMEM((SENDERS * blocks, rows, MAIN), jnp.float32),
-            pltpu.VMEM((members, rows, BLOCK), jnp.bfloat16),
+            pltpu.VMEM((members, groups * rows, SLOTS), jnp.float32),
+            pltpu.VMEM((SENDERS * blocks, groups * rows, SLOTS), jnp.float32),
             pltpu.VMEM((8 * members, BLOCK), jnp.float32),
             pltpu.VMEM((members, blocks, BLOCK), jnp.float32),
-            pltpu.VMEM((members, BLOCK), jnp.int32),
+            pltpu.VMEM((members, 1, row_total), jnp.int32),
             pltpu.VMEM((members, BLOCK), jnp.int32),
             pltpu.SMEM((members, BLOCK), jnp.int32),
             pltpu.SemaphoreType.DMA,
@@ -446,6 +447,7 @@
     far_b = lax.ppermute(turn_b, "section", ACROSS)
     core_b = lax.ppermute(own_b, "section", CORE)
     cross_a = lax.ppermute(far_a, "section", CORE)
+    far_b, core_a, core_b, cross_a = lax.optimization_barrier((far_b, core_a, core_b, cross_a))
     cross_b = lax.ppermute(far_b, "section", CORE)
     refreshed = assemble(
         section,

time: 134 us -> 132 us (0.985)
  starting transfers between devices: 30.5 us -> 37.5 us
  Pallas kernels: 38.8 us -> 32.1 us
  waiting for transfers between devices: 61.3 us -> 58.9 us
    pallas_call x1, Pallas kernels: 13.9 us -> 7.19 us  [owner_sums(): pl.pallas_call(sum_kernel, grid=(members // SENDERS,), in_specs=[pl.Block...]
    all_to_all x2, starting transfers between devices: 13.8 us -> 18.6 us  [exchange(): lax.all_to_all(rows, 'vocab', split_axis=0, concat_axis=0, tiled=True)]
    ppermute x1, waiting for transfers between devices: 4.68 us -> 0.38 us  [shards(): far_a = lax.ppermute(own_a, 'section', ACROSS)]
    ppermute x1, starting transfers between devices: 0.01 us -> 2.89 us  [shards(): core_a = lax.ppermute(own_a, 'section', CORE)]
    ppermute x1, waiting for transfers between devices: 11.5 us -> 9.47 us  [shards(): far_b = lax.ppermute(turn_b, 'section', ACROSS)]
    ppermute x1, waiting for transfers between devices: 0.01 us -> 1.74 us  [shards(): cross_b = lax.ppermute(far_b, 'section', CORE)]
    ppermute x1, waiting for transfers between devices: 0.01 us -> 1.55 us  [shards(): early = lax.ppermute(early, 'section', ACROSS)]
  transfers between devices with their start and end apart: 12 -> 12, of which waited for: 8 -> 10; matrix products, arithmetic and copies ran while one was open for 0% -> 0% of each run, Pallas kernels for 27% -> 23%
where the time goes in v7:
time: 132 us; the launch traced here: 131 us
  waiting for transfers between devices  58.9 us (45%)
  starting transfers between devices  37.5 us (28%)
  Pallas kernels  32.1 us (24%)
  local copies, waits for them, and re-layouts  2.11 us (2%)
    all_to_all x2, waiting for transfers between devices, exchange(): lax.all_to_all(rows, 'vocab', split_axis=0, concat_axis=0, tiled=True)  38.7 us
    all_to_all x2, starting transfers between devices, exchange(): lax.all_to_all(rows, 'vocab', split_axis=0, concat_axis=0, tiled=True)  18.6 us
    pallas_call x2, Pallas kernels, adam(): pl.pallas_call(functools.partial(adam_kernel, [begin - first for begin in...  11.1 us
    ppermute x1, waiting for transfers between devices, shards(): far_b = lax.ppermute(turn_b, 'section', ACROSS)  9.47 us
    pallas_call x1, Pallas kernels, owner_sums(): pl.pallas_call(sum_kernel, grid=(members // SENDERS,), in_specs=[pl.Block...  7.19 us
    pallas_call x1, Pallas kernels, head_parts(): pl.pallas_call(head_kernel, grid_spec=pltpu.PrefetchScalarGridSpec(num_sc...  6.53 us
    pallas_call x1, Pallas kernels, messages(): pl.pallas_call(message_kernel, grid=(4,), in_specs=[pl.BlockSpec(block_co...  4.8 us
    ppermute x1, starting transfers between devices, shards(): core_b = lax.ppermute(own_b, 'section', CORE)  4.29 us
  transfers between devices with their start and end apart: 12, of which 10 were waited for; matrix products, arithmetic and copies ran while one was open for 0% of the time, Pallas kernels for 23%

profile of v7, /device:TPU:25, one launch (start us, length us, event | category | flops | bytes accessed | tf_op | source)
XLA Modules:
  0.0 131.4 jit_solution(13724966007292007757)
XLA Ops:
  1.4 4.8 %shard_map.111 = bf16[32,40,1024]{2,1,0:T(8,128)(2,1)} custom-call(s32[1,32]{1,0:T(1,128)} %counts.1, s32[8,128]{1,0:T(8,128)} %bitcast.5, bf16[1024,1152]{1,0:T(8,128)(2,1)} %third.1, bf16[1024,1152]{1,0:T(8,128)(2,1)} %third.1, bf16[1024,1152]{1,0:T(8,128)(2,1)} %third.1), custom_call_target="tpu_custom_call" | custom-call | flops 301989888 | bytes 4980736 | tf_op jit(solution)/shard_map/pallas_call | solution.py:246
  6.2 8.9 %all-to-all-start = ((bf16[32,40,1024]{2,1,0:T(8,128)(2,1)}), bf16[32,40,1024]{2,1,0:T(8,128)(2,1)S(1)}, u32[]{:S(2)}, u32[]{:S(2)}) async-start(bf16[32,40,1024]{2,1,0:T(8,128)(2,1)} %shard_map.111), calls=%async_computation | async-start | bytes 5242880 | tf_op jit(solution)/shard_map/all_to_all | solution.py:424
  15.8 1.7 %collective-permute-done = bf16[512,520]{0,1:T(8,128)(2,1)} collective-permute-done((bf16[512,520]{0,1:T(8,128)(2,1)S(1)}, bf16[512,520]{0,1:T(8,128)(2,1)}, u32[]{:S(2)}, u32[]{:S(2)}) %collective-permute-start) | collective-permute-done | bytes 532512 | tf_op jit(solution)/shard_map/ppermute | solution.py:430
  17.4 6.5 %shard_map.112 = (bf16[520,1152]{1,0:T(8,128)(2,1)}, bf16[520,640]{1,0:T(8,128)(2,1)}, bf16[520,512]{1,0:T(8,128)(2,1)}) custom-call(s32[1]{0:T(128)} %bitcast.1.place, bf16[520,512]{1,0:T(8,128)(2,1)} %bitcast.4, bf16[520,512]{1,0:T(8,128)(2,1)} %bitcast.3.theirs, bf16[512,4608]{1,0:T(8,128)(2,1)} %hidden.1, ...), custom_call_target="tpu_custom_call" | custom-call | flops 2453667840 | bytes 10575872 | tf_op jit(solution)/shard_map/pallas_call | solution.py:54
  24.0 2.4 %collective-permute-start.2 = (bf16[520,640]{1,0:T(8,128)(2,1)}, bf16[520,640]{1,0:T(8,128)(2,1)S(1)}, u32[]{:S(2)}, u32[]{:S(2)}) collective-permute-start(bf16[520,640]{1,0:T(8,128)(2,1)} %get-tuple-element.27), channel_id=1, source_target_pairs={{0,64},{64,0},{32,96},{96,32},{1,65},{65,1},{33,97},{97,33},{2,66}... | collective-permute-start | bytes 1996808 | tf_op jit(solution)/shard_map/ppermute | solution.py:435
  26.4 24.2 %all-to-all-done.marks.got = bf16[32,40,1024]{2,1,0:T(8,128)(2,1)S(1)} async-done(((bf16[32,40,1024]{2,1,0:T(8,128)(2,1)}), bf16[32,40,1024]{2,1,0:T(8,128)(2,1)S(1)}, u32[]{:S(2)}, u32[]{:S(2)}) %all-to-all-start) | async-done | bytes 2621472 | tf_op jit(solution)/shard_map/all_to_all | solution.py:424
  50.6 7.2 %shard_map.113 = bf16[32,40,512]{2,1,0:T(8,128)(2,1)S(1)} custom-call(bf16[32,40,1024]{2,1,0:T(8,128)(2,1)S(1)} %all-to-all-done.marks.got, bf16[32,40,1024]{2,1,0:T(8,128)(2,1)S(1)} %all-to-all-done.marks.got), custom_call_target="tpu_custom_call" | custom-call | tf_op jit(solution)/shard_map/pallas_call | solution.py:168
  57.8 1.0 copy-done
  58.9 1.6 %collective-permute-done.2.more_0_ = bf16[520,640]{1,0:T(8,128)(2,1)S(1)} collective-permute-done((bf16[520,640]{1,0:T(8,128)(2,1)}, bf16[520,640]{1,0:T(8,128)(2,1)S(1)}, u32[]{:S(2)}, u32[]{:S(2)}) %collective-permute-start.2) | collective-permute-done | bytes 665632 | tf_op jit(solution)/shard_map/ppermute | solution.py:435
  60.4 9.7 %all-to-all-start.1 = ((bf16[32,40,512]{2,1,0:T(8,128)(2,1)}), bf16[32,40,512]{2,1,0:T(8,128)(2,1)S(1)}, u32[]{:S(2)}, u32[]{:S(2)}) async-start(bf16[32,40,512]{2,1,0:T(8,128)(2,1)} %copy-done), calls=%async_computation.1 | async-start | bytes 2621440 | tf_op jit(solution)/shard_map/all_to_all | solution.py:424
  70.2 1.9 %collective-permute-start.3 = (bf16[520,512]{1,0:T(8,128)(2,1)S(1)}, bf16[520,512]{1,0:T(8,128)(2,1)S(1)}, u32[]{:S(2)}, u32[]{:S(2)}) collective-permute-start(bf16[520,512]{1,0:T(8,128)(2,1)S(1)} %copy-done.3), channel_id=1, source_target_pairs={{0,64},{64,0},{32,96},{96,32},{1,65},{65,1},{33,97},{97,33},{2,66}... | collective-permute-start | bytes 1597448 | tf_op jit(solution)/shard_map/ppermute | solution.py:436
  72.1 14.5 %all-to-all-done.1.back.rest = bf16[32,40,512]{2,1,0:T(8,128)(2,1)S(1)} async-done(((bf16[32,40,512]{2,1,0:T(8,128)(2,1)}), bf16[32,40,512]{2,1,0:T(8,128)(2,1)S(1)}, u32[]{:S(2)}, u32[]{:S(2)}) %all-to-all-start.1) | async-done | bytes 1310752 | tf_op jit(solution)/shard_map/all_to_all | solution.py:424
  86.5 1.1 copy-done.1
  87.6 4.3 %shard_map.114 = (f32[520,1152]{1,0:T(8,128)}, f32[520,1152]{1,0:T(8,128)}, f32[520,1152]{1,0:T(8,128)}, bf16[520,512]{1,0:T(8,128)(2,1)S(1)}) custom-call(bf16[32,40,512]{2,1,0:T(8,128)(2,1)} %copy-done.1, bf16[32,40,512]{2,1,0:T(8,128)(2,1)} %copy-done.1, bf16[520,1152]{1,0:T(8,128)(2,1)} %get-tuple-element.29.head, ...), custom_call_target="tpu_custom_call" | custom-call | flops 136314880 | bytes 9584640 | tf_op jit(solution)/shard_map/pallas_call | solution.py:358
  91.9 1.8 %collective-permute-start.4 = (bf16[520,512]{1,0:T(8,128)(2,1)S(1)}, bf16[520,512]{1,0:T(8,128)(2,1)S(1)}, u32[]{:S(2)}, u32[]{:S(2)}) collective-permute-start(bf16[520,512]{1,0:T(8,128)(2,1)S(1)} %get-tuple-element.38.refs_0_), channel_id=1, source_target_pairs={{0,64},{64,0},{32,96},{96,32},{1,65},{65,1},{33,97},{97,33},{2,66}... | collective-permute-start | bytes 1597448 | tf_op jit(solution)/shard_map/ppermute | solution.py:441
  93.7 3.1 %collective-permute-done.3.more_1_ = bf16[520,512]{1,0:T(8,128)(2,1)S(1)} collective-permute-done((bf16[520,512]{1,0:T(8,128)(2,1)S(1)}, bf16[520,512]{1,0:T(8,128)(2,1)S(1)}, u32[]{:S(2)}, u32[]{:S(2)}) %collective-permute-start.3) | collective-permute-done | bytes 532512 | tf_op jit(solution)/shard_map/ppermute | solution.py:436
  96.8 6.7 %shard_map.115 = (f32[520,1152]{1,0:T(8,128)}, f32[520,1152]{1,0:T(8,128)}, f32[520,1152]{1,0:T(8,128)}, bf16[520,640]{1,0:T(8,128)(2,1)S(1)}) custom-call(bf16[32,40,512]{2,1,0:T(8,128)(2,1)} %copy-done.1, bf16[32,40,512]{2,1,0:T(8,128)(2,1)} %copy-done.1, ...), custom_call_target="tpu_custom_call", output_to_operand_aliasing={{0}: (8, {}), {1}: (9, {}), {2}: (10, {})} | custom-call | flops 170393600 | bytes 11980800 | tf_op jit(solution)/shard_map/pallas_call | solution.py:358
  103.6 4.3 %collective-permute-start.7 = (bf16[520,640]{1,0:T(8,128)(2,1)S(1)}, bf16[520,640]{1,0:T(8,128)(2,1)S(1)}, u32[]{:S(2)}, u32[]{:S(2)}) collective-permute-start(bf16[520,640]{1,0:T(8,128)(2,1)S(1)} %get-tuple-element.40.refs_1_), channel_id=1, source_target_pairs={{0,32},{32,0},{64,96},{96,64},{1,33},{33,1},{65,97},{97,65},{2,34}... | collective-permute-start | bytes 1996808 | tf_op jit(solution)/shard_map/ppermute | solution.py:448
  109.2 2.9 %collective-permute-start.6 = (bf16[520,512]{1,0:T(8,128)(2,1)S(1)}, bf16[520,512]{1,0:T(8,128)(2,1)S(1)}, u32[]{:S(2)}, u32[]{:S(2)}) collective-permute-start(bf16[520,512]{1,0:T(8,128)(2,1)S(1)} %get-tuple-element.38.refs_0_), channel_id=1, source_target_pairs={{0,32},{32,0},{64,96},{96,64},{1,33},{33,1},{65,97},{97,65},{2,34}... | collective-permute-start | bytes 1597448 | tf_op jit(solution)/shard_map/ppermute | solution.py:442
  112.0 1.5 %collective-permute-done.6.refs_2_ = bf16[520,512]{1,0:T(8,128)(2,1)S(1)} collective-permute-done((bf16[520,512]{1,0:T(8,128)(2,1)S(1)}, bf16[520,512]{1,0:T(8,128)(2,1)S(1)}, u32[]{:S(2)}, u32[]{:S(2)}) %collective-permute-start.6) | collective-permute-done | bytes 532512 | tf_op jit(solution)/shard_map/ppermute | solution.py:442
  114.4 9.5 %collective-permute-done.5.refs_5_ = bf16[520,640]{1,0:T(8,128)(2,1)S(1)} collective-permute-done((bf16[520,640]{1,0:T(8,128)(2,1)S(1)}, bf16[520,640]{1,0:T(8,128)(2,1)S(1)}, u32[]{:S(2)}, u32[]{:S(2)}) %collective-permute-start.5) | collective-permute-done | bytes 665632 | tf_op jit(solution)/shard_map/ppermute | solution.py:447
  123.8 3.3 %collective-permute-start.9 = (bf16[520,640]{1,0:T(8,128)(2,1)S(1)}, bf16[520,640]{1,0:T(8,128)(2,1)S(1)}, u32[]{:S(2)}, u32[]{:S(2)}) collective-permute-start(bf16[520,640]{1,0:T(8,128)(2,1)S(1)} %collective-permute-done.5.refs_5_), channel_id=1, source_target_pairs={{0,32},{32,0},{64,96},{96,64},{1,33},{33,1},{65,97},{97,65},{2,34}... | collective-permute-start | bytes 1996808 | tf_op jit(solution)/shard_map/ppermute | solution.py:451
  127.1 1.7 %collective-permute-done.9.refs_7_ = bf16[520,640]{1,0:T(8,128)(2,1)S(1)} collective-permute-done((bf16[520,640]{1,0:T(8,128)(2,1)S(1)}, bf16[520,640]{1,0:T(8,128)(2,1)S(1)}, u32[]{:S(2)}, u32[]{:S(2)}) %collective-permute-start.9) | collective-permute-done | bytes 665632 | tf_op jit(solution)/shard_map/ppermute | solution.py:451
  128.8 2.5 %shard_map.116 = bf16[520,4608]{1,0:T(8,128)(2,1)} custom-call(s32[1]{0:T(128)} %bitcast.1.place, bf16[520,512]{1,0:T(8,128)(2,1)S(1)} %get-tuple-element.38.refs_0_, bf16[520,640]{1,0:T(8,128)(2,1)S(1)} %get-tuple-element.40.refs_1_, bf16[520,512]{1,0:T(8,128)(2,1)S(1)} %collective-permute-done.6.refs_2_, ...), custom_call_target="tpu_custom_call" | custom-call | bytes 9584640 | tf_op jit(solution)/shard_map/pallas_call | solution.py:407
  (14 shorter events, 3.5 us)
Async XLA Ops:
  0.6 16.8 %collective-permute-start.1 = (bf16[512,4608]{1,0:T(8,128)(2,1)}, bf16[512,4608]{1,0:T(8,128)(2,1)}, u32[]{:S(2)}, u32[]{:S(2)}) collective-permute-start(bf16[512,4608]{1,0:T(8,128)(2,1)} %hidden.1), channel_id=1, source_target_pairs={{0,32},{32,0},{64,96},{96,64},{1,33},{33,1},{65,97},{97,65},{2,34}... | collective-permute-start | bytes 14155784 | tf_op jit(solution)/shard_map/ppermute | solution.py:429
  6.2 8.9 %copy-start.2 = (bf16[512,520]{0,1:T(8,128)(2,1)S(1)}, bf16[512,520]{0,1:T(8,128)(2,1)}, u32[]{:S(2)}) copy-start(bf16[512,520]{0,1:T(8,128)(2,1)} %param.12) | copy-start | bytes 1597444
  6.2 44.4 %all-to-all-start = ((bf16[32,40,1024]{2,1,0:T(8,128)(2,1)}), bf16[32,40,1024]{2,1,0:T(8,128)(2,1)S(1)}, u32[]{:S(2)}, u32[]{:S(2)}) async-start(bf16[32,40,1024]{2,1,0:T(8,128)(2,1)} %shard_map.111), calls=%async_computation | async-start | bytes 5242880 | tf_op jit(solution)/shard_map/all_to_all | solution.py:424
  15.1 2.4 %collective-permute-start = (bf16[512,520]{0,1:T(8,128)(2,1)S(1)}, bf16[512,520]{0,1:T(8,128)(2,1)}, u32[]{:S(2)}, u32[]{:S(2)}) collective-permute-start(bf16[512,520]{0,1:T(8,128)(2,1)S(1)} %copy-done.2), channel_id=1, source_target_pairs={{0,32},{32,0},{64,96},{96,64},{1,33},{33,1},{65,97},{97,65},{2,34}... | collective-permute-start | bytes 1597448 | tf_op jit(solution)/shard_map/ppermute | solution.py:430
  24.0 36.5 %collective-permute-start.2 = (bf16[520,640]{1,0:T(8,128)(2,1)}, bf16[520,640]{1,0:T(8,128)(2,1)S(1)}, u32[]{:S(2)}, u32[]{:S(2)}) collective-permute-start(bf16[520,640]{1,0:T(8,128)(2,1)} %get-tuple-element.27), channel_id=1, source_target_pairs={{0,64},{64,0},{32,96},{96,32},{1,65},{65,1},{33,97},{97,33},{2,66}... | collective-permute-start | bytes 1996808 | tf_op jit(solution)/shard_map/ppermute | solution.py:435
  57.8 1.1 copy-start
  58.9 11.3 %copy-start.3 = (bf16[520,512]{1,0:T(8,128)(2,1)S(1)}, bf16[520,512]{1,0:T(8,128)(2,1)}, u32[]{:S(2)}) copy-start(bf16[520,512]{1,0:T(8,128)(2,1)} %get-tuple-element.31) | copy-start | bytes 1597444
  60.4 26.1 %all-to-all-start.1 = ((bf16[32,40,512]{2,1,0:T(8,128)(2,1)}), bf16[32,40,512]{2,1,0:T(8,128)(2,1)S(1)}, u32[]{:S(2)}, u32[]{:S(2)}) async-start(bf16[32,40,512]{2,1,0:T(8,128)(2,1)} %copy-done), calls=%async_computation.1 | async-start | bytes 2621440 | tf_op jit(solution)/shard_map/all_to_all | solution.py:424
  70.2 26.6 %collective-permute-start.3 = (bf16[520,512]{1,0:T(8,128)(2,1)S(1)}, bf16[520,512]{1,0:T(8,128)(2,1)S(1)}, u32[]{:S(2)}, u32[]{:S(2)}) collective-permute-start(bf16[520,512]{1,0:T(8,128)(2,1)S(1)} %copy-done.3), channel_id=1, source_target_pairs={{0,64},{64,0},{32,96},{96,32},{1,65},{65,1},{33,97},{97,33},{2,66}... | collective-permute-start | bytes 1597448 | tf_op jit(solution)/shard_map/ppermute | solution.py:436
  86.5 1.1 copy-start.1
  91.9 16.3 %collective-permute-start.4 = (bf16[520,512]{1,0:T(8,128)(2,1)S(1)}, bf16[520,512]{1,0:T(8,128)(2,1)S(1)}, u32[]{:S(2)}, u32[]{:S(2)}) collective-permute-start(bf16[520,512]{1,0:T(8,128)(2,1)S(1)} %get-tuple-element.38.refs_0_), channel_id=1, source_target_pairs={{0,64},{64,0},{32,96},{96,32},{1,65},{65,1},{33,97},{97,33},{2,66}... | collective-permute-start | bytes 1597448 | tf_op jit(solution)/shard_map/ppermute | solution.py:441
  103.6 10.0 %collective-permute-start.7 = (bf16[520,640]{1,0:T(8,128)(2,1)S(1)}, bf16[520,640]{1,0:T(8,128)(2,1)S(1)}, u32[]{:S(2)}, u32[]{:S(2)}) collective-permute-start(bf16[520,640]{1,0:T(8,128)(2,1)S(1)} %get-tuple-element.40.refs_1_), channel_id=1, source_target_pairs={{0,32},{32,0},{64,96},{96,64},{1,33},{33,1},{65,97},{97,65},{2,34}... | collective-permute-start | bytes 1996808 | tf_op jit(solution)/shard_map/ppermute | solution.py:448
  108.2 15.6 %collective-permute-start.5 = (bf16[520,640]{1,0:T(8,128)(2,1)S(1)}, bf16[520,640]{1,0:T(8,128)(2,1)S(1)}, u32[]{:S(2)}, u32[]{:S(2)}) collective-permute-start(bf16[520,640]{1,0:T(8,128)(2,1)S(1)} %get-tuple-element.40.refs_1_), channel_id=1, source_target_pairs={{0,64},{64,0},{32,96},{96,32},{1,65},{65,1},{33,97},{97,33},{2,66}... | collective-permute-start | bytes 1996808 | tf_op jit(solution)/shard_map/ppermute | solution.py:447
  109.2 4.4 %collective-permute-start.6 = (bf16[520,512]{1,0:T(8,128)(2,1)S(1)}, bf16[520,512]{1,0:T(8,128)(2,1)S(1)}, u32[]{:S(2)}, u32[]{:S(2)}) collective-permute-start(bf16[520,512]{1,0:T(8,128)(2,1)S(1)} %get-tuple-element.38.refs_0_), channel_id=1, source_target_pairs={{0,32},{32,0},{64,96},{96,64},{1,33},{33,1},{65,97},{97,65},{2,34}... | collective-permute-start | bytes 1597448 | tf_op jit(solution)/shard_map/ppermute | solution.py:442
  112.0 2.3 %collective-permute-start.8 = (bf16[520,512]{1,0:T(8,128)(2,1)S(1)}, bf16[520,512]{1,0:T(8,128)(2,1)S(1)}, u32[]{:S(2)}, u32[]{:S(2)}) collective-permute-start(bf16[520,512]{1,0:T(8,128)(2,1)S(1)} %collective-permute-done.4.refs_4_), channel_id=1, source_target_pairs={{0,32},{32,0},{64,96},{96,64},{1,33},{33,1},{65,97},{97,65},{2,34}... | collective-permute-start | bytes 1597448 | tf_op jit(solution)/shard_map/ppermute | solution.py:449
  123.8 5.0 %collective-permute-start.9 = (bf16[520,640]{1,0:T(8,128)(2,1)S(1)}, bf16[520,640]{1,0:T(8,128)(2,1)S(1)}, u32[]{:S(2)}, u32[]{:S(2)}) collective-permute-start(bf16[520,640]{1,0:T(8,128)(2,1)S(1)} %collective-permute-done.5.refs_5_), channel_id=1, source_target_pairs={{0,32},{32,0},{64,96},{96,64},{1,33},{33,1},{65,97},{97,65},{2,34}... | collective-permute-start | bytes 1996808 | tf_op jit(solution)/shard_map/ppermute | solution.py:451

commit v8 on v7

--- a/solution.py
+++ b/solution.py
@@ -377,7 +377,7 @@
             pltpu.VMEM((slab_rows, lanes), jnp.float32),
         ],
         input_output_aliases={6 + len(far) + at: at for at in range(len(earlier))},
-        compiler_params=pltpu.CompilerParams(vmem_limit_bytes=52 * MIB),
+        compiler_params=pltpu.CompilerParams(vmem_limit_bytes=49 * MIB),
         cost_estimate=pl.CostEstimate(
             flops=4 * 128 * span * slab_rows,
             bytes_accessed=slab_rows * span * 36,

time: 132 us -> 132 us (level)
  waiting for transfers between devices: 58.9 us -> 60.3 us
  transfers between devices with their start and end apart: 12 -> 12, of which waited for: 10 -> 10; matrix products, arithmetic and copies ran while one was open for 0% -> 0% of each run, Pallas kernels for 23% -> 22%
where the time goes in v8:
time: 132 us; the launch traced here: 131 us
  waiting for transfers between devices  60.3 us (46%)
  starting transfers between devices  37.5 us (28%)
  Pallas kernels  31.8 us (24%)
    all_to_all x2, waiting for transfers between devices, exchange(): lax.all_to_all(rows, 'vocab', split_axis=0, concat_axis=0, tiled=True)  38.7 us
    all_to_all x2, starting transfers between devices, exchange(): lax.all_to_all(rows, 'vocab', split_axis=0, concat_axis=0, tiled=True)  18.6 us
    pallas_call x2, Pallas kernels, adam(): pl.pallas_call(functools.partial(adam_kernel, [begin - first for begin in...  10.7 us
    ppermute x1, waiting for transfers between devices, shards(): far_b = lax.ppermute(turn_b, 'section', ACROSS)  9.47 us
    pallas_call x1, Pallas kernels, owner_sums(): pl.pallas_call(sum_kernel, grid=(members // SENDERS,), in_specs=[pl.Block...  7.19 us
    pallas_call x1, Pallas kernels, head_parts(): pl.pallas_call(head_kernel, grid_spec=pltpu.PrefetchScalarGridSpec(num_sc...  6.55 us
    pallas_call x1, Pallas kernels, messages(): pl.pallas_call(message_kernel, grid=(4,), in_specs=[pl.BlockSpec(block_co...  4.8 us
    ppermute x1, waiting for transfers between devices, shards(): late = lax.ppermute(late, 'section', ACROSS)  4.44 us
  transfers between devices with their start and end apart: 12, of which 10 were waited for; matrix products, arithmetic and copies ran while one was open for 0% of the time, Pallas kernels for 22%

profile of v8, /device:TPU:25, one launch (start us, length us, event | category | flops | bytes accessed | tf_op | source)
XLA Modules:
  0.0 131.4 jit_solution(17568360209568649109)
XLA Ops:
  1.4 4.8 %shard_map.111 = bf16[32,40,1024]{2,1,0:T(8,128)(2,1)} custom-call(s32[1,32]{1,0:T(1,128)} %counts.1, s32[8,128]{1,0:T(8,128)} %bitcast.5, bf16[1024,1152]{1,0:T(8,128)(2,1)} %third.1, bf16[1024,1152]{1,0:T(8,128)(2,1)} %third.1, bf16[1024,1152]{1,0:T(8,128)(2,1)} %third.1), custom_call_target="tpu_custom_call" | custom-call | flops 301989888 | bytes 4980736 | tf_op jit(solution)/shard_map/pallas_call | solution.py:246
  6.2 8.9 %all-to-all-start = ((bf16[32,40,1024]{2,1,0:T(8,128)(2,1)}), bf16[32,40,1024]{2,1,0:T(8,128)(2,1)S(1)}, u32[]{:S(2)}, u32[]{:S(2)}) async-start(bf16[32,40,1024]{2,1,0:T(8,128)(2,1)} %shard_map.111), calls=%async_computation | async-start | bytes 5242880 | tf_op jit(solution)/shard_map/all_to_all | solution.py:424
  15.8 1.7 %collective-permute-done = bf16[512,520]{0,1:T(8,128)(2,1)} collective-permute-done((bf16[512,520]{0,1:T(8,128)(2,1)S(1)}, bf16[512,520]{0,1:T(8,128)(2,1)}, u32[]{:S(2)}, u32[]{:S(2)}) %collective-permute-start) | collective-permute-done | bytes 532512 | tf_op jit(solution)/shard_map/ppermute | solution.py:430
  17.4 6.5 %shard_map.112 = (bf16[520,1152]{1,0:T(8,128)(2,1)}, bf16[520,640]{1,0:T(8,128)(2,1)}, bf16[520,512]{1,0:T(8,128)(2,1)}) custom-call(s32[1]{0:T(128)} %bitcast.1.place, bf16[520,512]{1,0:T(8,128)(2,1)} %bitcast.4, bf16[520,512]{1,0:T(8,128)(2,1)} %bitcast.3.theirs, bf16[512,4608]{1,0:T(8,128)(2,1)} %hidden.1, ...), custom_call_target="tpu_custom_call" | custom-call | flops 2453667840 | bytes 10575872 | tf_op jit(solution)/shard_map/pallas_call | solution.py:54
  24.0 2.4 %collective-permute-start.2 = (bf16[520,640]{1,0:T(8,128)(2,1)}, bf16[520,640]{1,0:T(8,128)(2,1)S(1)}, u32[]{:S(2)}, u32[]{:S(2)}) collective-permute-start(bf16[520,640]{1,0:T(8,128)(2,1)} %get-tuple-element.27), channel_id=1, source_target_pairs={{0,64},{64,0},{32,96},{96,32},{1,65},{65,1},{33,97},{97,33},{2,66}... | collective-permute-start | bytes 1996808 | tf_op jit(solution)/shard_map/ppermute | solution.py:435
  26.4 24.2 %all-to-all-done.marks.got = bf16[32,40,1024]{2,1,0:T(8,128)(2,1)S(1)} async-done(((bf16[32,40,1024]{2,1,0:T(8,128)(2,1)}), bf16[32,40,1024]{2,1,0:T(8,128)(2,1)S(1)}, u32[]{:S(2)}, u32[]{:S(2)}) %all-to-all-start) | async-done | bytes 2621472 | tf_op jit(solution)/shard_map/all_to_all | solution.py:424
  50.6 7.2 %shard_map.113 = bf16[32,40,512]{2,1,0:T(8,128)(2,1)S(1)} custom-call(bf16[32,40,1024]{2,1,0:T(8,128)(2,1)S(1)} %all-to-all-done.marks.got, bf16[32,40,1024]{2,1,0:T(8,128)(2,1)S(1)} %all-to-all-done.marks.got), custom_call_target="tpu_custom_call" | custom-call | tf_op jit(solution)/shard_map/pallas_call | solution.py:168
  57.8 1.0 copy-done
  58.9 1.6 %collective-permute-done.2.more_0_ = bf16[520,640]{1,0:T(8,128)(2,1)S(1)} collective-permute-done((bf16[520,640]{1,0:T(8,128)(2,1)}, bf16[520,640]{1,0:T(8,128)(2,1)S(1)}, u32[]{:S(2)}, u32[]{:S(2)}) %collective-permute-start.2) | collective-permute-done | bytes 665632 | tf_op jit(solution)/shard_map/ppermute | solution.py:435
  60.4 9.7 %all-to-all-start.1 = ((bf16[32,40,512]{2,1,0:T(8,128)(2,1)}), bf16[32,40,512]{2,1,0:T(8,128)(2,1)S(1)}, u32[]{:S(2)}, u32[]{:S(2)}) async-start(bf16[32,40,512]{2,1,0:T(8,128)(2,1)} %copy-done), calls=%async_computation.1 | async-start | bytes 2621440 | tf_op jit(solution)/shard_map/all_to_all | solution.py:424
  70.2 1.9 %collective-permute-start.3 = (bf16[520,512]{1,0:T(8,128)(2,1)}, bf16[520,512]{1,0:T(8,128)(2,1)}, u32[]{:S(2)}, u32[]{:S(2)}) collective-permute-start(bf16[520,512]{1,0:T(8,128)(2,1)} %get-tuple-element.31), channel_id=1, source_target_pairs={{0,64},{64,0},{32,96},{96,32},{1,65},{65,1},{33,97},{97,33},{2,66}... | collective-permute-start | bytes 1597448 | tf_op jit(solution)/shard_map/ppermute | solution.py:436
  72.0 14.5 %all-to-all-done.1.back.rest = bf16[32,40,512]{2,1,0:T(8,128)(2,1)S(1)} async-done(((bf16[32,40,512]{2,1,0:T(8,128)(2,1)}), bf16[32,40,512]{2,1,0:T(8,128)(2,1)S(1)}, u32[]{:S(2)}, u32[]{:S(2)}) %all-to-all-start.1) | async-done | bytes 1310752 | tf_op jit(solution)/shard_map/all_to_all | solution.py:424
  86.5 4.2 %shard_map.114 = (f32[520,1152]{1,0:T(8,128)}, f32[520,1152]{1,0:T(8,128)}, f32[520,1152]{1,0:T(8,128)}, bf16[520,512]{1,0:T(8,128)(2,1)S(1)}) custom-call(bf16[32,40,512]{2,1,0:T(8,128)(2,1)S(1)} %all-to-all-done.1.back.rest, bf16[32,40,512]{2,1,0:T(8,128)(2,1)S(1)} %all-to-all-done.1.back.rest, bf16[520,1152]{1,0:T(8,128)(2,1)S(1)} %copy-done.1, ...), custom_call_target="tpu_custom_call" | custom-call | flops 136314880 | bytes 9584640 | tf_op jit(solution)/shard_map/pallas_call | solution.py:358
  90.7 1.8 %collective-permute-start.4 = (bf16[520,512]{1,0:T(8,128)(2,1)S(1)}, bf16[520,512]{1,0:T(8,128)(2,1)S(1)}, u32[]{:S(2)}, u32[]{:S(2)}) collective-permute-start(bf16[520,512]{1,0:T(8,128)(2,1)S(1)} %get-tuple-element.38.refs_0_), channel_id=1, source_target_pairs={{0,64},{64,0},{32,96},{96,32},{1,65},{65,1},{33,97},{97,33},{2,66}... | collective-permute-start | bytes 1597448 | tf_op jit(solution)/shard_map/ppermute | solution.py:441
  92.5 4.4 %collective-permute-done.3.more_1_ = bf16[520,512]{1,0:T(8,128)(2,1)} collective-permute-done((bf16[520,512]{1,0:T(8,128)(2,1)}, bf16[520,512]{1,0:T(8,128)(2,1)}, u32[]{:S(2)}, u32[]{:S(2)}) %collective-permute-start.3) | collective-permute-done | bytes 532512 | tf_op jit(solution)/shard_map/ppermute | solution.py:436
  96.9 6.6 %shard_map.115 = (f32[520,1152]{1,0:T(8,128)}, f32[520,1152]{1,0:T(8,128)}, f32[520,1152]{1,0:T(8,128)}, bf16[520,640]{1,0:T(8,128)(2,1)S(1)}) custom-call(bf16[32,40,512]{2,1,0:T(8,128)(2,1)S(1)} %all-to-all-done.1.back.rest, bf16[32,40,512]{2,1,0:T(8,128)(2,1)S(1)} %all-to-all-done.1.back.rest, ...), custom_call_target="tpu_custom_call", output_to_operand_aliasing={{0}: (8, {}), {1}: (9, {}), {2}: (10, {})} | custom-call | flops 170393600 | bytes 11980800 | tf_op jit(solution)/shard_map/pallas_call | solution.py:358
  103.5 4.3 %collective-permute-start.7 = (bf16[520,640]{1,0:T(8,128)(2,1)S(1)}, bf16[520,640]{1,0:T(8,128)(2,1)S(1)}, u32[]{:S(2)}, u32[]{:S(2)}) collective-permute-start(bf16[520,640]{1,0:T(8,128)(2,1)S(1)} %get-tuple-element.40.refs_1_), channel_id=1, source_target_pairs={{0,32},{32,0},{64,96},{96,64},{1,33},{33,1},{65,97},{97,65},{2,34}... | collective-permute-start | bytes 1996808 | tf_op jit(solution)/shard_map/ppermute | solution.py:448
  108.2 1.2 collective-permute-start.5
  109.4 2.6 %collective-permute-start.6 = (bf16[520,512]{1,0:T(8,128)(2,1)S(1)}, bf16[520,512]{1,0:T(8,128)(2,1)S(1)}, u32[]{:S(2)}, u32[]{:S(2)}) collective-permute-start(bf16[520,512]{1,0:T(8,128)(2,1)S(1)} %get-tuple-element.38.refs_0_), channel_id=1, source_target_pairs={{0,32},{32,0},{64,96},{96,64},{1,33},{33,1},{65,97},{97,65},{2,34}... | collective-permute-start | bytes 1597448 | tf_op jit(solution)/shard_map/ppermute | solution.py:442
  112.0 1.5 %collective-permute-done.6.refs_2_ = bf16[520,512]{1,0:T(8,128)(2,1)S(1)} collective-permute-done((bf16[520,512]{1,0:T(8,128)(2,1)S(1)}, bf16[520,512]{1,0:T(8,128)(2,1)S(1)}, u32[]{:S(2)}, u32[]{:S(2)}) %collective-permute-start.6) | collective-permute-done | bytes 532512 | tf_op jit(solution)/shard_map/ppermute | solution.py:442
  114.4 9.5 %collective-permute-done.5.refs_5_ = bf16[520,640]{1,0:T(8,128)(2,1)S(1)} collective-permute-done((bf16[520,640]{1,0:T(8,128)(2,1)S(1)}, bf16[520,640]{1,0:T(8,128)(2,1)S(1)}, u32[]{:S(2)}, u32[]{:S(2)}) %collective-permute-start.5) | collective-permute-done | bytes 665632 | tf_op jit(solution)/shard_map/ppermute | solution.py:447
  123.8 3.3 %collective-permute-start.9 = (bf16[520,640]{1,0:T(8,128)(2,1)S(1)}, bf16[520,640]{1,0:T(8,128)(2,1)S(1)}, u32[]{:S(2)}, u32[]{:S(2)}) collective-permute-start(bf16[520,640]{1,0:T(8,128)(2,1)S(1)} %collective-permute-done.5.refs_5_), channel_id=1, source_target_pairs={{0,32},{32,0},{64,96},{96,64},{1,33},{33,1},{65,97},{97,65},{2,34}... | collective-permute-start | bytes 1996808 | tf_op jit(solution)/shard_map/ppermute | solution.py:451
  127.1 1.7 %collective-permute-done.9.refs_7_ = bf16[520,640]{1,0:T(8,128)(2,1)S(1)} collective-permute-done((bf16[520,640]{1,0:T(8,128)(2,1)S(1)}, bf16[520,640]{1,0:T(8,128)(2,1)S(1)}, u32[]{:S(2)}, u32[]{:S(2)}) %collective-permute-start.9) | collective-permute-done | bytes 665632 | tf_op jit(solution)/shard_map/ppermute | solution.py:451
  128.8 2.5 %shard_map.116 = bf16[520,4608]{1,0:T(8,128)(2,1)} custom-call(s32[1]{0:T(128)} %bitcast.1.place, bf16[520,512]{1,0:T(8,128)(2,1)S(1)} %get-tuple-element.38.refs_0_, bf16[520,640]{1,0:T(8,128)(2,1)S(1)} %get-tuple-element.40.refs_1_, bf16[520,512]{1,0:T(8,128)(2,1)S(1)} %collective-permute-done.6.refs_2_, ...), custom_call_target="tpu_custom_call" | custom-call | bytes 9584640 | tf_op jit(solution)/shard_map/pallas_call | solution.py:407
  (12 shorter events, 2.7 us)
Async XLA Ops:
  0.6 16.8 %collective-permute-start.1 = (bf16[512,4608]{1,0:T(8,128)(2,1)}, bf16[512,4608]{1,0:T(8,128)(2,1)}, u32[]{:S(2)}, u32[]{:S(2)}) collective-permute-start(bf16[512,4608]{1,0:T(8,128)(2,1)} %hidden.1), channel_id=1, source_target_pairs={{0,32},{32,0},{64,96},{96,64},{1,33},{33,1},{65,97},{97,65},{2,34}... | collective-permute-start | bytes 14155784 | tf_op jit(solution)/shard_map/ppermute | solution.py:429
  6.2 8.9 %copy-start.2 = (bf16[512,520]{0,1:T(8,128)(2,1)S(1)}, bf16[512,520]{0,1:T(8,128)(2,1)}, u32[]{:S(2)}) copy-start(bf16[512,520]{0,1:T(8,128)(2,1)} %param.12) | copy-start | bytes 1597444
  6.2 44.4 %all-to-all-start = ((bf16[32,40,1024]{2,1,0:T(8,128)(2,1)}), bf16[32,40,1024]{2,1,0:T(8,128)(2,1)S(1)}, u32[]{:S(2)}, u32[]{:S(2)}) async-start(bf16[32,40,1024]{2,1,0:T(8,128)(2,1)} %shard_map.111), calls=%async_computation | async-start | bytes 5242880 | tf_op jit(solution)/shard_map/all_to_all | solution.py:424
  15.1 2.4 %collective-permute-start = (bf16[512,520]{0,1:T(8,128)(2,1)S(1)}, bf16[512,520]{0,1:T(8,128)(2,1)}, u32[]{:S(2)}, u32[]{:S(2)}) collective-permute-start(bf16[512,520]{0,1:T(8,128)(2,1)S(1)} %copy-done.2), channel_id=1, source_target_pairs={{0,32},{32,0},{64,96},{96,64},{1,33},{33,1},{65,97},{97,65},{2,34}... | collective-permute-start | bytes 1597448 | tf_op jit(solution)/shard_map/ppermute | solution.py:430
  24.0 36.5 %collective-permute-start.2 = (bf16[520,640]{1,0:T(8,128)(2,1)}, bf16[520,640]{1,0:T(8,128)(2,1)S(1)}, u32[]{:S(2)}, u32[]{:S(2)}) collective-permute-start(bf16[520,640]{1,0:T(8,128)(2,1)} %get-tuple-element.27), channel_id=1, source_target_pairs={{0,64},{64,0},{32,96},{96,32},{1,65},{65,1},{33,97},{97,33},{2,66}... | collective-permute-start | bytes 1996808 | tf_op jit(solution)/shard_map/ppermute | solution.py:435
  57.8 1.1 copy-start
  58.9 27.6 %copy-start.1 = (bf16[520,1152]{1,0:T(8,128)(2,1)S(1)}, bf16[520,1152]{1,0:T(8,128)(2,1)}, u32[]{:S(2)}) copy-start(bf16[520,1152]{1,0:T(8,128)(2,1)} %get-tuple-element.29.head) | copy-start | bytes 3594244
  60.4 26.1 %all-to-all-start.1 = ((bf16[32,40,512]{2,1,0:T(8,128)(2,1)}), bf16[32,40,512]{2,1,0:T(8,128)(2,1)S(1)}, u32[]{:S(2)}, u32[]{:S(2)}) async-start(bf16[32,40,512]{2,1,0:T(8,128)(2,1)} %copy-done), calls=%async_computation.1 | async-start | bytes 2621440 | tf_op jit(solution)/shard_map/all_to_all | solution.py:424
  70.2 26.7 %collective-permute-start.3 = (bf16[520,512]{1,0:T(8,128)(2,1)}, bf16[520,512]{1,0:T(8,128)(2,1)}, u32[]{:S(2)}, u32[]{:S(2)}) collective-permute-start(bf16[520,512]{1,0:T(8,128)(2,1)} %get-tuple-element.31), channel_id=1, source_target_pairs={{0,64},{64,0},{32,96},{96,32},{1,65},{65,1},{33,97},{97,33},{2,66}... | collective-permute-start | bytes 1597448 | tf_op jit(solution)/shard_map/ppermute | solution.py:436
  90.7 17.5 %collective-permute-start.4 = (bf16[520,512]{1,0:T(8,128)(2,1)S(1)}, bf16[520,512]{1,0:T(8,128)(2,1)S(1)}, u32[]{:S(2)}, u32[]{:S(2)}) collective-permute-start(bf16[520,512]{1,0:T(8,128)(2,1)S(1)} %get-tuple-element.38.refs_0_), channel_id=1, source_target_pairs={{0,64},{64,0},{32,96},{96,32},{1,65},{65,1},{33,97},{97,33},{2,66}... | collective-permute-start | bytes 1597448 | tf_op jit(solution)/shard_map/ppermute | solution.py:441
  103.5 10.1 %collective-permute-start.7 = (bf16[520,640]{1,0:T(8,128)(2,1)S(1)}, bf16[520,640]{1,0:T(8,128)(2,1)S(1)}, u32[]{:S(2)}, u32[]{:S(2)}) collective-permute-start(bf16[520,640]{1,0:T(8,128)(2,1)S(1)} %get-tuple-element.40.refs_1_), channel_id=1, source_target_pairs={{0,32},{32,0},{64,96},{96,64},{1,33},{33,1},{65,97},{97,65},{2,34}... | collective-permute-start | bytes 1996808 | tf_op jit(solution)/shard_map/ppermute | solution.py:448
  108.2 15.6 %collective-permute-start.5 = (bf16[520,640]{1,0:T(8,128)(2,1)S(1)}, bf16[520,640]{1,0:T(8,128)(2,1)S(1)}, u32[]{:S(2)}, u32[]{:S(2)}) collective-permute-start(bf16[520,640]{1,0:T(8,128)(2,1)S(1)} %get-tuple-element.40.refs_1_), channel_id=1, source_target_pairs={{0,64},{64,0},{32,96},{96,32},{1,65},{65,1},{33,97},{97,33},{2,66}... | collective-permute-start | bytes 1996808 | tf_op jit(solution)/shard_map/ppermute | solution.py:447
  109.4 4.2 %collective-permute-start.6 = (bf16[520,512]{1,0:T(8,128)(2,1)S(1)}, bf16[520,512]{1,0:T(8,128)(2,1)S(1)}, u32[]{:S(2)}, u32[]{:S(2)}) collective-permute-start(bf16[520,512]{1,0:T(8,128)(2,1)S(1)} %get-tuple-element.38.refs_0_), channel_id=1, source_target_pairs={{0,32},{32,0},{64,96},{96,64},{1,33},{33,1},{65,97},{97,65},{2,34}... | collective-permute-start | bytes 1597448 | tf_op jit(solution)/shard_map/ppermute | solution.py:442
  112.0 2.3 %collective-permute-start.8 = (bf16[520,512]{1,0:T(8,128)(2,1)S(1)}, bf16[520,512]{1,0:T(8,128)(2,1)S(1)}, u32[]{:S(2)}, u32[]{:S(2)}) collective-permute-start(bf16[520,512]{1,0:T(8,128)(2,1)S(1)} %collective-permute-done.4.refs_4_), channel_id=1, source_target_pairs={{0,32},{32,0},{64,96},{96,64},{1,33},{33,1},{65,97},{97,65},{2,34}... | collective-permute-start | bytes 1597448 | tf_op jit(solution)/shard_map/ppermute | solution.py:449
  123.8 5.0 %collective-permute-start.9 = (bf16[520,640]{1,0:T(8,128)(2,1)S(1)}, bf16[520,640]{1,0:T(8,128)(2,1)S(1)}, u32[]{:S(2)}, u32[]{:S(2)}) collective-permute-start(bf16[520,640]{1,0:T(8,128)(2,1)S(1)} %collective-permute-done.5.refs_5_), channel_id=1, source_target_pairs={{0,32},{32,0},{64,96},{96,64},{1,33},{33,1},{65,97},{97,65},{2,34}... | collective-permute-start | bytes 1996808 | tf_op jit(solution)/shard_map/ppermute | solution.py:451
